TPU v7x, 256 devices: a whole 4x4x8 slice. The times are simulated.
256 devices in a mesh: space: 16 (over y_hi, x, core), chan: 16 (over z, y_lo).
Axes of the slice: x: 4, y: 4 (y_hi: 2, y_lo: 2; y = y_hi * 2 + y_lo), z: 8, core: 2. Of those that a mesh axis runs over, the one named last changes fastest.
Arguments:
- inputs: bfloat16 [256, 48, 1024], P('chan', 'space'), may hold values from -6 to 6
- first_weight: bfloat16 [27, 256, 256], P(None, 'chan'), may hold values from -0.109375 to 0.109375
- second_weight: bfloat16 [27, 256, 256], P(None, 'chan'), may hold values from -0.109375 to 0.109375
- cotangent: bfloat16 [256, 48, 1024], P('chan', 'space'), may hold values from -6 to 6
Outputs:
- features: bfloat16 [256, 48, 1024], P('chan', 'space')
- grad_first: float32 [27, 256, 256], P(None, 'chan')
- grad_second: float32 [27, 256, 256], P(None, 'chan')
- grad_inputs: bfloat16 [256, 48, 1024], P('chan', 'space')
All inputs are finite; a program needn't handle non-finite values.
Results may differ from a plain program's by a relative error of at most 0.025.
Values may be sent and summed in bfloat16 or wider, within the bound.
No kernel may reach another device: no remote copies, remote signals or barrier semaphores. Data moves between devices by JAX's collectives and lax.ppermute only.
A program may use at most 64 MiB of HBM per device.

v0:
```python
import functools

import jax
import jax.numpy as jnp
import numpy as np
from jax import lax
from jax.experimental import pallas as pl
from jax.experimental.pallas import tpu as pltpu
from jax.sharding import PartitionSpec as P

SIDE = 32
FLAT = SIDE * SIDE
PLANES = 3
PIECE = 16
SLOTS = 4
BLOCK = SLOTS * PIECE
TAPS = 27
ROWS = 9 * BLOCK
COLS = 3 * BLOCK
NEAR = (0, 1, 2, 3)
FAR = (0, 8, 4, 12)
FIRST, SECOND = (FAR, NEAR), (NEAR, FAR)
LIMIT = 24 * 1024 * 1024
BF = jnp.bfloat16
F32 = jnp.float32


def call(body, outs, scratch, scalars, arrays, flops):
    moved = sum(int(np.prod(x.shape)) * x.dtype.itemsize for x in (*arrays, *outs))
    spec = pl.BlockSpec(memory_space=pltpu.VMEM)
    return pl.pallas_call(
        body,
        out_shape=outs,
        in_specs=[pl.BlockSpec(memory_space=pltpu.SMEM)] * len(scalars) + [spec] * len(arrays),
        out_specs=[spec] * len(outs),
        scratch_shapes=scratch,
        compiler_params=pltpu.CompilerParams(vmem_limit_bytes=LIMIT),
        cost_estimate=pl.CostEstimate(flops=flops, bytes_accessed=moved, transcendentals=0),
    )(*scalars, *arrays)


def shape(dims, dtype=BF):
    return jax.ShapeDtypeStruct(dims, dtype)


def chosen(chan, take, give):
    row = lax.broadcasted_iota(jnp.int32, (256, 256), 0)
    col = lax.broadcasted_iota(jnp.int32, (256, 256), 1)
    n, m = col // BLOCK, (col // PIECE) % SLOTS
    block = chan ^ (n % 2 * give[1]) ^ (n // 2 * give[2]) ^ (m % 2 * take[1]) ^ (m // 2 * take[2])
    return (row == block * PIECE + col % PIECE).astype(BF)


HALF = 14 * PIECE
TALL, SPLIT = 9 * PIECE, 5 * PIECE
GRAD_ROWS = TALL + SPLIT
HELD = SLOTS * GRAD_ROWS
PLAIN = ((0, 0), (1, 0), (2, 0), (3, 0))
PASSED = ((0, 0), (1, HALF), (1, 0), (2, 0))
ARRIVED = ((0, 0), (2, HALF), (1, 0), (2, 0))
LANES = 2 * BLOCK


def split_body(take, give, spots, chan_ref, weight_ref, *out_refs):
    pick = chosen(chan_ref[0], take, give)
    moved = jnp.dot(weight_ref[...], pick, preferred_element_type=F32).astype(BF)
    for n, (k, row) in enumerate(spots):
        part, out = moved[:, n * BLOCK : (n + 1) * BLOCK], out_refs[k]
        out[row : row + HALF, :BLOCK] = part[:HALF]
        out[row : row + HALF - PIECE, BLOCK:] = part[HALF:]
        out[row + HALF - PIECE : row + HALF, BLOCK:] = jnp.zeros((PIECE, BLOCK), BF)


def split_weight(chan, weight, take, give, sent):
    rows = TAPS * PIECE
    return call(
        functools.partial(split_body, take, give, sent),
        [shape((HALF * sum(k == j for k, _ in sent), LANES)) for j in range(1 + max(sent)[0])],
        [],
        [chan],
        [weight.reshape(rows, 256)],
        2 * rows * 256 * 256,
    )


def stitch_body(left_ref, right_ref, out_ref):
    out_ref[:HALF, :] = left_ref[...]
    out_ref[HALF:, :] = right_ref[HALF:, :]


def stitch(left, right):
    return call(stitch_body, [shape((2 * HALF, LANES))], [], [], [left, right], 0)[0]


def arrange_body(spots, *refs):
    fwd_ref, bwd_ref = refs[-2:]
    for a in range(3):
        for b in range(3):
            for c in range(3):
                k = 9 * a + 3 * b + c
                row, lane = PIECE * (k % 14), BLOCK * (k // 14)
                block = jnp.concatenate(
                    [refs[j][at + row : at + row + PIECE, lane : lane + BLOCK] for j, at in spots], axis=0
                )
                turned = block.astype(F32).T.astype(BF)
                at = COLS * b + BLOCK * a
                fwd_ref[BLOCK * c : BLOCK * (c + 1), at : at + BLOCK] = block
                at = COLS * (2 - b) + BLOCK * (2 - a)
                bwd_ref[BLOCK * (2 - c) : BLOCK * (3 - c), at : at + BLOCK] = turned


def arrange_weight(pieces, spots):
    return call(
        functools.partial(arrange_body, spots), [shape((COLS, ROWS))] * 2, [], [], pieces, 0
    )


def edges():
    cell = lax.broadcasted_iota(jnp.int32, (1, FLAT), 1)
    col = cell % SIDE
    return cell, col


def fill(slab, refs, field):
    for p in range(PLANES):
        for m, ref in enumerate(refs[:SLOTS]):
            at = BLOCK * (p + 1) + PIECE * m
            field[at : at + PIECE, :] = ref[p]
    off, core = (ref[...].reshape(BLOCK, FLAT) for ref in refs[SLOTS:])
    off = jnp.where((slab == 0) | (slab == 15), jnp.zeros_like(off), off)
    odd = slab % 2 == 1
    field[:BLOCK, :] = jnp.where(odd, core, off)
    field[BLOCK * (PLANES + 1) :, :] = jnp.where(odd, off, core)


def lift(rows, shift, cell):
    moved = pltpu.roll(rows, -shift % FLAT, 1)
    if shift > 0:
        end = jnp.where(cell[:, -LANES:] < FLAT - SIDE, moved[:, -LANES:], 0.0)
        return jnp.concatenate([moved[:, :-LANES], end], axis=1)
    end = jnp.where(cell[:, :LANES] >= SIDE, moved[:, :LANES], 0.0)
    return jnp.concatenate([end, moved[:, LANES:]], axis=1)


def conv_body(space_ref, weight_ref, *refs):
    own_ref, o1, o2, o3, up, field, down = refs[-7:]
    fill(space_ref[0], refs[:-7], field)
    cell, col = edges()
    for p in range(PLANES + 2):
        plane = slice(BLOCK * p, BLOCK * (p + 1))
        rows = field[plane, :].astype(F32)
        down[plane, :] = lift(rows, SIDE, cell).astype(BF)
        up[plane, :] = lift(rows, -SIDE, cell).astype(BF)
    weight = weight_ref[...]
    for d in range(PLANES):
        window = slice(BLOCK * d, BLOCK * d + COLS)
        terms = sum(
            jnp.dot(weight[:, COLS * b : COLS * (b + 1)], rows[window, :], preferred_element_type=F32)
            for b, rows in enumerate((up, field, down))
        )
        left, mid, right = (terms[BLOCK * c : BLOCK * (c + 1)] for c in range(3))
        left = jnp.where(col >= 1, pltpu.roll(left, 1, 1), 0.0)
        right = jnp.where(col < SIDE - 1, pltpu.roll(right, FLAT - 1, 1), 0.0)
        total = mid + left + right
        own_ref[d] = total[:PIECE]
        for n, out in enumerate((o1, o2, o3), 1):
            out[d] = total[PIECE * n : PIECE * (n + 1)].astype(BF)


def conv(space, weight, slots):
    piece = (PLANES, PIECE, FLAT)
    return call(
        conv_body,
        [shape(piece, F32)] + [shape(piece)] * 3,
        [pltpu.VMEM((BLOCK * (PLANES + 2), FLAT), BF)] * 3,
        [space],
        [weight, *slots],
        2 * ROWS * COLS * FLAT * PLANES,
    )


def moves(err, cell, col):
    for c in range(3):
        if c == 0:
            one = jnp.where(col < SIDE - 1, pltpu.roll(err, FLAT - 1, 1), 0.0)
        elif c == 2:
            one = jnp.where(col >= 1, pltpu.roll(err, 1, 1), 0.0)
        else:
            one = err
        for b in range(3):
            if b == 0:
                two = jnp.where(cell < FLAT - SIDE, pltpu.roll(one, FLAT - SIDE, 1), 0.0)
            elif b == 2:
                two = jnp.where(cell >= SIDE, pltpu.roll(one, SIDE, 1), 0.0)
            else:
                two = one
            yield 3 * b + c, two.astype(BF)


def across(lhs, rhs):
    return lax.dot_general(lhs, rhs, (((1,), (1,)), ((), ())), preferred_element_type=F32)


def grad_body(spots, space_ref, *refs):
    slots, errs = refs[:6], refs[6:10]
    outs, (field, moved, total) = refs[10:-3], refs[-3:]
    fill(space_ref[0], slots, field)
    cell, col = edges()
    total[...] = jnp.zeros((ROWS, COLS), F32)

    @pl.loop(0, PLANES)
    def _(d):
        err = jnp.concatenate([e[d] for e in errs], axis=0).astype(F32)
        for q, two in moves(err, cell, col):
            for n in range(SLOTS):
                at = n * TALL + q * PIECE
                moved[at : at + PIECE, :] = two[PIECE * n : PIECE * (n + 1)]
        rows = pl.ds(pl.multiple_of(BLOCK * d, BLOCK), COLS)
        total[...] += across(moved[...], field[rows, :])

    for n in range(SLOTS):
        part = total[n * TALL : (n + 1) * TALL, :].astype(BF)
        out, at = outs[spots[n][0]], spots[n][1]
        end = at + GRAD_ROWS
        out[at : at + TALL, :] = part[:, : 2 * BLOCK]
        out[at + TALL : end, :BLOCK] = part[:SPLIT, 2 * BLOCK :]
        out[at + TALL : end - PIECE, BLOCK:] = part[SPLIT:, 2 * BLOCK :]
        out[end - PIECE : end, BLOCK:] = jnp.zeros((PIECE, BLOCK), BF)


def weight_grad(space, slots, errs, sent):
    return call(
        functools.partial(grad_body, sent),
        [shape((HALF * sum(k == j for k, _ in sent), LANES)) for j in range(1 + max(sent)[0])],
        [
            pltpu.VMEM((BLOCK * (PLANES + 2), FLAT), BF),
            pltpu.VMEM((ROWS, FLAT), BF),
            pltpu.VMEM((ROWS, COLS), F32),
        ],
        [space],
        [*slots, *errs],
        2 * ROWS * COLS * FLAT * PLANES,
    )


def keep_body(space_ref, *refs):
    odd = space_ref[0] % 2 == 1
    pieces, (keep_ref, give_ref) = refs[:-2], refs[-2:]
    for n, (k, at) in enumerate(ARRIVED):
        first, second = pieces[n][...], pieces[SLOTS + k][at : at + GRAD_ROWS, :]
        rows = slice(n * GRAD_ROWS, (n + 1) * GRAD_ROWS)
        keep_ref[rows, :] = jnp.where(odd, second, first)
        give_ref[rows, :] = jnp.where(odd, first, second)


def total_body(*refs):
    terms = [ref[...].astype(F32) for ref in refs[:-1]]
    while len(terms) > 1:
        terms = [left + right for left, right in zip(terms[::2], terms[1::2])]
    refs[-1][...] = terms[0].astype(BF)


def total(pieces):
    return call(total_body, [shape((HELD, LANES))], [], [], pieces, 0)[0]


def finish_body(space_ref, chan_ref, mine_ref, got_ref, first_ref, second_ref):
    odd = space_ref[0] % 2 == 1
    first = jnp.where(odd, got_ref[...], mine_ref[...])
    second = jnp.where(odd, mine_ref[...], got_ref[...])
    for held, out, (take, give) in ((first, first_ref, FIRST), (second, second_ref, SECOND)):
        pick = chosen(chan_ref[0], take, give)
        for a in range(3):
            parts = []
            for n in range(SLOTS):
                at = n * GRAD_ROWS
                if a < 2:
                    parts.append(held[at : at + TALL, a * BLOCK : (a + 1) * BLOCK])
                else:
                    high = held[at + TALL : at + GRAD_ROWS, :BLOCK]
                    low = held[at + TALL : at + GRAD_ROWS - PIECE, BLOCK:]
                    parts.append(jnp.concatenate([high, low], axis=0))
            wide = jnp.concatenate(parts, axis=1)
            out[9 * a : 9 * (a + 1)] = across(wide, pick).reshape(9, PIECE, 256)


def finish(space, chan, mine, got):
    return call(
        finish_body,
        [shape((TAPS, PIECE, 256), F32)] * 2,
        [],
        [space, chan],
        [mine, got],
        2 * TAPS * PIECE * 256 * 256,
    )


def by_chan(array, mask):
    return lax.ppermute(array, "chan", [(i, i ^ mask) for i in range(16)]) if mask else array


def by_space(array, mask):
    return lax.ppermute(array, "space", [(i, i ^ mask) for i in range(16)])


def over_chan(arrays, masks):
    return [by_chan(array, mask) for array, mask in zip(arrays, masks)]


def gather(array, masks):
    return over_chan([array] * SLOTS, masks)


def edge_body(space_ref, s0, s1, s2, s3, off_ref, core_ref):
    odd = space_ref[0] % 2 == 1
    for m, ref in enumerate((s0, s1, s2, s3)):
        first, last = ref[0], ref[PLANES - 1]
        off_ref[m] = jnp.where(odd, last, first)
        core_ref[m] = jnp.where(odd, first, last)


def borders(space, slots):
    off, core = call(edge_body, [shape((SLOTS, PIECE, FLAT))] * 2, [], [space], slots, 0)
    outward = [(i, (i + 1 if i % 2 else i - 1) % 16) for i in range(16)]
    return [lax.ppermute(off, "space", outward), by_space(core, 1)]


def add(pieces):
    total = pieces[0].astype(F32)
    for piece in pieces[1:]:
        total = total + piece.astype(F32)
    return total


def slope(value):
    sig = jax.nn.sigmoid(value)
    return sig * (1.0 + value * (1.0 - sig))


tie = lax.optimization_barrier


def shards(inputs, first_weight, second_weight, cotangent):
    space = lax.axis_index("space").astype(jnp.int32).reshape(1)
    chan = lax.axis_index("chan").astype(jnp.int32).reshape(1)
    inputs = inputs.transpose(1, 0, 2)
    cotangent = cotangent.transpose(1, 0, 2)

    in_slots = gather(inputs, FAR)
    pieces = over_chan(split_weight(chan, first_weight, *FIRST, PLAIN), NEAR)
    more = split_weight(chan, second_weight, *SECOND, PASSED)
    in_slots, pieces, more = tie((in_slots, pieces, more))
    in_slots += borders(space, in_slots)
    fwd_first, bwd_first = arrange_weight(pieces, PLAIN)
    one = by_chan(more[1], FAR[2])
    in_slots, fwd_first = tie((in_slots, fwd_first))
    parts, one = tie((conv(space, fwd_first, in_slots), one))
    sums = over_chan(parts, NEAR)
    sums[1], one = tie((sums[1], one))
    two = by_chan(stitch(more[2], one), FAR[3])
    pre_first = add(sums)
    hidden = jax.nn.silu(pre_first).astype(BF)

    hid_slots = gather(hidden, NEAR)
    hid_slots, two = tie((hid_slots, two))
    hid_slots += borders(space, hid_slots)
    fwd_second, bwd_second = arrange_weight([more[0], one, two], ARRIVED)
    pre_second = add(over_chan(conv(space, fwd_second, hid_slots), FAR))
    features = jax.nn.silu(pre_second).astype(BF)
    err_second = (cotangent.astype(F32) * slope(pre_second)).astype(BF)

    err2_slots = gather(err_second, FAR)
    edge = borders(space, err2_slots)
    grads = weight_grad(space, hid_slots, err2_slots, PASSED)
    edge, grads = tie((edge, grads))
    parts, grads = tie((conv(space, bwd_second, err2_slots + edge), grads))
    sums = over_chan(parts, NEAR)
    one = by_chan(grads[1], FAR[2])
    sums, one = tie((sums, one))
    grad_hidden = add(sums).astype(BF)
    err_first = (grad_hidden.astype(F32) * slope(pre_first)).astype(BF)

    err1_slots = gather(err_first, NEAR)
    two = by_chan(stitch(grads[2], one), FAR[3])
    err1_slots, two = tie((err1_slots, two))
    firsts = over_chan(weight_grad(space, in_slots, err1_slots, PLAIN), NEAR)
    edge = borders(space, err1_slots)
    firsts, edge = tie((firsts, edge))
    keep, give = call(
        keep_body, [shape((HELD, LANES))] * 2, [], [space], [*firsts, grads[0], one, two], 0
    )
    got, parts = tie((by_space(give, 1), conv(space, bwd_first, err1_slots + edge)))
    mine, parts = tie((total([keep, got]), parts))
    got, far = tie((by_space(mine, 8), by_chan(parts[1], FAR[1])))
    mine = total([mine, got])
    mine, parts = tie((mine, parts))
    rest = [by_space(mine, 2 * m) for m in (1, 2, 3)]
    rest, near, side = tie((rest, by_chan(parts[2], FAR[2]), by_chan(parts[3], FAR[3])))
    mine = total([mine, *rest])
    grad_first, grad_second = finish(space, chan, mine, by_space(mine, 1))
    grad_inputs = add([parts[0], near, far, side]).astype(BF)
    return (
        features.transpose(1, 0, 2),
        grad_first,
        grad_second,
        grad_inputs.transpose(1, 0, 2),
    )


def solution(mesh):
    slab = P("chan", "space", None)
    filters = P(None, "chan", None)
    return jax.shard_map(
        shards,
        mesh=mesh,
        in_specs=(slab, filters, filters, slab),
        out_specs=(slab, filters, filters, slab),
        check_vma=False,
    )
```

profile of v0, /device:TPU:1, one launch (start us, length us, event | category | flops | bytes accessed | tf_op | source)
XLA Modules:
  0.0 162.7 jit_solution(8130114703197238314)
XLA Ops:
  1.9 2.2 %collective-permute-start.3 = (bf16[224,128]{1,0:T(8,128)(2,1)S(1)}, bf16[224,128]{1,0:T(8,128)(2,1)S(1)}, u32[]{:S(2)}, u32[]{:S(2)}) collective-permute-start(bf16[224,128]{1,0:T(8,128)(2,1)S(1)} %get-tuple-element.130), channel_id=1, source_target_pairs={{0,1},{1,0},{2,3},{3,2},{4,5},{5,4},{6,7},{7,6},{8,9},{9,8},{10,11... | collective-permute-start | bytes 172040 | tf_op jit(solution)/shard_map/ppermute | solution.py:299
  4.2 6.0 %collective-permute-start.2 = (bf16[3,16,1024]{2,1,0:T(8,128)(2,1)}, bf16[3,16,1024]{2,1,0:T(8,128)(2,1)S(1)}, u32[]{:S(2)}, u32[]{:S(2)}) collective-permute-start(bf16[3,16,1024]{2,1,0:T(8,128)(2,1)} %bitcast.15), channel_id=1, source_target_pairs={{0,12},{1,13},{2,14},{3,15},{4,8},{5,9},{6,10},{7,11},{8,4},{9,5},... | collective-permute-start | bytes 294920 | tf_op jit(solution)/shard_map/ppermute | solution.py:299
  14.0 5.8 %collective-permute-done.4.refs_2_ = bf16[224,128]{1,0:T(8,128)(2,1)S(1)} collective-permute-done((bf16[224,128]{1,0:T(8,128)(2,1)S(1)}, bf16[224,128]{1,0:T(8,128)(2,1)S(1)}, u32[]{:S(2)}, u32[]{:S(2)}) %collective-permute-start.4) | collective-permute-done | bytes 57376 | tf_op jit(solution)/shard_map/ppermute | solution.py:299
  19.9 2.9 %collective-permute-done.5.refs_3_ = bf16[224,128]{1,0:T(8,128)(2,1)S(1)} collective-permute-done((bf16[224,128]{1,0:T(8,128)(2,1)S(1)}, bf16[224,128]{1,0:T(8,128)(2,1)S(1)}, u32[]{:S(2)}, u32[]{:S(2)}) %collective-permute-start.5) | collective-permute-done | bytes 57376 | tf_op jit(solution)/shard_map/ppermute | solution.py:299
  22.8 2.6 %collective-permute-start.6 = (bf16[4,16,1024]{2,1,0:T(8,128)(2,1)S(1)}, bf16[4,16,1024]{2,1,0:T(8,128)(2,1)S(1)}, u32[]{:S(2)}, u32[]{:S(2)}) collective-permute-start(bf16[4,16,1024]{2,1,0:T(8,128)(2,1)S(1)} %get-tuple-element.141), channel_id=1, source_target_pairs={{0,240},{16,32},{32,16},{48,64},{64,48},{80,96},{96,80},{112,128},... | collective-permute-start | bytes 393224 | tf_op jit(solution)/shard_map/ppermute | solution.py:325
  25.5 2.9 %collective-permute-start.7 = (bf16[4,16,1024]{2,1,0:T(8,128)(2,1)S(1)}, bf16[4,16,1024]{2,1,0:T(8,128)(2,1)S(1)}, u32[]{:S(2)}, u32[]{:S(2)}) collective-permute-start(bf16[4,16,1024]{2,1,0:T(8,128)(2,1)S(1)} %get-tuple-element.142), channel_id=1, source_target_pairs={{0,16},{16,0},{32,48},{48,32},{64,80},{80,64},{96,112},{112,96},{1... | collective-permute-start | bytes 393224 | tf_op jit(solution)/shard_map/ppermute | solution.py:303
  29.2 1.4 shard_map.78
  30.6 1.4 shard_map.79
  32.0 4.6 %collective-permute-done.8.right_ref.refs_1_ = bf16[448,128]{1,0:T(8,128)(2,1)S(1)} collective-permute-done((bf16[448,128]{1,0:T(8,128)(2,1)S(1)}, bf16[448,128]{1,0:T(8,128)(2,1)S(1)}, u32[]{:S(2)}, u32[]{:S(2)}) %collective-permute-start.8) | collective-permute-done | bytes 114720 | tf_op jit(solution)/shard_map/ppermute | solution.py:299
  37.0 2.2 %collective-permute-start.11 = (bf16[3,16,1024]{2,1,0:T(8,128)(2,1)S(1)}, bf16[3,16,1024]{2,1,0:T(8,128)(2,1)S(1)}, u32[]{:S(2)}, u32[]{:S(2)}) collective-permute-start(bf16[3,16,1024]{2,1,0:T(8,128)(2,1)S(1)} %get-tuple-element.166), channel_id=1, source_target_pairs={{0,3},{1,2},{2,1},{3,0},{4,7},{5,6},{6,5},{7,4},{8,11},{9,10},{10,... | collective-permute-start | bytes 294920 | tf_op jit(solution)/shard_map/ppermute | solution.py:299
  40.7 2.0 %collective-permute-done.11 = bf16[3,16,1024]{2,1,0:T(8,128)(2,1)S(1)} collective-permute-done((bf16[3,16,1024]{2,1,0:T(8,128)(2,1)S(1)}, bf16[3,16,1024]{2,1,0:T(8,128)(2,1)S(1)}, u32[]{:S(2)}, u32[]{:S(2)}) %collective-permute-start.11) | collective-permute-done | bytes 98336 | tf_op jit(solution)/shard_map/ppermute | solution.py:299
  45.6 2.6 %collective-permute-done.14.s3.refs_3_ = bf16[3,16,1024]{2,1,0:T(8,128)(2,1)S(1)} collective-permute-done((bf16[3,16,1024]{2,1,0:T(8,128)(2,1)S(1)}, bf16[3,16,1024]{2,1,0:T(8,128)(2,1)S(1)}, u32[]{:S(2)}, u32[]{:S(2)}) %collective-permute-start.14) | collective-permute-done | bytes 98336 | tf_op jit(solution)/shard_map/ppermute | solution.py:299
  49.1 2.5 %collective-permute-start.16 = (bf16[4,16,1024]{2,1,0:T(8,128)(2,1)S(1)}, bf16[4,16,1024]{2,1,0:T(8,128)(2,1)S(1)}, u32[]{:S(2)}, u32[]{:S(2)}) collective-permute-start(bf16[4,16,1024]{2,1,0:T(8,128)(2,1)S(1)} %get-tuple-element.174), channel_id=1, source_target_pairs={{0,240},{16,32},{32,16},{48,64},{64,48},{80,96},{96,80},{112,128},... | collective-permute-start | bytes 393224 | tf_op jit(solution)/shard_map/ppermute | solution.py:325
  51.6 2.0 %collective-permute-start.17 = (bf16[4,16,1024]{2,1,0:T(8,128)(2,1)S(1)}, bf16[4,16,1024]{2,1,0:T(8,128)(2,1)S(1)}, u32[]{:S(2)}, u32[]{:S(2)}) collective-permute-start(bf16[4,16,1024]{2,1,0:T(8,128)(2,1)S(1)} %get-tuple-element.175), channel_id=1, source_target_pairs={{0,16},{16,0},{32,48},{48,32},{64,80},{80,64},{96,112},{112,96},{1... | collective-permute-start | bytes 393224 | tf_op jit(solution)/shard_map/ppermute | solution.py:303
  53.6 1.4 shard_map.81
  55.0 1.4 shard_map.83
  56.4 1.5 collective-permute-start.18
  57.9 1.7 %collective-permute-start.19 = (bf16[3,16,1024]{2,1,0:T(8,128)(2,1)S(1)}, bf16[3,16,1024]{2,1,0:T(8,128)(2,1)S(1)}, u32[]{:S(2)}, u32[]{:S(2)}) collective-permute-start(bf16[3,16,1024]{2,1,0:T(8,128)(2,1)S(1)} %get-tuple-element.178), channel_id=1, source_target_pairs={{0,4},{1,5},{2,6},{3,7},{4,0},{5,1},{6,2},{7,3},{8,12},{9,13},{10,... | collective-permute-start | bytes 294920 | tf_op jit(solution)/shard_map/ppermute | solution.py:299
  59.6 2.6 %collective-permute-start.20 = (bf16[3,16,1024]{2,1,0:T(8,128)(2,1)S(1)}, bf16[3,16,1024]{2,1,0:T(8,128)(2,1)S(1)}, u32[]{:S(2)}, u32[]{:S(2)}) collective-permute-start(bf16[3,16,1024]{2,1,0:T(8,128)(2,1)S(1)} %get-tuple-element.179), channel_id=1, source_target_pairs={{0,12},{1,13},{2,14},{3,15},{4,8},{5,9},{6,10},{7,11},{8,4},{9,5},... | collective-permute-start | bytes 294920 | tf_op jit(solution)/shard_map/ppermute | solution.py:299
  62.2 2.3 %collective-permute-done.18 = bf16[3,16,1024]{2,1,0:T(8,128)(2,1)S(1)} collective-permute-done((bf16[3,16,1024]{2,1,0:T(8,128)(2,1)S(1)}, bf16[3,16,1024]{2,1,0:T(8,128)(2,1)S(1)}, u32[]{:S(2)}, u32[]{:S(2)}) %collective-permute-start.18) | collective-permute-done | bytes 98336 | tf_op jit(solution)/shard_map/ppermute | solution.py:299
  66.2 3.3 %collective-permute-start.23 = (bf16[3,16,1024]{2,1,0:T(8,128)(2,1)S(1)}, bf16[3,16,1024]{2,1,0:T(8,128)(2,1)S(1)}, u32[]{:S(2)}, u32[]{:S(2)}) collective-permute-start(bf16[3,16,1024]{2,1,0:T(8,128)(2,1)S(1)} %get-tuple-element.254.s0.refs_6_.refs_0_), channel_id=1, source_target_pairs={{0,12},{1,13},{2,14},{3,15},{4,8},{5,9},{6,10},{7,11},{8,4},{9,5},... | collective-permute-start | bytes 294920 | tf_op jit(solution)/shard_map/ppermute | solution.py:299
  70.1 2.0 %collective-permute-start.21 = (bf16[3,16,1024]{2,1,0:T(8,128)(2,1)S(1)}, bf16[3,16,1024]{2,1,0:T(8,128)(2,1)S(1)}, u32[]{:S(2)}, u32[]{:S(2)}) collective-permute-start(bf16[3,16,1024]{2,1,0:T(8,128)(2,1)S(1)} %get-tuple-element.254.s0.refs_6_.refs_0_), channel_id=1, source_target_pairs={{0,8},{1,9},{2,10},{3,11},{4,12},{5,13},{6,14},{7,15},{8,0},{9,1},... | collective-permute-start | bytes 294920 | tf_op jit(solution)/shard_map/ppermute | solution.py:299
  72.1 2.2 %collective-permute-done.23.s3.refs_9_.refs_3_ = bf16[3,16,1024]{2,1,0:T(8,128)(2,1)S(1)} collective-permute-done((bf16[3,16,1024]{2,1,0:T(8,128)(2,1)S(1)}, bf16[3,16,1024]{2,1,0:T(8,128)(2,1)S(1)}, u32[]{:S(2)}, u32[]{:S(2)}) %collective-permute-start.23) | collective-permute-done | bytes 98336 | tf_op jit(solution)/shard_map/ppermute | solution.py:299
  74.6 4.6 %collective-permute-done.21.s1.refs_7_.refs_1_ = bf16[3,16,1024]{2,1,0:T(8,128)(2,1)S(1)} collective-permute-done((bf16[3,16,1024]{2,1,0:T(8,128)(2,1)S(1)}, bf16[3,16,1024]{2,1,0:T(8,128)(2,1)S(1)}, u32[]{:S(2)}, u32[]{:S(2)}) %collective-permute-start.21) | collective-permute-done | bytes 98336 | tf_op jit(solution)/shard_map/ppermute | solution.py:299
  79.2 7.0 %collective-permute-start.24 = (bf16[4,16,1024]{2,1,0:T(8,128)(2,1)S(1)}, bf16[4,16,1024]{2,1,0:T(8,128)(2,1)S(1)}, u32[]{:S(2)}, u32[]{:S(2)}) collective-permute-start(bf16[4,16,1024]{2,1,0:T(8,128)(2,1)S(1)} %get-tuple-element.181), channel_id=1, source_target_pairs={{0,240},{16,32},{32,16},{48,64},{64,48},{80,96},{96,80},{112,128},... | collective-permute-start | bytes 393224 | tf_op jit(solution)/shard_map/ppermute | solution.py:325
  86.3 2.5 %collective-permute-start.25 = (bf16[4,16,1024]{2,1,0:T(8,128)(2,1)S(1)}, bf16[4,16,1024]{2,1,0:T(8,128)(2,1)S(1)}, u32[]{:S(2)}, u32[]{:S(2)}) collective-permute-start(bf16[4,16,1024]{2,1,0:T(8,128)(2,1)S(1)} %get-tuple-element.182), channel_id=1, source_target_pairs={{0,16},{16,0},{32,48},{48,32},{64,80},{80,64},{96,112},{112,96},{1... | collective-permute-start | bytes 393224 | tf_op jit(solution)/shard_map/ppermute | solution.py:303
  88.8 2.4 %shard_map.85 = (bf16[224,128]{1,0:T(8,128)(2,1)S(1)}, bf16[448,128]{1,0:T(8,128)(2,1)S(1)}, bf16[224,128]{1,0:T(8,128)(2,1)S(1)}) custom-call(s32[1]{0:T(128)} %bitcast.space_ref, bf16[3,16,1024]{2,1,0:T(8,128)(2,1)S(1)} %multiply_convert_fusion.2.s0.refs_0_, bf16[3,16,1024]{2,1,0:T(8,128)(2,1)S(1)} %collective-permute-done.12.s1.refs_1_, ...), custom_call_target="tpu_custom_call" | custom-call | flops 679477248 | bytes 1277952 | tf_op jit(solution)/shard_map/pallas_call | solution.py:31
  91.2 1.4 shard_map.86
  92.6 3.1 %collective-permute-start.29 = (bf16[448,128]{1,0:T(8,128)(2,1)S(1)}, bf16[448,128]{1,0:T(8,128)(2,1)S(1)}, u32[]{:S(2)}, u32[]{:S(2)}) collective-permute-start(bf16[448,128]{1,0:T(8,128)(2,1)S(1)} %get-tuple-element.199), channel_id=1, source_target_pairs={{0,4},{1,5},{2,6},{3,7},{4,0},{5,1},{6,2},{7,3},{8,12},{9,13},{10,... | collective-permute-start | bytes 344072 | tf_op jit(solution)/shard_map/ppermute | solution.py:299
  95.7 1.3 collective-permute-start.26
  99.2 1.3 collective-permute-done.27
  101.7 2.8 %collective-permute-start.33 = (bf16[448,128]{1,0:T(8,128)(2,1)S(1)}, bf16[448,128]{1,0:T(8,128)(2,1)S(1)}, u32[]{:S(2)}, u32[]{:S(2)}) collective-permute-start(bf16[448,128]{1,0:T(8,128)(2,1)S(1)} %shard_map.87), channel_id=1, source_target_pairs={{0,12},{1,13},{2,14},{3,15},{4,8},{5,9},{6,10},{7,11},{8,4},{9,5},... | collective-permute-start | bytes 344072 | tf_op jit(solution)/shard_map/ppermute | solution.py:299
  104.6 3.0 %collective-permute-start.32 = (bf16[3,16,1024]{2,1,0:T(8,128)(2,1)S(1)}, bf16[3,16,1024]{2,1,0:T(8,128)(2,1)S(1)}, u32[]{:S(2)}, u32[]{:S(2)}) collective-permute-start(bf16[3,16,1024]{2,1,0:T(8,128)(2,1)S(1)} %multiply_convert_fusion.refs_6_.s0.refs_0_), channel_id=1, source_target_pairs={{0,3},{1,2},{2,1},{3,0},{4,7},{5,6},{6,5},{7,4},{8,11},{9,10},{10,... | collective-permute-start | bytes 294920 | tf_op jit(solution)/shard_map/ppermute | solution.py:299
  108.5 1.9 %collective-permute-done.32.refs_9_.s3.refs_3_ = bf16[3,16,1024]{2,1,0:T(8,128)(2,1)S(1)} collective-permute-done((bf16[3,16,1024]{2,1,0:T(8,128)(2,1)S(1)}, bf16[3,16,1024]{2,1,0:T(8,128)(2,1)S(1)}, u32[]{:S(2)}, u32[]{:S(2)}) %collective-permute-start.32) | collective-permute-done | bytes 98336 | tf_op jit(solution)/shard_map/ppermute | solution.py:299
  111.5 4.4 %collective-permute-start.37 = (bf16[4,16,1024]{2,1,0:T(8,128)(2,1)S(1)}, bf16[4,16,1024]{2,1,0:T(8,128)(2,1)S(1)}, u32[]{:S(2)}, u32[]{:S(2)}) collective-permute-start(bf16[4,16,1024]{2,1,0:T(8,128)(2,1)S(1)} %get-tuple-element.214), channel_id=1, source_target_pairs={{0,240},{16,32},{32,16},{48,64},{64,48},{80,96},{96,80},{112,128},... | collective-permute-start | bytes 393224 | tf_op jit(solution)/shard_map/ppermute | solution.py:325
  115.9 4.9 %collective-permute-start.38 = (bf16[4,16,1024]{2,1,0:T(8,128)(2,1)S(1)}, bf16[4,16,1024]{2,1,0:T(8,128)(2,1)S(1)}, u32[]{:S(2)}, u32[]{:S(2)}) collective-permute-start(bf16[4,16,1024]{2,1,0:T(8,128)(2,1)S(1)} %get-tuple-element.215), channel_id=1, source_target_pairs={{0,16},{16,0},{32,48},{48,32},{64,80},{80,64},{96,112},{112,96},{1... | collective-permute-start | bytes 393224 | tf_op jit(solution)/shard_map/ppermute | solution.py:303
  120.8 2.4 %shard_map.88 = (bf16[224,128]{1,0:T(8,128)(2,1)S(1)}, bf16[224,128]{1,0:T(8,128)(2,1)S(1)}, bf16[224,128]{1,0:T(8,128)(2,1)S(1)}, bf16[224,128]{1,0:T(8,128)(2,1)S(1)}) custom-call(s32[1]{0:T(128)} %bitcast.space_ref, bf16[3,16,1024]{2,1,0:T(8,128)(2,1)S(1)} %bitcast.20, bf16[3,16,1024]{2,1,0:T(8,128)(2,1)S(1)} %collective-permute-done.s1.refs_1_, ...), custom_call_target="tpu_custom_call" | custom-call | flops 679477248 | bytes 1277952 | tf_op jit(solution)/shard_map/pallas_call | solution.py:31
  128.9 1.6 collective-permute-start.39
  130.6 1.4 shard_map.91
  132.0 3.5 %collective-permute-start.40 = (bf16[896,128]{1,0:T(8,128)(2,1)S(1)}, bf16[896,128]{1,0:T(8,128)(2,1)S(1)}, u32[]{:S(2)}, u32[]{:S(2)}) collective-permute-start(bf16[896,128]{1,0:T(8,128)(2,1)S(1)} %shard_map.92.refs_0_), channel_id=1, source_target_pairs={{0,128},{16,144},{32,160},{48,176},{64,192},{80,208},{96,224},{112... | collective-permute-start | bytes 688136 | tf_op jit(solution)/shard_map/ppermute | solution.py:303
  136.7 8.5 %collective-permute-done.41 = bf16[3,16,1024]{2,1,0:T(8,128)(2,1)S(1)} collective-permute-done((bf16[3,16,1024]{2,1,0:T(8,128)(2,1)S(1)}, bf16[3,16,1024]{2,1,0:T(8,128)(2,1)S(1)}, u32[]{:S(2)}, u32[]{:S(2)}) %collective-permute-start.41) | collective-permute-done | bytes 98336 | tf_op jit(solution)/shard_map/ppermute | solution.py:299
  146.3 2.2 %collective-permute-start.42 = (bf16[896,128]{1,0:T(8,128)(2,1)S(1)}, bf16[896,128]{1,0:T(8,128)(2,1)S(1)}, u32[]{:S(2)}, u32[]{:S(2)}) collective-permute-start(bf16[896,128]{1,0:T(8,128)(2,1)S(1)} %shard_map.93.refs_0_), channel_id=1, source_target_pairs={{0,32},{16,48},{32,0},{48,16},{64,96},{80,112},{96,64},{112,80},{1... | collective-permute-start | bytes 688136 | tf_op jit(solution)/shard_map/ppermute | solution.py:303
  148.5 1.5 collective-permute-start.45
  150.1 1.5 collective-permute-start.46
  151.6 1.6 collective-permute-done.45
  153.2 3.1 %collective-permute-done.46 = bf16[3,16,1024]{2,1,0:T(8,128)(2,1)S(1)} collective-permute-done((bf16[3,16,1024]{2,1,0:T(8,128)(2,1)S(1)}, bf16[3,16,1024]{2,1,0:T(8,128)(2,1)S(1)}, u32[]{:S(2)}, u32[]{:S(2)}) %collective-permute-start.46) | collective-permute-done | bytes 98336 | tf_op jit(solution)/shard_map/ppermute | solution.py:299
  157.5 2.7 %collective-permute-start.47 = (bf16[896,128]{1,0:T(8,128)(2,1)S(1)}, bf16[896,128]{1,0:T(8,128)(2,1)S(1)}, u32[]{:S(2)}, u32[]{:S(2)}) collective-permute-start(bf16[896,128]{1,0:T(8,128)(2,1)S(1)} %shard_map.94.mine_ref), channel_id=1, source_target_pairs={{0,16},{16,0},{32,48},{48,32},{64,80},{80,64},{96,112},{112,96},{1... | collective-permute-start | bytes 688136 | tf_op jit(solution)/shard_map/ppermute | solution.py:303
  161.4 1.3 shard_map.95
  (81 shorter events, 30.1 us)
Async XLA Ops:
  1.9 11.1 %collective-permute-start.3 = (bf16[224,128]{1,0:T(8,128)(2,1)S(1)}, bf16[224,128]{1,0:T(8,128)(2,1)S(1)}, u32[]{:S(2)}, u32[]{:S(2)}) collective-permute-start(bf16[224,128]{1,0:T(8,128)(2,1)S(1)} %get-tuple-element.130), channel_id=1, source_target_pairs={{0,1},{1,0},{2,3},{3,2},{4,5},{5,4},{6,7},{7,6},{8,9},{9,8},{10,11... | collective-permute-start | bytes 172040 | tf_op jit(solution)/shard_map/ppermute | solution.py:299
  4.2 18.6 %collective-permute-start.2 = (bf16[3,16,1024]{2,1,0:T(8,128)(2,1)}, bf16[3,16,1024]{2,1,0:T(8,128)(2,1)S(1)}, u32[]{:S(2)}, u32[]{:S(2)}) collective-permute-start(bf16[3,16,1024]{2,1,0:T(8,128)(2,1)} %bitcast.15), channel_id=1, source_target_pairs={{0,12},{1,13},{2,14},{3,15},{4,8},{5,9},{6,10},{7,11},{8,4},{9,5},... | collective-permute-start | bytes 294920 | tf_op jit(solution)/shard_map/ppermute | solution.py:299
  10.2 12.6 %collective-permute-start.1 = (bf16[3,16,1024]{2,1,0:T(8,128)(2,1)}, bf16[3,16,1024]{2,1,0:T(8,128)(2,1)S(1)}, u32[]{:S(2)}, u32[]{:S(2)}) collective-permute-start(bf16[3,16,1024]{2,1,0:T(8,128)(2,1)} %bitcast.16), channel_id=1, source_target_pairs={{0,4},{1,5},{2,6},{3,7},{4,0},{5,1},{6,2},{7,3},{8,12},{9,13},{10,... | collective-permute-start | bytes 294920 | tf_op jit(solution)/shard_map/ppermute | solution.py:299
  11.4 11.4 %collective-permute-start = (bf16[3,16,1024]{2,1,0:T(8,128)(2,1)}, bf16[3,16,1024]{2,1,0:T(8,128)(2,1)S(1)}, u32[]{:S(2)}, u32[]{:S(2)}) collective-permute-start(bf16[3,16,1024]{2,1,0:T(8,128)(2,1)} %bitcast.17), channel_id=1, source_target_pairs={{0,8},{1,9},{2,10},{3,11},{4,12},{5,13},{6,14},{7,15},{8,0},{9,1},... | collective-permute-start | bytes 294920 | tf_op jit(solution)/shard_map/ppermute | solution.py:299
  12.3 7.6 %collective-permute-start.4 = (bf16[224,128]{1,0:T(8,128)(2,1)S(1)}, bf16[224,128]{1,0:T(8,128)(2,1)S(1)}, u32[]{:S(2)}, u32[]{:S(2)}) collective-permute-start(bf16[224,128]{1,0:T(8,128)(2,1)S(1)} %get-tuple-element.131), channel_id=1, source_target_pairs={{0,2},{1,3},{2,0},{3,1},{4,6},{5,7},{6,4},{7,5},{8,10},{9,11},{10,... | collective-permute-start | bytes 172040 | tf_op jit(solution)/shard_map/ppermute | solution.py:299
  13.0 9.7 %collective-permute-start.5 = (bf16[224,128]{1,0:T(8,128)(2,1)S(1)}, bf16[224,128]{1,0:T(8,128)(2,1)S(1)}, u32[]{:S(2)}, u32[]{:S(2)}) collective-permute-start(bf16[224,128]{1,0:T(8,128)(2,1)S(1)} %get-tuple-element.132), channel_id=1, source_target_pairs={{0,3},{1,2},{2,1},{3,0},{4,7},{5,6},{6,5},{7,4},{8,11},{9,10},{10,... | collective-permute-start | bytes 172040 | tf_op jit(solution)/shard_map/ppermute | solution.py:299
  22.8 7.8 %collective-permute-start.6 = (bf16[4,16,1024]{2,1,0:T(8,128)(2,1)S(1)}, bf16[4,16,1024]{2,1,0:T(8,128)(2,1)S(1)}, u32[]{:S(2)}, u32[]{:S(2)}) collective-permute-start(bf16[4,16,1024]{2,1,0:T(8,128)(2,1)S(1)} %get-tuple-element.141), channel_id=1, source_target_pairs={{0,240},{16,32},{32,16},{48,64},{64,48},{80,96},{96,80},{112,128},... | collective-permute-start | bytes 393224 | tf_op jit(solution)/shard_map/ppermute | solution.py:325
  25.5 5.1 %collective-permute-start.7 = (bf16[4,16,1024]{2,1,0:T(8,128)(2,1)S(1)}, bf16[4,16,1024]{2,1,0:T(8,128)(2,1)S(1)}, u32[]{:S(2)}, u32[]{:S(2)}) collective-permute-start(bf16[4,16,1024]{2,1,0:T(8,128)(2,1)S(1)} %get-tuple-element.142), channel_id=1, source_target_pairs={{0,16},{16,0},{32,48},{48,32},{64,80},{80,64},{96,112},{112,96},{1... | collective-permute-start | bytes 393224 | tf_op jit(solution)/shard_map/ppermute | solution.py:303
  28.4 8.1 %collective-permute-start.8 = (bf16[448,128]{1,0:T(8,128)(2,1)S(1)}, bf16[448,128]{1,0:T(8,128)(2,1)S(1)}, u32[]{:S(2)}, u32[]{:S(2)}) collective-permute-start(bf16[448,128]{1,0:T(8,128)(2,1)S(1)} %get-tuple-element.159), channel_id=1, source_target_pairs={{0,4},{1,5},{2,6},{3,7},{4,0},{5,1},{6,2},{7,3},{8,12},{9,13},{10,... | collective-permute-start | bytes 344072 | tf_op jit(solution)/shard_map/ppermute | solution.py:299
  36.5 3.5 %collective-permute-start.9 = (bf16[3,16,1024]{2,1,0:T(8,128)(2,1)S(1)}, bf16[3,16,1024]{2,1,0:T(8,128)(2,1)S(1)}, u32[]{:S(2)}, u32[]{:S(2)}) collective-permute-start(bf16[3,16,1024]{2,1,0:T(8,128)(2,1)S(1)} %get-tuple-element.160), channel_id=1, source_target_pairs={{0,1},{1,0},{2,3},{3,2},{4,5},{5,4},{6,7},{7,6},{8,9},{9,8},{10,11... | collective-permute-start | bytes 294920 | tf_op jit(solution)/shard_map/ppermute | solution.py:299
  37.0 3.8 %collective-permute-start.10 = (bf16[3,16,1024]{2,1,0:T(8,128)(2,1)S(1)}, bf16[3,16,1024]{2,1,0:T(8,128)(2,1)S(1)}, u32[]{:S(2)}, u32[]{:S(2)}) collective-permute-start(bf16[3,16,1024]{2,1,0:T(8,128)(2,1)S(1)} %get-tuple-element.165), channel_id=1, source_target_pairs={{0,2},{1,3},{2,0},{3,1},{4,6},{5,7},{6,4},{7,5},{8,10},{9,11},{10,... | collective-permute-start | bytes 294920 | tf_op jit(solution)/shard_map/ppermute | solution.py:299
  37.0 5.8 %collective-permute-start.11 = (bf16[3,16,1024]{2,1,0:T(8,128)(2,1)S(1)}, bf16[3,16,1024]{2,1,0:T(8,128)(2,1)S(1)}, u32[]{:S(2)}, u32[]{:S(2)}) collective-permute-start(bf16[3,16,1024]{2,1,0:T(8,128)(2,1)S(1)} %get-tuple-element.166), channel_id=1, source_target_pairs={{0,3},{1,2},{2,1},{3,0},{4,7},{5,6},{6,5},{7,4},{8,11},{9,10},{10,... | collective-permute-start | bytes 294920 | tf_op jit(solution)/shard_map/ppermute | solution.py:299
  40.0 9.0 %collective-permute-start.15 = (bf16[448,128]{1,0:T(8,128)(2,1)S(1)}, bf16[448,128]{1,0:T(8,128)(2,1)S(1)}, u32[]{:S(2)}, u32[]{:S(2)}) collective-permute-start(bf16[448,128]{1,0:T(8,128)(2,1)S(1)} %shard_map.80), channel_id=1, source_target_pairs={{0,12},{1,13},{2,14},{3,15},{4,8},{5,9},{6,10},{7,11},{8,4},{9,5},... | collective-permute-start | bytes 344072 | tf_op jit(solution)/shard_map/ppermute | solution.py:299
  42.9 5.3 %collective-permute-start.14 = (bf16[3,16,1024]{2,1,0:T(8,128)(2,1)S(1)}, bf16[3,16,1024]{2,1,0:T(8,128)(2,1)S(1)}, u32[]{:S(2)}, u32[]{:S(2)}) collective-permute-start(bf16[3,16,1024]{2,1,0:T(8,128)(2,1)S(1)} %multiply_convert_fusion.2.s0.refs_0_), channel_id=1, source_target_pairs={{0,3},{1,2},{2,1},{3,0},{4,7},{5,6},{6,5},{7,4},{8,11},{9,10},{10,... | collective-permute-start | bytes 294920 | tf_op jit(solution)/shard_map/ppermute | solution.py:299
  43.8 4.6 %collective-permute-start.13 = (bf16[3,16,1024]{2,1,0:T(8,128)(2,1)S(1)}, bf16[3,16,1024]{2,1,0:T(8,128)(2,1)S(1)}, u32[]{:S(2)}, u32[]{:S(2)}) collective-permute-start(bf16[3,16,1024]{2,1,0:T(8,128)(2,1)S(1)} %multiply_convert_fusion.2.s0.refs_0_), channel_id=1, source_target_pairs={{0,2},{1,3},{2,0},{3,1},{4,6},{5,7},{6,4},{7,5},{8,10},{9,11},{10,... | collective-permute-start | bytes 294920 | tf_op jit(solution)/shard_map/ppermute | solution.py:299
  44.6 4.5 %collective-permute-start.12 = (bf16[3,16,1024]{2,1,0:T(8,128)(2,1)S(1)}, bf16[3,16,1024]{2,1,0:T(8,128)(2,1)S(1)}, u32[]{:S(2)}, u32[]{:S(2)}) collective-permute-start(bf16[3,16,1024]{2,1,0:T(8,128)(2,1)S(1)} %multiply_convert_fusion.2.s0.refs_0_), channel_id=1, source_target_pairs={{0,1},{1,0},{2,3},{3,2},{4,5},{5,4},{6,7},{7,6},{8,9},{9,8},{10,11... | collective-permute-start | bytes 294920 | tf_op jit(solution)/shard_map/ppermute | solution.py:299
  49.1 5.9 %collective-permute-start.16 = (bf16[4,16,1024]{2,1,0:T(8,128)(2,1)S(1)}, bf16[4,16,1024]{2,1,0:T(8,128)(2,1)S(1)}, u32[]{:S(2)}, u32[]{:S(2)}) collective-permute-start(bf16[4,16,1024]{2,1,0:T(8,128)(2,1)S(1)} %get-tuple-element.174), channel_id=1, source_target_pairs={{0,240},{16,32},{32,16},{48,64},{64,48},{80,96},{96,80},{112,128},... | collective-permute-start | bytes 393224 | tf_op jit(solution)/shard_map/ppermute | solution.py:325
  51.6 3.4 %collective-permute-start.17 = (bf16[4,16,1024]{2,1,0:T(8,128)(2,1)S(1)}, bf16[4,16,1024]{2,1,0:T(8,128)(2,1)S(1)}, u32[]{:S(2)}, u32[]{:S(2)}) collective-permute-start(bf16[4,16,1024]{2,1,0:T(8,128)(2,1)S(1)} %get-tuple-element.175), channel_id=1, source_target_pairs={{0,16},{16,0},{32,48},{48,32},{64,80},{80,64},{96,112},{112,96},{1... | collective-permute-start | bytes 393224 | tf_op jit(solution)/shard_map/ppermute | solution.py:303
  56.4 8.0 %collective-permute-start.18 = (bf16[3,16,1024]{2,1,0:T(8,128)(2,1)S(1)}, bf16[3,16,1024]{2,1,0:T(8,128)(2,1)S(1)}, u32[]{:S(2)}, u32[]{:S(2)}) collective-permute-start(bf16[3,16,1024]{2,1,0:T(8,128)(2,1)S(1)} %get-tuple-element.177), channel_id=1, source_target_pairs={{0,8},{1,9},{2,10},{3,11},{4,12},{5,13},{6,14},{7,15},{8,0},{9,1},... | collective-permute-start | bytes 294920 | tf_op jit(solution)/shard_map/ppermute | solution.py:299
  57.9 6.6 %collective-permute-start.19 = (bf16[3,16,1024]{2,1,0:T(8,128)(2,1)S(1)}, bf16[3,16,1024]{2,1,0:T(8,128)(2,1)S(1)}, u32[]{:S(2)}, u32[]{:S(2)}) collective-permute-start(bf16[3,16,1024]{2,1,0:T(8,128)(2,1)S(1)} %get-tuple-element.178), channel_id=1, source_target_pairs={{0,4},{1,5},{2,6},{3,7},{4,0},{5,1},{6,2},{7,3},{8,12},{9,13},{10,... | collective-permute-start | bytes 294920 | tf_op jit(solution)/shard_map/ppermute | solution.py:299
  59.6 5.9 %collective-permute-start.20 = (bf16[3,16,1024]{2,1,0:T(8,128)(2,1)S(1)}, bf16[3,16,1024]{2,1,0:T(8,128)(2,1)S(1)}, u32[]{:S(2)}, u32[]{:S(2)}) collective-permute-start(bf16[3,16,1024]{2,1,0:T(8,128)(2,1)S(1)} %get-tuple-element.179), channel_id=1, source_target_pairs={{0,12},{1,13},{2,14},{3,15},{4,8},{5,9},{6,10},{7,11},{8,4},{9,5},... | collective-permute-start | bytes 294920 | tf_op jit(solution)/shard_map/ppermute | solution.py:299
  66.2 8.1 %collective-permute-start.23 = (bf16[3,16,1024]{2,1,0:T(8,128)(2,1)S(1)}, bf16[3,16,1024]{2,1,0:T(8,128)(2,1)S(1)}, u32[]{:S(2)}, u32[]{:S(2)}) collective-permute-start(bf16[3,16,1024]{2,1,0:T(8,128)(2,1)S(1)} %get-tuple-element.254.s0.refs_6_.refs_0_), channel_id=1, source_target_pairs={{0,12},{1,13},{2,14},{3,15},{4,8},{5,9},{6,10},{7,11},{8,4},{9,5},... | collective-permute-start | bytes 294920 | tf_op jit(solution)/shard_map/ppermute | solution.py:299
  69.6 5.1 %collective-permute-start.22 = (bf16[3,16,1024]{2,1,0:T(8,128)(2,1)S(1)}, bf16[3,16,1024]{2,1,0:T(8,128)(2,1)S(1)}, u32[]{:S(2)}, u32[]{:S(2)}) collective-permute-start(bf16[3,16,1024]{2,1,0:T(8,128)(2,1)S(1)} %get-tuple-element.254.s0.refs_6_.refs_0_), channel_id=1, source_target_pairs={{0,4},{1,5},{2,6},{3,7},{4,0},{5,1},{6,2},{7,3},{8,12},{9,13},{10,... | collective-permute-start | bytes 294920 | tf_op jit(solution)/shard_map/ppermute | solution.py:299
  70.1 9.1 %collective-permute-start.21 = (bf16[3,16,1024]{2,1,0:T(8,128)(2,1)S(1)}, bf16[3,16,1024]{2,1,0:T(8,128)(2,1)S(1)}, u32[]{:S(2)}, u32[]{:S(2)}) collective-permute-start(bf16[3,16,1024]{2,1,0:T(8,128)(2,1)S(1)} %get-tuple-element.254.s0.refs_6_.refs_0_), channel_id=1, source_target_pairs={{0,8},{1,9},{2,10},{3,11},{4,12},{5,13},{6,14},{7,15},{8,0},{9,1},... | collective-permute-start | bytes 294920 | tf_op jit(solution)/shard_map/ppermute | solution.py:299
  79.2 12.0 %collective-permute-start.24 = (bf16[4,16,1024]{2,1,0:T(8,128)(2,1)S(1)}, bf16[4,16,1024]{2,1,0:T(8,128)(2,1)S(1)}, u32[]{:S(2)}, u32[]{:S(2)}) collective-permute-start(bf16[4,16,1024]{2,1,0:T(8,128)(2,1)S(1)} %get-tuple-element.181), channel_id=1, source_target_pairs={{0,240},{16,32},{32,16},{48,64},{64,48},{80,96},{96,80},{112,128},... | collective-permute-start | bytes 393224 | tf_op jit(solution)/shard_map/ppermute | solution.py:325
  86.3 4.9 %collective-permute-start.25 = (bf16[4,16,1024]{2,1,0:T(8,128)(2,1)S(1)}, bf16[4,16,1024]{2,1,0:T(8,128)(2,1)S(1)}, u32[]{:S(2)}, u32[]{:S(2)}) collective-permute-start(bf16[4,16,1024]{2,1,0:T(8,128)(2,1)S(1)} %get-tuple-element.182), channel_id=1, source_target_pairs={{0,16},{16,0},{32,48},{48,32},{64,80},{80,64},{96,112},{112,96},{1... | collective-permute-start | bytes 393224 | tf_op jit(solution)/shard_map/ppermute | solution.py:303
  92.6 9.1 %collective-permute-start.29 = (bf16[448,128]{1,0:T(8,128)(2,1)S(1)}, bf16[448,128]{1,0:T(8,128)(2,1)S(1)}, u32[]{:S(2)}, u32[]{:S(2)}) collective-permute-start(bf16[448,128]{1,0:T(8,128)(2,1)S(1)} %get-tuple-element.199), channel_id=1, source_target_pairs={{0,4},{1,5},{2,6},{3,7},{4,0},{5,1},{6,2},{7,3},{8,12},{9,13},{10,... | collective-permute-start | bytes 344072 | tf_op jit(solution)/shard_map/ppermute | solution.py:299
  95.7 3.5 %collective-permute-start.26 = (bf16[3,16,1024]{2,1,0:T(8,128)(2,1)S(1)}, bf16[3,16,1024]{2,1,0:T(8,128)(2,1)S(1)}, u32[]{:S(2)}, u32[]{:S(2)}) collective-permute-start(bf16[3,16,1024]{2,1,0:T(8,128)(2,1)S(1)} %get-tuple-element.196), channel_id=1, source_target_pairs={{0,1},{1,0},{2,3},{3,2},{4,5},{5,4},{6,7},{7,6},{8,9},{9,8},{10,11... | collective-permute-start | bytes 294920 | tf_op jit(solution)/shard_map/ppermute | solution.py:299
  97.0 3.5 %collective-permute-start.27 = (bf16[3,16,1024]{2,1,0:T(8,128)(2,1)S(1)}, bf16[3,16,1024]{2,1,0:T(8,128)(2,1)S(1)}, u32[]{:S(2)}, u32[]{:S(2)}) collective-permute-start(bf16[3,16,1024]{2,1,0:T(8,128)(2,1)S(1)} %get-tuple-element.197), channel_id=1, source_target_pairs={{0,2},{1,3},{2,0},{3,1},{4,6},{5,7},{6,4},{7,5},{8,10},{9,11},{10,... | collective-permute-start | bytes 294920 | tf_op jit(solution)/shard_map/ppermute | solution.py:299
  97.2 4.5 %collective-permute-start.28 = (bf16[3,16,1024]{2,1,0:T(8,128)(2,1)S(1)}, bf16[3,16,1024]{2,1,0:T(8,128)(2,1)S(1)}, u32[]{:S(2)}, u32[]{:S(2)}) collective-permute-start(bf16[3,16,1024]{2,1,0:T(8,128)(2,1)S(1)} %get-tuple-element.198), channel_id=1, source_target_pairs={{0,3},{1,2},{2,1},{3,0},{4,7},{5,6},{6,5},{7,4},{8,11},{9,10},{10,... | collective-permute-start | bytes 294920 | tf_op jit(solution)/shard_map/ppermute | solution.py:299
  101.7 9.7 %collective-permute-start.33 = (bf16[448,128]{1,0:T(8,128)(2,1)S(1)}, bf16[448,128]{1,0:T(8,128)(2,1)S(1)}, u32[]{:S(2)}, u32[]{:S(2)}) collective-permute-start(bf16[448,128]{1,0:T(8,128)(2,1)S(1)} %shard_map.87), channel_id=1, source_target_pairs={{0,12},{1,13},{2,14},{3,15},{4,8},{5,9},{6,10},{7,11},{8,4},{9,5},... | collective-permute-start | bytes 344072 | tf_op jit(solution)/shard_map/ppermute | solution.py:299
  104.6 5.8 %collective-permute-start.32 = (bf16[3,16,1024]{2,1,0:T(8,128)(2,1)S(1)}, bf16[3,16,1024]{2,1,0:T(8,128)(2,1)S(1)}, u32[]{:S(2)}, u32[]{:S(2)}) collective-permute-start(bf16[3,16,1024]{2,1,0:T(8,128)(2,1)S(1)} %multiply_convert_fusion.refs_6_.s0.refs_0_), channel_id=1, source_target_pairs={{0,3},{1,2},{2,1},{3,0},{4,7},{5,6},{6,5},{7,4},{8,11},{9,10},{10,... | collective-permute-start | bytes 294920 | tf_op jit(solution)/shard_map/ppermute | solution.py:299
  107.6 3.8 %collective-permute-start.31 = (bf16[3,16,1024]{2,1,0:T(8,128)(2,1)S(1)}, bf16[3,16,1024]{2,1,0:T(8,128)(2,1)S(1)}, u32[]{:S(2)}, u32[]{:S(2)}) collective-permute-start(bf16[3,16,1024]{2,1,0:T(8,128)(2,1)S(1)} %multiply_convert_fusion.refs_6_.s0.refs_0_), channel_id=1, source_target_pairs={{0,2},{1,3},{2,0},{3,1},{4,6},{5,7},{6,4},{7,5},{8,10},{9,11},{10,... | collective-permute-start | bytes 294920 | tf_op jit(solution)/shard_map/ppermute | solution.py:299
  107.6 3.8 %collective-permute-start.30 = (bf16[3,16,1024]{2,1,0:T(8,128)(2,1)S(1)}, bf16[3,16,1024]{2,1,0:T(8,128)(2,1)S(1)}, u32[]{:S(2)}, u32[]{:S(2)}) collective-permute-start(bf16[3,16,1024]{2,1,0:T(8,128)(2,1)S(1)} %multiply_convert_fusion.refs_6_.s0.refs_0_), channel_id=1, source_target_pairs={{0,1},{1,0},{2,3},{3,2},{4,5},{5,4},{6,7},{7,6},{8,9},{9,8},{10,11... | collective-permute-start | bytes 294920 | tf_op jit(solution)/shard_map/ppermute | solution.py:299
  111.5 17.4 %collective-permute-start.37 = (bf16[4,16,1024]{2,1,0:T(8,128)(2,1)S(1)}, bf16[4,16,1024]{2,1,0:T(8,128)(2,1)S(1)}, u32[]{:S(2)}, u32[]{:S(2)}) collective-permute-start(bf16[4,16,1024]{2,1,0:T(8,128)(2,1)S(1)} %get-tuple-element.214), channel_id=1, source_target_pairs={{0,240},{16,32},{32,16},{48,64},{64,48},{80,96},{96,80},{112,128},... | collective-permute-start | bytes 393224 | tf_op jit(solution)/shard_map/ppermute | solution.py:325
  115.9 13.0 %collective-permute-start.38 = (bf16[4,16,1024]{2,1,0:T(8,128)(2,1)S(1)}, bf16[4,16,1024]{2,1,0:T(8,128)(2,1)S(1)}, u32[]{:S(2)}, u32[]{:S(2)}) collective-permute-start(bf16[4,16,1024]{2,1,0:T(8,128)(2,1)S(1)} %get-tuple-element.215), channel_id=1, source_target_pairs={{0,16},{16,0},{32,48},{48,32},{64,80},{80,64},{96,112},{112,96},{1... | collective-permute-start | bytes 393224 | tf_op jit(solution)/shard_map/ppermute | solution.py:303
  123.2 3.6 %collective-permute-start.34 = (bf16[224,128]{1,0:T(8,128)(2,1)S(1)}, bf16[224,128]{1,0:T(8,128)(2,1)S(1)}, u32[]{:S(2)}, u32[]{:S(2)}) collective-permute-start(bf16[224,128]{1,0:T(8,128)(2,1)S(1)} %get-tuple-element.211), channel_id=1, source_target_pairs={{0,1},{1,0},{2,3},{3,2},{4,5},{5,4},{6,7},{7,6},{8,9},{9,8},{10,11... | collective-permute-start | bytes 172040 | tf_op jit(solution)/shard_map/ppermute | solution.py:299
  124.4 3.3 %collective-permute-start.35 = (bf16[224,128]{1,0:T(8,128)(2,1)S(1)}, bf16[224,128]{1,0:T(8,128)(2,1)S(1)}, u32[]{:S(2)}, u32[]{:S(2)}) collective-permute-start(bf16[224,128]{1,0:T(8,128)(2,1)S(1)} %get-tuple-element.212), channel_id=1, source_target_pairs={{0,2},{1,3},{2,0},{3,1},{4,6},{5,7},{6,4},{7,5},{8,10},{9,11},{10,... | collective-permute-start | bytes 172040 | tf_op jit(solution)/shard_map/ppermute | solution.py:299
  124.7 4.1 %collective-permute-start.36 = (bf16[224,128]{1,0:T(8,128)(2,1)S(1)}, bf16[224,128]{1,0:T(8,128)(2,1)S(1)}, u32[]{:S(2)}, u32[]{:S(2)}) collective-permute-start(bf16[224,128]{1,0:T(8,128)(2,1)S(1)} %get-tuple-element.213), channel_id=1, source_target_pairs={{0,3},{1,2},{2,1},{3,0},{4,7},{5,6},{6,5},{7,4},{8,11},{9,10},{10,... | collective-permute-start | bytes 172040 | tf_op jit(solution)/shard_map/ppermute | solution.py:299
  128.9 3.0 %collective-permute-start.39 = (bf16[896,128]{1,0:T(8,128)(2,1)S(1)}, bf16[896,128]{1,0:T(8,128)(2,1)S(1)}, u32[]{:S(2)}, u32[]{:S(2)}) collective-permute-start(bf16[896,128]{1,0:T(8,128)(2,1)S(1)} %get-tuple-element.223), channel_id=1, source_target_pairs={{0,16},{16,0},{32,48},{48,32},{64,80},{80,64},{96,112},{112,96},{1... | collective-permute-start | bytes 688136 | tf_op jit(solution)/shard_map/ppermute | solution.py:303
  132.0 13.1 %collective-permute-start.40 = (bf16[896,128]{1,0:T(8,128)(2,1)S(1)}, bf16[896,128]{1,0:T(8,128)(2,1)S(1)}, u32[]{:S(2)}, u32[]{:S(2)}) collective-permute-start(bf16[896,128]{1,0:T(8,128)(2,1)S(1)} %shard_map.92.refs_0_), channel_id=1, source_target_pairs={{0,128},{16,144},{32,160},{48,176},{64,192},{80,208},{96,224},{112... | collective-permute-start | bytes 688136 | tf_op jit(solution)/shard_map/ppermute | solution.py:303
  135.5 9.6 %collective-permute-start.41 = (bf16[3,16,1024]{2,1,0:T(8,128)(2,1)S(1)}, bf16[3,16,1024]{2,1,0:T(8,128)(2,1)S(1)}, u32[]{:S(2)}, u32[]{:S(2)}) collective-permute-start(bf16[3,16,1024]{2,1,0:T(8,128)(2,1)S(1)} %get-tuple-element.237), channel_id=1, source_target_pairs={{0,8},{1,9},{2,10},{3,11},{4,12},{5,13},{6,14},{7,15},{8,0},{9,1},... | collective-permute-start | bytes 294920 | tf_op jit(solution)/shard_map/ppermute | solution.py:299
  145.2 11.1 %collective-permute-start.44 = (bf16[896,128]{1,0:T(8,128)(2,1)S(1)}, bf16[896,128]{1,0:T(8,128)(2,1)S(1)}, u32[]{:S(2)}, u32[]{:S(2)}) collective-permute-start(bf16[896,128]{1,0:T(8,128)(2,1)S(1)} %shard_map.93.refs_0_), channel_id=1, source_target_pairs={{0,96},{16,112},{32,64},{48,80},{64,32},{80,48},{96,0},{112,16},{1... | collective-permute-start | bytes 688136 | tf_op jit(solution)/shard_map/ppermute | solution.py:303
  146.3 10.0 %collective-permute-start.43 = (bf16[896,128]{1,0:T(8,128)(2,1)S(1)}, bf16[896,128]{1,0:T(8,128)(2,1)S(1)}, u32[]{:S(2)}, u32[]{:S(2)}) collective-permute-start(bf16[896,128]{1,0:T(8,128)(2,1)S(1)} %shard_map.93.refs_0_), channel_id=1, source_target_pairs={{0,64},{16,80},{32,96},{48,112},{64,0},{80,16},{96,32},{112,48},{1... | collective-permute-start | bytes 688136 | tf_op jit(solution)/shard_map/ppermute | solution.py:303
  146.3 11.1 %collective-permute-start.42 = (bf16[896,128]{1,0:T(8,128)(2,1)S(1)}, bf16[896,128]{1,0:T(8,128)(2,1)S(1)}, u32[]{:S(2)}, u32[]{:S(2)}) collective-permute-start(bf16[896,128]{1,0:T(8,128)(2,1)S(1)} %shard_map.93.refs_0_), channel_id=1, source_target_pairs={{0,32},{16,48},{32,0},{48,16},{64,96},{80,112},{96,64},{112,80},{1... | collective-permute-start | bytes 688136 | tf_op jit(solution)/shard_map/ppermute | solution.py:303
  148.5 4.7 %collective-permute-start.45 = (bf16[3,16,1024]{2,1,0:T(8,128)(2,1)S(1)}, bf16[3,16,1024]{2,1,0:T(8,128)(2,1)S(1)}, u32[]{:S(2)}, u32[]{:S(2)}) collective-permute-start(bf16[3,16,1024]{2,1,0:T(8,128)(2,1)S(1)} %get-tuple-element.243), channel_id=1, source_target_pairs={{0,4},{1,5},{2,6},{3,7},{4,0},{5,1},{6,2},{7,3},{8,12},{9,13},{10,... | collective-permute-start | bytes 294920 | tf_op jit(solution)/shard_map/ppermute | solution.py:299
  150.1 6.2 %collective-permute-start.46 = (bf16[3,16,1024]{2,1,0:T(8,128)(2,1)S(1)}, bf16[3,16,1024]{2,1,0:T(8,128)(2,1)S(1)}, u32[]{:S(2)}, u32[]{:S(2)}) collective-permute-start(bf16[3,16,1024]{2,1,0:T(8,128)(2,1)S(1)} %get-tuple-element.244), channel_id=1, source_target_pairs={{0,12},{1,13},{2,14},{3,15},{4,8},{5,9},{6,10},{7,11},{8,4},{9,5},... | collective-permute-start | bytes 294920 | tf_op jit(solution)/shard_map/ppermute | solution.py:299
  157.5 3.8 %collective-permute-start.47 = (bf16[896,128]{1,0:T(8,128)(2,1)S(1)}, bf16[896,128]{1,0:T(8,128)(2,1)S(1)}, u32[]{:S(2)}, u32[]{:S(2)}) collective-permute-start(bf16[896,128]{1,0:T(8,128)(2,1)S(1)} %shard_map.94.mine_ref), channel_id=1, source_target_pairs={{0,16},{16,0},{32,48},{48,32},{64,80},{80,64},{96,112},{112,96},{1... | collective-permute-start | bytes 688136 | tf_op jit(solution)/shard_map/ppermute | solution.py:303
  (4 other events, 32.6 us)
where the time goes:
time: 163 us
  starting transfers between devices  89.1 us (55%)
  waiting for transfers between devices  54.5 us (33%)
  Pallas kernels  15.5 us (10%)
  other arithmetic  1.72 us (1%)
    ppermute x34, waiting for transfers between devices, by_chan(): lax.ppermute(array, 'chan', [(i, i ^ mask) for i in range(16)])  53 us
    ppermute x34, starting transfers between devices, by_chan(): lax.ppermute(array, 'chan', [(i, i ^ mask) for i in range(16)])  48.9 us
    ppermute x10, starting transfers between devices, by_space(): return lax.ppermute(array, 'space', [(i, i ^ mask) for i in range(16)])  23.5 us
    ppermute x4, starting transfers between devices, borders(): return [lax.ppermute(off, 'space', outward), by_space(core, 1)]  16.6 us
    pallas_call x21, Pallas kernels, call(): pl.pallas_call(body, out_shape=outs, in_specs=[pl.BlockSpec(memory_space=...  15.5 us
  transfers between devices with their start and end apart: 48, of which 27 were waited for; matrix products, arithmetic and copies ran while one was open for 1% of the time, Pallas kernels for 7%

commit v1 on v0

--- a/solution.py
+++ b/solution.py
@@ -311,18 +311,32 @@
     return over_chan([array] * SLOTS, masks)
 
 
-def edge_body(space_ref, s0, s1, s2, s3, off_ref, core_ref):
-    odd = space_ref[0] % 2 == 1
-    for m, ref in enumerate((s0, s1, s2, s3)):
+def edge_body(cross, space_ref, s0, s1, s2, s3, off_ref, core_ref):
+    slab = space_ref[0]
+    odd, middle = slab % 2 == 1, (slab == 7) | (slab == 8)
+    slots = (s0, s1, s2, s3)
+    for m, ref in enumerate(slots):
         first, last = ref[0], ref[PLANES - 1]
-        off_ref[m] = jnp.where(odd, last, first)
+        outer = jnp.where(odd, last, first)
+        if cross:
+            peer = slots[m ^ 1]
+            outer = jnp.where(middle, jnp.where(odd, peer[PLANES - 1], peer[0]), outer)
+        off_ref[m] = outer
         core_ref[m] = jnp.where(odd, first, last)
 
 
-def borders(space, slots):
-    off, core = call(edge_body, [shape((SLOTS, PIECE, FLAT))] * 2, [], [space], slots, 0)
-    outward = [(i, (i + 1 if i % 2 else i - 1) % 16) for i in range(16)]
-    return [lax.ppermute(off, "space", outward), by_space(core, 1)]
+def outward(slab, chan, cross):
+    if slab in (0, 15):
+        return 16 * slab + (chan ^ 1)
+    there = slab + 1 if slab % 2 else slab - 1
+    return 16 * there + (chan ^ (cross and slab in (7, 8)))
+
+
+def borders(space, slots, cross):
+    body = functools.partial(edge_body, cross)
+    off, core = call(body, [shape((SLOTS, PIECE, FLAT))] * 2, [], [space], slots, 0)
+    pairs = [(16 * i + c, outward(i, c, cross)) for i in range(16) for c in range(16)]
+    return [lax.ppermute(off, ("space", "chan"), pairs), by_space(core, 1)]
 
 
 def add(pieces):
@@ -350,12 +364,11 @@
     pieces = over_chan(split_weight(chan, first_weight, *FIRST, PLAIN), NEAR)
     more = split_weight(chan, second_weight, *SECOND, PASSED)
     in_slots, pieces, more = tie((in_slots, pieces, more))
-    in_slots += borders(space, in_slots)
+    in_slots += borders(space, in_slots, False)
     fwd_first, bwd_first = arrange_weight(pieces, PLAIN)
     one = by_chan(more[1], FAR[2])
     in_slots, fwd_first = tie((in_slots, fwd_first))
-    parts, one = tie((conv(space, fwd_first, in_slots), one))
-    sums = over_chan(parts, NEAR)
+    sums = over_chan(conv(space, fwd_first, in_slots), NEAR)
     sums[1], one = tie((sums[1], one))
     two = by_chan(stitch(more[2], one), FAR[3])
     pre_first = add(sums)
@@ -363,18 +376,17 @@
 
     hid_slots = gather(hidden, NEAR)
     hid_slots, two = tie((hid_slots, two))
-    hid_slots += borders(space, hid_slots)
+    hid_slots += borders(space, hid_slots, True)
     fwd_second, bwd_second = arrange_weight([more[0], one, two], ARRIVED)
     pre_second = add(over_chan(conv(space, fwd_second, hid_slots), FAR))
     features = jax.nn.silu(pre_second).astype(BF)
     err_second = (cotangent.astype(F32) * slope(pre_second)).astype(BF)
 
     err2_slots = gather(err_second, FAR)
-    edge = borders(space, err2_slots)
+    edge = borders(space, err2_slots, False)
     grads = weight_grad(space, hid_slots, err2_slots, PASSED)
     edge, grads = tie((edge, grads))
-    parts, grads = tie((conv(space, bwd_second, err2_slots + edge), grads))
-    sums = over_chan(parts, NEAR)
+    sums = over_chan(conv(space, bwd_second, err2_slots + edge), NEAR)
     one = by_chan(grads[1], FAR[2])
     sums, one = tie((sums, one))
     grad_hidden = add(sums).astype(BF)
@@ -383,19 +395,20 @@
     err1_slots = gather(err_first, NEAR)
     two = by_chan(stitch(grads[2], one), FAR[3])
     err1_slots, two = tie((err1_slots, two))
-    firsts = over_chan(weight_grad(space, in_slots, err1_slots, PLAIN), NEAR)
-    edge = borders(space, err1_slots)
+    firsts, err1_slots = tie((weight_grad(space, in_slots, err1_slots, PLAIN), err1_slots))
+    firsts = over_chan(firsts, NEAR)
+    edge = borders(space, err1_slots, True)
     firsts, edge = tie((firsts, edge))
     keep, give = call(
         keep_body, [shape((HELD, LANES))] * 2, [], [space], [*firsts, grads[0], one, two], 0
     )
     got, parts = tie((by_space(give, 1), conv(space, bwd_first, err1_slots + edge)))
     mine, parts = tie((total([keep, got]), parts))
-    got, far = tie((by_space(mine, 8), by_chan(parts[1], FAR[1])))
+    got, near = tie((by_space(mine, 8), by_chan(parts[2], FAR[2])))
     mine = total([mine, got])
     mine, parts = tie((mine, parts))
     rest = [by_space(mine, 2 * m) for m in (1, 2, 3)]
-    rest, near, side = tie((rest, by_chan(parts[2], FAR[2]), by_chan(parts[3], FAR[3])))
+    rest, far, side = tie((rest, by_chan(parts[1], FAR[1]), by_chan(parts[3], FAR[3])))
     mine = total([mine, *rest])
     grad_first, grad_second = finish(space, chan, mine, by_space(mine, 1))
     grad_inputs = add([parts[0], near, far, side]).astype(BF)

time: 163 us -> 158 us (0.969)
  starting transfers between devices: 89.1 us -> 79.1 us
  waiting for transfers between devices: 54.5 us -> 60.2 us
    ppermute x10, starting transfers between devices: 23.5 us -> 16.2 us  [by_space(): return lax.ppermute(array, 'space', [(i, i ^ mask) for i in range(16)])]
    ppermute x34, waiting for transfers between devices: 53 us -> 57.6 us  [by_chan(): lax.ppermute(array, 'chan', [(i, i ^ mask) for i in range(16)])]
    ppermute x4, waiting for transfers between devices: 0.01 us -> 2.2 us  [borders(): return [lax.ppermute(off, ('space', 'chan'), pairs), by_space(core, 1)]]
    ppermute x34, starting transfers between devices: 48.9 us -> 47.1 us  [by_chan(): lax.ppermute(array, 'chan', [(i, i ^ mask) for i in range(16)])]
  transfers between devices with their start and end apart: 48 -> 48, of which waited for: 27 -> 27; matrix products, arithmetic and copies ran while one was open for 1% -> 1% of each run, Pallas kernels for 7% -> 6%
where the time goes in v1:
time: 158 us
  starting transfers between devices  79.1 us (50%)
  waiting for transfers between devices  60.2 us (38%)
  Pallas kernels  15.4 us (10%)
  other arithmetic  1.73 us (1%)
    ppermute x34, waiting for transfers between devices, by_chan(): lax.ppermute(array, 'chan', [(i, i ^ mask) for i in range(16)])  57.6 us
    ppermute x34, starting transfers between devices, by_chan(): lax.ppermute(array, 'chan', [(i, i ^ mask) for i in range(16)])  47.1 us
    ppermute x10, starting transfers between devices, by_space(): return lax.ppermute(array, 'space', [(i, i ^ mask) for i in range(16)])  16.2 us
    ppermute x4, starting transfers between devices, borders(): return [lax.ppermute(off, ('space', 'chan'), pairs), by_space(core, 1)]  15.8 us
    pallas_call x21, Pallas kernels, call(): pl.pallas_call(body, out_shape=outs, in_specs=[pl.BlockSpec(memory_space=...  15.4 us
  transfers between devices with their start and end apart: 48, of which 27 were waited for; matrix products, arithmetic and copies ran while one was open for 1% of the time, Pallas kernels for 6%

profile of v1, /device:TPU:1, one launch (start us, length us, event | category | flops | bytes accessed | tf_op | source)
XLA Modules:
  0.0 158.3 jit_solution(1769744994941657735)
XLA Ops:
  1.9 2.2 %collective-permute-start.3 = (bf16[224,128]{1,0:T(8,128)(2,1)S(1)}, bf16[224,128]{1,0:T(8,128)(2,1)S(1)}, u32[]{:S(2)}, u32[]{:S(2)}) collective-permute-start(bf16[224,128]{1,0:T(8,128)(2,1)S(1)} %get-tuple-element.126), channel_id=1, source_target_pairs={{0,1},{1,0},{2,3},{3,2},{4,5},{5,4},{6,7},{7,6},{8,9},{9,8},{10,11... | collective-permute-start | bytes 172040 | tf_op jit(solution)/shard_map/ppermute | solution.py:299
  4.2 6.0 %collective-permute-start.2 = (bf16[3,16,1024]{2,1,0:T(8,128)(2,1)}, bf16[3,16,1024]{2,1,0:T(8,128)(2,1)S(1)}, u32[]{:S(2)}, u32[]{:S(2)}) collective-permute-start(bf16[3,16,1024]{2,1,0:T(8,128)(2,1)} %bitcast.15), channel_id=1, source_target_pairs={{0,12},{1,13},{2,14},{3,15},{4,8},{5,9},{6,10},{7,11},{8,4},{9,5},... | collective-permute-start | bytes 294920 | tf_op jit(solution)/shard_map/ppermute | solution.py:299
  14.0 5.8 %collective-permute-done.4.refs_2_ = bf16[224,128]{1,0:T(8,128)(2,1)S(1)} collective-permute-done((bf16[224,128]{1,0:T(8,128)(2,1)S(1)}, bf16[224,128]{1,0:T(8,128)(2,1)S(1)}, u32[]{:S(2)}, u32[]{:S(2)}) %collective-permute-start.4) | collective-permute-done | bytes 57376 | tf_op jit(solution)/shard_map/ppermute | solution.py:299
  19.9 2.9 %collective-permute-done.5.refs_3_ = bf16[224,128]{1,0:T(8,128)(2,1)S(1)} collective-permute-done((bf16[224,128]{1,0:T(8,128)(2,1)S(1)}, bf16[224,128]{1,0:T(8,128)(2,1)S(1)}, u32[]{:S(2)}, u32[]{:S(2)}) %collective-permute-start.5) | collective-permute-done | bytes 57376 | tf_op jit(solution)/shard_map/ppermute | solution.py:299
  22.8 2.6 %collective-permute-start.6 = (bf16[4,16,1024]{2,1,0:T(8,128)(2,1)S(1)}, bf16[4,16,1024]{2,1,0:T(8,128)(2,1)S(1)}, u32[]{:S(2)}, u32[]{:S(2)}) collective-permute-start(bf16[4,16,1024]{2,1,0:T(8,128)(2,1)S(1)} %get-tuple-element.137), channel_id=1, source_target_pairs={{0,1},{1,0},{2,3},{3,2},{4,5},{5,4},{6,7},{7,6},{8,9},{9,8},{10,11... | collective-permute-start | bytes 393224 | tf_op jit(solution)/shard_map/ppermute | solution.py:339
  26.8 1.4 shard_map.78
  28.4 1.3 shard_map.79
  33.6 1.2 collective-permute-start.15
  35.0 3.1 %collective-permute-done.11 = bf16[3,16,1024]{2,1,0:T(8,128)(2,1)S(1)} collective-permute-done((bf16[3,16,1024]{2,1,0:T(8,128)(2,1)S(1)}, bf16[3,16,1024]{2,1,0:T(8,128)(2,1)S(1)}, u32[]{:S(2)}, u32[]{:S(2)}) %collective-permute-start.11) | collective-permute-done | bytes 98336 | tf_op jit(solution)/shard_map/ppermute | solution.py:299
  39.5 1.4 collective-permute-start.12
  40.9 1.9 %collective-permute-done.14.s3.refs_3_ = bf16[3,16,1024]{2,1,0:T(8,128)(2,1)S(1)} collective-permute-done((bf16[3,16,1024]{2,1,0:T(8,128)(2,1)S(1)}, bf16[3,16,1024]{2,1,0:T(8,128)(2,1)S(1)}, u32[]{:S(2)}, u32[]{:S(2)}) %collective-permute-start.14) | collective-permute-done | bytes 98336 | tf_op jit(solution)/shard_map/ppermute | solution.py:299
  43.7 4.6 %collective-permute-start.16 = (bf16[4,16,1024]{2,1,0:T(8,128)(2,1)S(1)}, bf16[4,16,1024]{2,1,0:T(8,128)(2,1)S(1)}, u32[]{:S(2)}, u32[]{:S(2)}) collective-permute-start(bf16[4,16,1024]{2,1,0:T(8,128)(2,1)S(1)} %get-tuple-element.165), channel_id=1, source_target_pairs={{0,1},{1,0},{2,3},{3,2},{4,5},{5,4},{6,7},{7,6},{8,9},{9,8},{10,11... | collective-permute-start | bytes 393224 | tf_op jit(solution)/shard_map/ppermute | solution.py:339
  48.5 1.4 shard_map.81
  49.9 1.4 collective-permute-done.16.refs_4_
  51.3 1.3 shard_map.83
  52.6 2.0 %collective-permute-start.18 = (bf16[3,16,1024]{2,1,0:T(8,128)(2,1)S(1)}, bf16[3,16,1024]{2,1,0:T(8,128)(2,1)S(1)}, u32[]{:S(2)}, u32[]{:S(2)}) collective-permute-start(bf16[3,16,1024]{2,1,0:T(8,128)(2,1)S(1)} %get-tuple-element.168), channel_id=1, source_target_pairs={{0,8},{1,9},{2,10},{3,11},{4,12},{5,13},{6,14},{7,15},{8,0},{9,1},... | collective-permute-start | bytes 294920 | tf_op jit(solution)/shard_map/ppermute | solution.py:299
  54.6 1.4 collective-permute-start.19
  56.0 2.4 %collective-permute-start.20 = (bf16[3,16,1024]{2,1,0:T(8,128)(2,1)S(1)}, bf16[3,16,1024]{2,1,0:T(8,128)(2,1)S(1)}, u32[]{:S(2)}, u32[]{:S(2)}) collective-permute-start(bf16[3,16,1024]{2,1,0:T(8,128)(2,1)S(1)} %get-tuple-element.170), channel_id=1, source_target_pairs={{0,12},{1,13},{2,14},{3,15},{4,8},{5,9},{6,10},{7,11},{8,4},{9,5},... | collective-permute-start | bytes 294920 | tf_op jit(solution)/shard_map/ppermute | solution.py:299
  58.4 2.6 %collective-permute-done.18 = bf16[3,16,1024]{2,1,0:T(8,128)(2,1)S(1)} collective-permute-done((bf16[3,16,1024]{2,1,0:T(8,128)(2,1)S(1)}, bf16[3,16,1024]{2,1,0:T(8,128)(2,1)S(1)}, u32[]{:S(2)}, u32[]{:S(2)}) %collective-permute-start.18) | collective-permute-done | bytes 98336 | tf_op jit(solution)/shard_map/ppermute | solution.py:299
  61.0 4.7 %collective-permute-done.19 = bf16[3,16,1024]{2,1,0:T(8,128)(2,1)S(1)} collective-permute-done((bf16[3,16,1024]{2,1,0:T(8,128)(2,1)S(1)}, bf16[3,16,1024]{2,1,0:T(8,128)(2,1)S(1)}, u32[]{:S(2)}, u32[]{:S(2)}) %collective-permute-start.19) | collective-permute-done | bytes 98336 | tf_op jit(solution)/shard_map/ppermute | solution.py:299
  66.5 3.0 %collective-permute-start.23 = (bf16[3,16,1024]{2,1,0:T(8,128)(2,1)S(1)}, bf16[3,16,1024]{2,1,0:T(8,128)(2,1)S(1)}, u32[]{:S(2)}, u32[]{:S(2)}) collective-permute-start(bf16[3,16,1024]{2,1,0:T(8,128)(2,1)S(1)} %get-tuple-element.246.s0.refs_6_.refs_0_), channel_id=1, source_target_pairs={{0,12},{1,13},{2,14},{3,15},{4,8},{5,9},{6,10},{7,11},{8,4},{9,5},... | collective-permute-start | bytes 294920 | tf_op jit(solution)/shard_map/ppermute | solution.py:299
  70.4 2.1 %collective-permute-start.21 = (bf16[3,16,1024]{2,1,0:T(8,128)(2,1)S(1)}, bf16[3,16,1024]{2,1,0:T(8,128)(2,1)S(1)}, u32[]{:S(2)}, u32[]{:S(2)}) collective-permute-start(bf16[3,16,1024]{2,1,0:T(8,128)(2,1)S(1)} %get-tuple-element.246.s0.refs_6_.refs_0_), channel_id=1, source_target_pairs={{0,8},{1,9},{2,10},{3,11},{4,12},{5,13},{6,14},{7,15},{8,0},{9,1},... | collective-permute-start | bytes 294920 | tf_op jit(solution)/shard_map/ppermute | solution.py:299
  72.4 1.3 collective-permute-done.23.s3.refs_9_.refs_3_
  73.8 2.7 %collective-permute-done.22.s2.refs_8_.refs_2_ = bf16[3,16,1024]{2,1,0:T(8,128)(2,1)S(1)} collective-permute-done((bf16[3,16,1024]{2,1,0:T(8,128)(2,1)S(1)}, bf16[3,16,1024]{2,1,0:T(8,128)(2,1)S(1)}, u32[]{:S(2)}, u32[]{:S(2)}) %collective-permute-start.22) | collective-permute-done | bytes 98336 | tf_op jit(solution)/shard_map/ppermute | solution.py:299
  76.4 4.7 %collective-permute-done.21.s1.refs_7_.refs_1_ = bf16[3,16,1024]{2,1,0:T(8,128)(2,1)S(1)} collective-permute-done((bf16[3,16,1024]{2,1,0:T(8,128)(2,1)S(1)}, bf16[3,16,1024]{2,1,0:T(8,128)(2,1)S(1)}, u32[]{:S(2)}, u32[]{:S(2)}) %collective-permute-start.21) | collective-permute-done | bytes 98336 | tf_op jit(solution)/shard_map/ppermute | solution.py:299
  81.2 1.5 collective-permute-start.24
  83.0 2.4 %shard_map.85 = (bf16[224,128]{1,0:T(8,128)(2,1)S(1)}, bf16[448,128]{1,0:T(8,128)(2,1)S(1)}, bf16[224,128]{1,0:T(8,128)(2,1)S(1)}) custom-call(s32[1]{0:T(128)} %bitcast.space_ref, bf16[3,16,1024]{2,1,0:T(8,128)(2,1)S(1)} %multiply_convert_fusion.2.s0.refs_0_, bf16[3,16,1024]{2,1,0:T(8,128)(2,1)S(1)} %collective-permute-done.12.s1.refs_1_, ...), custom_call_target="tpu_custom_call" | custom-call | flops 679477248 | bytes 1277952 | tf_op jit(solution)/shard_map/pallas_call | solution.py:31
  86.0 2.9 %collective-permute-start.29 = (bf16[448,128]{1,0:T(8,128)(2,1)S(1)}, bf16[448,128]{1,0:T(8,128)(2,1)S(1)}, u32[]{:S(2)}, u32[]{:S(2)}) collective-permute-start(bf16[448,128]{1,0:T(8,128)(2,1)S(1)} %get-tuple-element.183), channel_id=1, source_target_pairs={{0,4},{1,5},{2,6},{3,7},{4,0},{5,1},{6,2},{7,3},{8,12},{9,13},{10,... | collective-permute-start | bytes 344072 | tf_op jit(solution)/shard_map/ppermute | solution.py:299
  88.9 1.4 shard_map.86
  91.4 1.6 collective-permute-start.28
  94.1 1.6 %collective-permute-done.27 = bf16[3,16,1024]{2,1,0:T(8,128)(2,1)S(1)} collective-permute-done((bf16[3,16,1024]{2,1,0:T(8,128)(2,1)S(1)}, bf16[3,16,1024]{2,1,0:T(8,128)(2,1)S(1)}, u32[]{:S(2)}, u32[]{:S(2)}) %collective-permute-start.27) | collective-permute-done | bytes 98336 | tf_op jit(solution)/shard_map/ppermute | solution.py:299
  95.7 3.0 %collective-permute-done.28 = bf16[3,16,1024]{2,1,0:T(8,128)(2,1)S(1)} collective-permute-done((bf16[3,16,1024]{2,1,0:T(8,128)(2,1)S(1)}, bf16[3,16,1024]{2,1,0:T(8,128)(2,1)S(1)}, u32[]{:S(2)}, u32[]{:S(2)}) %collective-permute-start.28) | collective-permute-done | bytes 98336 | tf_op jit(solution)/shard_map/ppermute | solution.py:299
  99.0 1.8 %collective-permute-start.32 = (bf16[3,16,1024]{2,1,0:T(8,128)(2,1)S(1)}, bf16[3,16,1024]{2,1,0:T(8,128)(2,1)S(1)}, u32[]{:S(2)}, u32[]{:S(2)}) collective-permute-start(bf16[3,16,1024]{2,1,0:T(8,128)(2,1)S(1)} %multiply_convert_fusion.refs_6_.s0.refs_0_), channel_id=1, source_target_pairs={{0,3},{1,2},{2,1},{3,0},{4,7},{5,6},{6,5},{7,4},{8,11},{9,10},{10,... | collective-permute-start | bytes 294920 | tf_op jit(solution)/shard_map/ppermute | solution.py:299
  101.9 1.7 %collective-permute-done.32.refs_9_.s3.refs_3_ = bf16[3,16,1024]{2,1,0:T(8,128)(2,1)S(1)} collective-permute-done((bf16[3,16,1024]{2,1,0:T(8,128)(2,1)S(1)}, bf16[3,16,1024]{2,1,0:T(8,128)(2,1)S(1)}, u32[]{:S(2)}, u32[]{:S(2)}) %collective-permute-start.32) | collective-permute-done | bytes 98336 | tf_op jit(solution)/shard_map/ppermute | solution.py:299
  103.7 1.9 %collective-permute-done.31.refs_8_.s2.refs_2_ = bf16[3,16,1024]{2,1,0:T(8,128)(2,1)S(1)} collective-permute-done((bf16[3,16,1024]{2,1,0:T(8,128)(2,1)S(1)}, bf16[3,16,1024]{2,1,0:T(8,128)(2,1)S(1)}, u32[]{:S(2)}, u32[]{:S(2)}) %collective-permute-start.31) | collective-permute-done | bytes 98336 | tf_op jit(solution)/shard_map/ppermute | solution.py:299
  105.6 2.4 %shard_map.88 = (bf16[224,128]{1,0:T(8,128)(2,1)S(1)}, bf16[224,128]{1,0:T(8,128)(2,1)S(1)}, bf16[224,128]{1,0:T(8,128)(2,1)S(1)}, bf16[224,128]{1,0:T(8,128)(2,1)S(1)}) custom-call(s32[1]{0:T(128)} %bitcast.space_ref, bf16[3,16,1024]{2,1,0:T(8,128)(2,1)S(1)} %bitcast.20, bf16[3,16,1024]{2,1,0:T(8,128)(2,1)S(1)} %collective-permute-done.s1.refs_1_, ...), custom_call_target="tpu_custom_call" | custom-call | flops 679477248 | bytes 1277952 | tf_op jit(solution)/shard_map/pallas_call | solution.py:31
  108.1 7.1 %collective-permute-start.37 = (bf16[4,16,1024]{2,1,0:T(8,128)(2,1)S(1)}, bf16[4,16,1024]{2,1,0:T(8,128)(2,1)S(1)}, u32[]{:S(2)}, u32[]{:S(2)}) collective-permute-start(bf16[4,16,1024]{2,1,0:T(8,128)(2,1)S(1)} %get-tuple-element.206), channel_id=1, source_target_pairs={{0,1},{1,0},{2,3},{3,2},{4,5},{5,4},{6,7},{7,6},{8,9},{9,8},{10,11... | collective-permute-start | bytes 393224 | tf_op jit(solution)/shard_map/ppermute | solution.py:339
  118.5 2.7 %collective-permute-done.36.refs_3_ = bf16[224,128]{1,0:T(8,128)(2,1)S(1)} collective-permute-done((bf16[224,128]{1,0:T(8,128)(2,1)S(1)}, bf16[224,128]{1,0:T(8,128)(2,1)S(1)}, u32[]{:S(2)}, u32[]{:S(2)}) %collective-permute-start.36) | collective-permute-done | bytes 57376 | tf_op jit(solution)/shard_map/ppermute | solution.py:299
  121.3 1.7 %collective-permute-start.39 = (bf16[896,128]{1,0:T(8,128)(2,1)S(1)}, bf16[896,128]{1,0:T(8,128)(2,1)S(1)}, u32[]{:S(2)}, u32[]{:S(2)}) collective-permute-start(bf16[896,128]{1,0:T(8,128)(2,1)S(1)} %get-tuple-element.215), channel_id=1, source_target_pairs={{0,16},{16,0},{32,48},{48,32},{64,80},{80,64},{96,112},{112,96},{1... | collective-permute-start | bytes 688136 | tf_op jit(solution)/shard_map/ppermute | solution.py:303
  123.0 1.4 shard_map.91
  124.5 7.9 %collective-permute-start.40 = (bf16[896,128]{1,0:T(8,128)(2,1)S(1)}, bf16[896,128]{1,0:T(8,128)(2,1)S(1)}, u32[]{:S(2)}, u32[]{:S(2)}) collective-permute-start(bf16[896,128]{1,0:T(8,128)(2,1)S(1)} %shard_map.92.refs_0_), channel_id=1, source_target_pairs={{0,128},{16,144},{32,160},{48,176},{64,192},{80,208},{96,224},{112... | collective-permute-start | bytes 688136 | tf_op jit(solution)/shard_map/ppermute | solution.py:303
  133.3 6.2 %collective-permute-done.41 = bf16[3,16,1024]{2,1,0:T(8,128)(2,1)S(1)} collective-permute-done((bf16[3,16,1024]{2,1,0:T(8,128)(2,1)S(1)}, bf16[3,16,1024]{2,1,0:T(8,128)(2,1)S(1)}, u32[]{:S(2)}, u32[]{:S(2)}) %collective-permute-start.41) | collective-permute-done | bytes 98336 | tf_op jit(solution)/shard_map/ppermute | solution.py:299
  140.2 1.4 collective-permute-start.43
  141.5 1.3 collective-permute-start.42
  142.9 3.7 %collective-permute-start.45 = (bf16[3,16,1024]{2,1,0:T(8,128)(2,1)S(1)}, bf16[3,16,1024]{2,1,0:T(8,128)(2,1)S(1)}, u32[]{:S(2)}, u32[]{:S(2)}) collective-permute-start(bf16[3,16,1024]{2,1,0:T(8,128)(2,1)S(1)} %get-tuple-element.235), channel_id=1, source_target_pairs={{0,8},{1,9},{2,10},{3,11},{4,12},{5,13},{6,14},{7,15},{8,0},{9,1},... | collective-permute-start | bytes 294920 | tf_op jit(solution)/shard_map/ppermute | solution.py:299
  146.6 6.7 %collective-permute-done.45 = bf16[3,16,1024]{2,1,0:T(8,128)(2,1)S(1)} collective-permute-done((bf16[3,16,1024]{2,1,0:T(8,128)(2,1)S(1)}, bf16[3,16,1024]{2,1,0:T(8,128)(2,1)S(1)}, u32[]{:S(2)}, u32[]{:S(2)}) %collective-permute-start.45) | collective-permute-done | bytes 98336 | tf_op jit(solution)/shard_map/ppermute | solution.py:299
  153.4 2.5 %collective-permute-start.47 = (bf16[896,128]{1,0:T(8,128)(2,1)S(1)}, bf16[896,128]{1,0:T(8,128)(2,1)S(1)}, u32[]{:S(2)}, u32[]{:S(2)}) collective-permute-start(bf16[896,128]{1,0:T(8,128)(2,1)S(1)} %shard_map.94.mine_ref), channel_id=1, source_target_pairs={{0,16},{16,0},{32,48},{48,32},{64,80},{80,64},{96,112},{112,96},{1... | collective-permute-start | bytes 688136 | tf_op jit(solution)/shard_map/ppermute | solution.py:303
  157.0 1.3 shard_map.95
  (81 shorter events, 25.8 us)
Async XLA Ops:
  1.9 11.1 %collective-permute-start.3 = (bf16[224,128]{1,0:T(8,128)(2,1)S(1)}, bf16[224,128]{1,0:T(8,128)(2,1)S(1)}, u32[]{:S(2)}, u32[]{:S(2)}) collective-permute-start(bf16[224,128]{1,0:T(8,128)(2,1)S(1)} %get-tuple-element.126), channel_id=1, source_target_pairs={{0,1},{1,0},{2,3},{3,2},{4,5},{5,4},{6,7},{7,6},{8,9},{9,8},{10,11... | collective-permute-start | bytes 172040 | tf_op jit(solution)/shard_map/ppermute | solution.py:299
  4.2 18.6 %collective-permute-start.2 = (bf16[3,16,1024]{2,1,0:T(8,128)(2,1)}, bf16[3,16,1024]{2,1,0:T(8,128)(2,1)S(1)}, u32[]{:S(2)}, u32[]{:S(2)}) collective-permute-start(bf16[3,16,1024]{2,1,0:T(8,128)(2,1)} %bitcast.15), channel_id=1, source_target_pairs={{0,12},{1,13},{2,14},{3,15},{4,8},{5,9},{6,10},{7,11},{8,4},{9,5},... | collective-permute-start | bytes 294920 | tf_op jit(solution)/shard_map/ppermute | solution.py:299
  10.2 12.6 %collective-permute-start.1 = (bf16[3,16,1024]{2,1,0:T(8,128)(2,1)}, bf16[3,16,1024]{2,1,0:T(8,128)(2,1)S(1)}, u32[]{:S(2)}, u32[]{:S(2)}) collective-permute-start(bf16[3,16,1024]{2,1,0:T(8,128)(2,1)} %bitcast.16), channel_id=1, source_target_pairs={{0,4},{1,5},{2,6},{3,7},{4,0},{5,1},{6,2},{7,3},{8,12},{9,13},{10,... | collective-permute-start | bytes 294920 | tf_op jit(solution)/shard_map/ppermute | solution.py:299
  11.4 11.4 %collective-permute-start = (bf16[3,16,1024]{2,1,0:T(8,128)(2,1)}, bf16[3,16,1024]{2,1,0:T(8,128)(2,1)S(1)}, u32[]{:S(2)}, u32[]{:S(2)}) collective-permute-start(bf16[3,16,1024]{2,1,0:T(8,128)(2,1)} %bitcast.17), channel_id=1, source_target_pairs={{0,8},{1,9},{2,10},{3,11},{4,12},{5,13},{6,14},{7,15},{8,0},{9,1},... | collective-permute-start | bytes 294920 | tf_op jit(solution)/shard_map/ppermute | solution.py:299
  12.3 7.6 %collective-permute-start.4 = (bf16[224,128]{1,0:T(8,128)(2,1)S(1)}, bf16[224,128]{1,0:T(8,128)(2,1)S(1)}, u32[]{:S(2)}, u32[]{:S(2)}) collective-permute-start(bf16[224,128]{1,0:T(8,128)(2,1)S(1)} %get-tuple-element.127), channel_id=1, source_target_pairs={{0,2},{1,3},{2,0},{3,1},{4,6},{5,7},{6,4},{7,5},{8,10},{9,11},{10,... | collective-permute-start | bytes 172040 | tf_op jit(solution)/shard_map/ppermute | solution.py:299
  13.0 9.7 %collective-permute-start.5 = (bf16[224,128]{1,0:T(8,128)(2,1)S(1)}, bf16[224,128]{1,0:T(8,128)(2,1)S(1)}, u32[]{:S(2)}, u32[]{:S(2)}) collective-permute-start(bf16[224,128]{1,0:T(8,128)(2,1)S(1)} %get-tuple-element.128), channel_id=1, source_target_pairs={{0,3},{1,2},{2,1},{3,0},{4,7},{5,6},{6,5},{7,4},{8,11},{9,10},{10,... | collective-permute-start | bytes 172040 | tf_op jit(solution)/shard_map/ppermute | solution.py:299
  22.8 5.6 %collective-permute-start.6 = (bf16[4,16,1024]{2,1,0:T(8,128)(2,1)S(1)}, bf16[4,16,1024]{2,1,0:T(8,128)(2,1)S(1)}, u32[]{:S(2)}, u32[]{:S(2)}) collective-permute-start(bf16[4,16,1024]{2,1,0:T(8,128)(2,1)S(1)} %get-tuple-element.137), channel_id=1, source_target_pairs={{0,1},{1,0},{2,3},{3,2},{4,5},{5,4},{6,7},{7,6},{8,9},{9,8},{10,11... | collective-permute-start | bytes 393224 | tf_op jit(solution)/shard_map/ppermute | solution.py:339
  25.5 3.0 %collective-permute-start.7 = (bf16[4,16,1024]{2,1,0:T(8,128)(2,1)S(1)}, bf16[4,16,1024]{2,1,0:T(8,128)(2,1)S(1)}, u32[]{:S(2)}, u32[]{:S(2)}) collective-permute-start(bf16[4,16,1024]{2,1,0:T(8,128)(2,1)S(1)} %get-tuple-element.138), channel_id=1, source_target_pairs={{0,16},{16,0},{32,48},{48,32},{64,80},{80,64},{96,112},{112,96},{1... | collective-permute-start | bytes 393224 | tf_op jit(solution)/shard_map/ppermute | solution.py:303
  25.6 7.7 %collective-permute-start.9 = (bf16[448,128]{1,0:T(8,128)(2,1)S(1)}, bf16[448,128]{1,0:T(8,128)(2,1)S(1)}, u32[]{:S(2)}, u32[]{:S(2)}) collective-permute-start(bf16[448,128]{1,0:T(8,128)(2,1)S(1)} %get-tuple-element.152), channel_id=1, source_target_pairs={{0,4},{1,5},{2,6},{3,7},{4,0},{5,1},{6,2},{7,3},{8,12},{9,13},{10,... | collective-permute-start | bytes 344072 | tf_op jit(solution)/shard_map/ppermute | solution.py:299
  29.8 3.8 %collective-permute-start.8 = (bf16[3,16,1024]{2,1,0:T(8,128)(2,1)S(1)}, bf16[3,16,1024]{2,1,0:T(8,128)(2,1)S(1)}, u32[]{:S(2)}, u32[]{:S(2)}) collective-permute-start(bf16[3,16,1024]{2,1,0:T(8,128)(2,1)S(1)} %get-tuple-element.151), channel_id=1, source_target_pairs={{0,1},{1,0},{2,3},{3,2},{4,5},{5,4},{6,7},{7,6},{8,9},{9,8},{10,11... | collective-permute-start | bytes 294920 | tf_op jit(solution)/shard_map/ppermute | solution.py:299
  30.8 4.2 %collective-permute-start.10 = (bf16[3,16,1024]{2,1,0:T(8,128)(2,1)S(1)}, bf16[3,16,1024]{2,1,0:T(8,128)(2,1)S(1)}, u32[]{:S(2)}, u32[]{:S(2)}) collective-permute-start(bf16[3,16,1024]{2,1,0:T(8,128)(2,1)S(1)} %get-tuple-element.156), channel_id=1, source_target_pairs={{0,2},{1,3},{2,0},{3,1},{4,6},{5,7},{6,4},{7,5},{8,10},{9,11},{10,... | collective-permute-start | bytes 294920 | tf_op jit(solution)/shard_map/ppermute | solution.py:299
  31.9 6.2 %collective-permute-start.11 = (bf16[3,16,1024]{2,1,0:T(8,128)(2,1)S(1)}, bf16[3,16,1024]{2,1,0:T(8,128)(2,1)S(1)}, u32[]{:S(2)}, u32[]{:S(2)}) collective-permute-start(bf16[3,16,1024]{2,1,0:T(8,128)(2,1)S(1)} %get-tuple-element.157), channel_id=1, source_target_pairs={{0,3},{1,2},{2,1},{3,0},{4,7},{5,6},{6,5},{7,4},{8,11},{9,10},{10,... | collective-permute-start | bytes 294920 | tf_op jit(solution)/shard_map/ppermute | solution.py:299
  33.6 10.1 %collective-permute-start.15 = (bf16[448,128]{1,0:T(8,128)(2,1)S(1)}, bf16[448,128]{1,0:T(8,128)(2,1)S(1)}, u32[]{:S(2)}, u32[]{:S(2)}) collective-permute-start(bf16[448,128]{1,0:T(8,128)(2,1)S(1)} %shard_map.80), channel_id=1, source_target_pairs={{0,12},{1,13},{2,14},{3,15},{4,8},{5,9},{6,10},{7,11},{8,4},{9,5},... | collective-permute-start | bytes 344072 | tf_op jit(solution)/shard_map/ppermute | solution.py:299
  38.2 4.6 %collective-permute-start.14 = (bf16[3,16,1024]{2,1,0:T(8,128)(2,1)S(1)}, bf16[3,16,1024]{2,1,0:T(8,128)(2,1)S(1)}, u32[]{:S(2)}, u32[]{:S(2)}) collective-permute-start(bf16[3,16,1024]{2,1,0:T(8,128)(2,1)S(1)} %multiply_convert_fusion.2.s0.refs_0_), channel_id=1, source_target_pairs={{0,3},{1,2},{2,1},{3,0},{4,7},{5,6},{6,5},{7,4},{8,11},{9,10},{10,... | collective-permute-start | bytes 294920 | tf_op jit(solution)/shard_map/ppermute | solution.py:299
  38.3 4.5 %collective-permute-start.13 = (bf16[3,16,1024]{2,1,0:T(8,128)(2,1)S(1)}, bf16[3,16,1024]{2,1,0:T(8,128)(2,1)S(1)}, u32[]{:S(2)}, u32[]{:S(2)}) collective-permute-start(bf16[3,16,1024]{2,1,0:T(8,128)(2,1)S(1)} %multiply_convert_fusion.2.s0.refs_0_), channel_id=1, source_target_pairs={{0,2},{1,3},{2,0},{3,1},{4,6},{5,7},{6,4},{7,5},{8,10},{9,11},{10,... | collective-permute-start | bytes 294920 | tf_op jit(solution)/shard_map/ppermute | solution.py:299
  39.5 4.2 %collective-permute-start.12 = (bf16[3,16,1024]{2,1,0:T(8,128)(2,1)S(1)}, bf16[3,16,1024]{2,1,0:T(8,128)(2,1)S(1)}, u32[]{:S(2)}, u32[]{:S(2)}) collective-permute-start(bf16[3,16,1024]{2,1,0:T(8,128)(2,1)S(1)} %multiply_convert_fusion.2.s0.refs_0_), channel_id=1, source_target_pairs={{0,1},{1,0},{2,3},{3,2},{4,5},{5,4},{6,7},{7,6},{8,9},{9,8},{10,11... | collective-permute-start | bytes 294920 | tf_op jit(solution)/shard_map/ppermute | solution.py:299
  43.7 7.6 %collective-permute-start.16 = (bf16[4,16,1024]{2,1,0:T(8,128)(2,1)S(1)}, bf16[4,16,1024]{2,1,0:T(8,128)(2,1)S(1)}, u32[]{:S(2)}, u32[]{:S(2)}) collective-permute-start(bf16[4,16,1024]{2,1,0:T(8,128)(2,1)S(1)} %get-tuple-element.165), channel_id=1, source_target_pairs={{0,1},{1,0},{2,3},{3,2},{4,5},{5,4},{6,7},{7,6},{8,9},{9,8},{10,11... | collective-permute-start | bytes 393224 | tf_op jit(solution)/shard_map/ppermute | solution.py:339
  48.3 3.0 %collective-permute-start.17 = (bf16[4,16,1024]{2,1,0:T(8,128)(2,1)S(1)}, bf16[4,16,1024]{2,1,0:T(8,128)(2,1)S(1)}, u32[]{:S(2)}, u32[]{:S(2)}) collective-permute-start(bf16[4,16,1024]{2,1,0:T(8,128)(2,1)S(1)} %get-tuple-element.166), channel_id=1, source_target_pairs={{0,16},{16,0},{32,48},{48,32},{64,80},{80,64},{96,112},{112,96},{1... | collective-permute-start | bytes 393224 | tf_op jit(solution)/shard_map/ppermute | solution.py:303
  52.6 8.4 %collective-permute-start.18 = (bf16[3,16,1024]{2,1,0:T(8,128)(2,1)S(1)}, bf16[3,16,1024]{2,1,0:T(8,128)(2,1)S(1)}, u32[]{:S(2)}, u32[]{:S(2)}) collective-permute-start(bf16[3,16,1024]{2,1,0:T(8,128)(2,1)S(1)} %get-tuple-element.168), channel_id=1, source_target_pairs={{0,8},{1,9},{2,10},{3,11},{4,12},{5,13},{6,14},{7,15},{8,0},{9,1},... | collective-permute-start | bytes 294920 | tf_op jit(solution)/shard_map/ppermute | solution.py:299
  54.6 11.1 %collective-permute-start.19 = (bf16[3,16,1024]{2,1,0:T(8,128)(2,1)S(1)}, bf16[3,16,1024]{2,1,0:T(8,128)(2,1)S(1)}, u32[]{:S(2)}, u32[]{:S(2)}) collective-permute-start(bf16[3,16,1024]{2,1,0:T(8,128)(2,1)S(1)} %get-tuple-element.169), channel_id=1, source_target_pairs={{0,4},{1,5},{2,6},{3,7},{4,0},{5,1},{6,2},{7,3},{8,12},{9,13},{10,... | collective-permute-start | bytes 294920 | tf_op jit(solution)/shard_map/ppermute | solution.py:299
  56.0 9.7 %collective-permute-start.20 = (bf16[3,16,1024]{2,1,0:T(8,128)(2,1)S(1)}, bf16[3,16,1024]{2,1,0:T(8,128)(2,1)S(1)}, u32[]{:S(2)}, u32[]{:S(2)}) collective-permute-start(bf16[3,16,1024]{2,1,0:T(8,128)(2,1)S(1)} %get-tuple-element.170), channel_id=1, source_target_pairs={{0,12},{1,13},{2,14},{3,15},{4,8},{5,9},{6,10},{7,11},{8,4},{9,5},... | collective-permute-start | bytes 294920 | tf_op jit(solution)/shard_map/ppermute | solution.py:299
  66.5 7.3 %collective-permute-start.23 = (bf16[3,16,1024]{2,1,0:T(8,128)(2,1)S(1)}, bf16[3,16,1024]{2,1,0:T(8,128)(2,1)S(1)}, u32[]{:S(2)}, u32[]{:S(2)}) collective-permute-start(bf16[3,16,1024]{2,1,0:T(8,128)(2,1)S(1)} %get-tuple-element.246.s0.refs_6_.refs_0_), channel_id=1, source_target_pairs={{0,12},{1,13},{2,14},{3,15},{4,8},{5,9},{6,10},{7,11},{8,4},{9,5},... | collective-permute-start | bytes 294920 | tf_op jit(solution)/shard_map/ppermute | solution.py:299
  69.5 7.0 %collective-permute-start.22 = (bf16[3,16,1024]{2,1,0:T(8,128)(2,1)S(1)}, bf16[3,16,1024]{2,1,0:T(8,128)(2,1)S(1)}, u32[]{:S(2)}, u32[]{:S(2)}) collective-permute-start(bf16[3,16,1024]{2,1,0:T(8,128)(2,1)S(1)} %get-tuple-element.246.s0.refs_6_.refs_0_), channel_id=1, source_target_pairs={{0,4},{1,5},{2,6},{3,7},{4,0},{5,1},{6,2},{7,3},{8,12},{9,13},{10,... | collective-permute-start | bytes 294920 | tf_op jit(solution)/shard_map/ppermute | solution.py:299
  70.4 10.8 %collective-permute-start.21 = (bf16[3,16,1024]{2,1,0:T(8,128)(2,1)S(1)}, bf16[3,16,1024]{2,1,0:T(8,128)(2,1)S(1)}, u32[]{:S(2)}, u32[]{:S(2)}) collective-permute-start(bf16[3,16,1024]{2,1,0:T(8,128)(2,1)S(1)} %get-tuple-element.246.s0.refs_6_.refs_0_), channel_id=1, source_target_pairs={{0,8},{1,9},{2,10},{3,11},{4,12},{5,13},{6,14},{7,15},{8,0},{9,1},... | collective-permute-start | bytes 294920 | tf_op jit(solution)/shard_map/ppermute | solution.py:299
  81.2 4.8 %collective-permute-start.24 = (bf16[4,16,1024]{2,1,0:T(8,128)(2,1)S(1)}, bf16[4,16,1024]{2,1,0:T(8,128)(2,1)S(1)}, u32[]{:S(2)}, u32[]{:S(2)}) collective-permute-start(bf16[4,16,1024]{2,1,0:T(8,128)(2,1)S(1)} %get-tuple-element.172), channel_id=1, source_target_pairs={{0,1},{1,0},{2,3},{3,2},{4,5},{5,4},{6,7},{7,6},{8,9},{9,8},{10,11... | collective-permute-start | bytes 393224 | tf_op jit(solution)/shard_map/ppermute | solution.py:339
  82.7 3.3 %collective-permute-start.25 = (bf16[4,16,1024]{2,1,0:T(8,128)(2,1)S(1)}, bf16[4,16,1024]{2,1,0:T(8,128)(2,1)S(1)}, u32[]{:S(2)}, u32[]{:S(2)}) collective-permute-start(bf16[4,16,1024]{2,1,0:T(8,128)(2,1)S(1)} %get-tuple-element.173), channel_id=1, source_target_pairs={{0,16},{16,0},{32,48},{48,32},{64,80},{80,64},{96,112},{112,96},{1... | collective-permute-start | bytes 393224 | tf_op jit(solution)/shard_map/ppermute | solution.py:303
  86.0 12.7 %collective-permute-start.29 = (bf16[448,128]{1,0:T(8,128)(2,1)S(1)}, bf16[448,128]{1,0:T(8,128)(2,1)S(1)}, u32[]{:S(2)}, u32[]{:S(2)}) collective-permute-start(bf16[448,128]{1,0:T(8,128)(2,1)S(1)} %get-tuple-element.183), channel_id=1, source_target_pairs={{0,4},{1,5},{2,6},{3,7},{4,0},{5,1},{6,2},{7,3},{8,12},{9,13},{10,... | collective-permute-start | bytes 344072 | tf_op jit(solution)/shard_map/ppermute | solution.py:299
  90.2 3.8 %collective-permute-start.26 = (bf16[3,16,1024]{2,1,0:T(8,128)(2,1)S(1)}, bf16[3,16,1024]{2,1,0:T(8,128)(2,1)S(1)}, u32[]{:S(2)}, u32[]{:S(2)}) collective-permute-start(bf16[3,16,1024]{2,1,0:T(8,128)(2,1)S(1)} %get-tuple-element.180), channel_id=1, source_target_pairs={{0,1},{1,0},{2,3},{3,2},{4,5},{5,4},{6,7},{7,6},{8,9},{9,8},{10,11... | collective-permute-start | bytes 294920 | tf_op jit(solution)/shard_map/ppermute | solution.py:299
  91.4 4.3 %collective-permute-start.27 = (bf16[3,16,1024]{2,1,0:T(8,128)(2,1)S(1)}, bf16[3,16,1024]{2,1,0:T(8,128)(2,1)S(1)}, u32[]{:S(2)}, u32[]{:S(2)}) collective-permute-start(bf16[3,16,1024]{2,1,0:T(8,128)(2,1)S(1)} %get-tuple-element.181), channel_id=1, source_target_pairs={{0,2},{1,3},{2,0},{3,1},{4,6},{5,7},{6,4},{7,5},{8,10},{9,11},{10,... | collective-permute-start | bytes 294920 | tf_op jit(solution)/shard_map/ppermute | solution.py:299
  91.4 7.3 %collective-permute-start.28 = (bf16[3,16,1024]{2,1,0:T(8,128)(2,1)S(1)}, bf16[3,16,1024]{2,1,0:T(8,128)(2,1)S(1)}, u32[]{:S(2)}, u32[]{:S(2)}) collective-permute-start(bf16[3,16,1024]{2,1,0:T(8,128)(2,1)S(1)} %get-tuple-element.182), channel_id=1, source_target_pairs={{0,3},{1,2},{2,1},{3,0},{4,7},{5,6},{6,5},{7,4},{8,11},{9,10},{10,... | collective-permute-start | bytes 294920 | tf_op jit(solution)/shard_map/ppermute | solution.py:299
  98.7 6.9 %collective-permute-start.33 = (bf16[448,128]{1,0:T(8,128)(2,1)S(1)}, bf16[448,128]{1,0:T(8,128)(2,1)S(1)}, u32[]{:S(2)}, u32[]{:S(2)}) collective-permute-start(bf16[448,128]{1,0:T(8,128)(2,1)S(1)} %shard_map.87), channel_id=1, source_target_pairs={{0,12},{1,13},{2,14},{3,15},{4,8},{5,9},{6,10},{7,11},{8,4},{9,5},... | collective-permute-start | bytes 344072 | tf_op jit(solution)/shard_map/ppermute | solution.py:299
  99.0 4.7 %collective-permute-start.32 = (bf16[3,16,1024]{2,1,0:T(8,128)(2,1)S(1)}, bf16[3,16,1024]{2,1,0:T(8,128)(2,1)S(1)}, u32[]{:S(2)}, u32[]{:S(2)}) collective-permute-start(bf16[3,16,1024]{2,1,0:T(8,128)(2,1)S(1)} %multiply_convert_fusion.refs_6_.s0.refs_0_), channel_id=1, source_target_pairs={{0,3},{1,2},{2,1},{3,0},{4,7},{5,6},{6,5},{7,4},{8,11},{9,10},{10,... | collective-permute-start | bytes 294920 | tf_op jit(solution)/shard_map/ppermute | solution.py:299
  100.8 4.8 %collective-permute-start.31 = (bf16[3,16,1024]{2,1,0:T(8,128)(2,1)S(1)}, bf16[3,16,1024]{2,1,0:T(8,128)(2,1)S(1)}, u32[]{:S(2)}, u32[]{:S(2)}) collective-permute-start(bf16[3,16,1024]{2,1,0:T(8,128)(2,1)S(1)} %multiply_convert_fusion.refs_6_.s0.refs_0_), channel_id=1, source_target_pairs={{0,2},{1,3},{2,0},{3,1},{4,6},{5,7},{6,4},{7,5},{8,10},{9,11},{10,... | collective-permute-start | bytes 294920 | tf_op jit(solution)/shard_map/ppermute | solution.py:299
  100.9 4.7 %collective-permute-start.30 = (bf16[3,16,1024]{2,1,0:T(8,128)(2,1)S(1)}, bf16[3,16,1024]{2,1,0:T(8,128)(2,1)S(1)}, u32[]{:S(2)}, u32[]{:S(2)}) collective-permute-start(bf16[3,16,1024]{2,1,0:T(8,128)(2,1)S(1)} %multiply_convert_fusion.refs_6_.s0.refs_0_), channel_id=1, source_target_pairs={{0,1},{1,0},{2,3},{3,2},{4,5},{5,4},{6,7},{7,6},{8,9},{9,8},{10,11... | collective-permute-start | bytes 294920 | tf_op jit(solution)/shard_map/ppermute | solution.py:299
  108.1 13.2 %collective-permute-start.37 = (bf16[4,16,1024]{2,1,0:T(8,128)(2,1)S(1)}, bf16[4,16,1024]{2,1,0:T(8,128)(2,1)S(1)}, u32[]{:S(2)}, u32[]{:S(2)}) collective-permute-start(bf16[4,16,1024]{2,1,0:T(8,128)(2,1)S(1)} %get-tuple-element.206), channel_id=1, source_target_pairs={{0,1},{1,0},{2,3},{3,2},{4,5},{5,4},{6,7},{7,6},{8,9},{9,8},{10,11... | collective-permute-start | bytes 393224 | tf_op jit(solution)/shard_map/ppermute | solution.py:339
  115.1 6.1 %collective-permute-start.38 = (bf16[4,16,1024]{2,1,0:T(8,128)(2,1)S(1)}, bf16[4,16,1024]{2,1,0:T(8,128)(2,1)S(1)}, u32[]{:S(2)}, u32[]{:S(2)}) collective-permute-start(bf16[4,16,1024]{2,1,0:T(8,128)(2,1)S(1)} %get-tuple-element.207), channel_id=1, source_target_pairs={{0,16},{16,0},{32,48},{48,32},{64,80},{80,64},{96,112},{112,96},{1... | collective-permute-start | bytes 393224 | tf_op jit(solution)/shard_map/ppermute | solution.py:303
  115.1 3.0 %collective-permute-start.34 = (bf16[224,128]{1,0:T(8,128)(2,1)S(1)}, bf16[224,128]{1,0:T(8,128)(2,1)S(1)}, u32[]{:S(2)}, u32[]{:S(2)}) collective-permute-start(bf16[224,128]{1,0:T(8,128)(2,1)S(1)} %get-tuple-element.199), channel_id=1, source_target_pairs={{0,1},{1,0},{2,3},{3,2},{4,5},{5,4},{6,7},{7,6},{8,9},{9,8},{10,11... | collective-permute-start | bytes 172040 | tf_op jit(solution)/shard_map/ppermute | solution.py:299
  115.5 3.0 %collective-permute-start.35 = (bf16[224,128]{1,0:T(8,128)(2,1)S(1)}, bf16[224,128]{1,0:T(8,128)(2,1)S(1)}, u32[]{:S(2)}, u32[]{:S(2)}) collective-permute-start(bf16[224,128]{1,0:T(8,128)(2,1)S(1)} %get-tuple-element.200), channel_id=1, source_target_pairs={{0,2},{1,3},{2,0},{3,1},{4,6},{5,7},{6,4},{7,5},{8,10},{9,11},{10,... | collective-permute-start | bytes 172040 | tf_op jit(solution)/shard_map/ppermute | solution.py:299
  116.7 4.5 %collective-permute-start.36 = (bf16[224,128]{1,0:T(8,128)(2,1)S(1)}, bf16[224,128]{1,0:T(8,128)(2,1)S(1)}, u32[]{:S(2)}, u32[]{:S(2)}) collective-permute-start(bf16[224,128]{1,0:T(8,128)(2,1)S(1)} %get-tuple-element.201), channel_id=1, source_target_pairs={{0,3},{1,2},{2,1},{3,0},{4,7},{5,6},{6,5},{7,4},{8,11},{9,10},{10,... | collective-permute-start | bytes 172040 | tf_op jit(solution)/shard_map/ppermute | solution.py:299
  121.3 3.1 %collective-permute-start.39 = (bf16[896,128]{1,0:T(8,128)(2,1)S(1)}, bf16[896,128]{1,0:T(8,128)(2,1)S(1)}, u32[]{:S(2)}, u32[]{:S(2)}) collective-permute-start(bf16[896,128]{1,0:T(8,128)(2,1)S(1)} %get-tuple-element.215), channel_id=1, source_target_pairs={{0,16},{16,0},{32,48},{48,32},{64,80},{80,64},{96,112},{112,96},{1... | collective-permute-start | bytes 688136 | tf_op jit(solution)/shard_map/ppermute | solution.py:303
  124.5 15.0 %collective-permute-start.40 = (bf16[896,128]{1,0:T(8,128)(2,1)S(1)}, bf16[896,128]{1,0:T(8,128)(2,1)S(1)}, u32[]{:S(2)}, u32[]{:S(2)}) collective-permute-start(bf16[896,128]{1,0:T(8,128)(2,1)S(1)} %shard_map.92.refs_0_), channel_id=1, source_target_pairs={{0,128},{16,144},{32,160},{48,176},{64,192},{80,208},{96,224},{112... | collective-permute-start | bytes 688136 | tf_op jit(solution)/shard_map/ppermute | solution.py:303
  132.4 7.1 %collective-permute-start.41 = (bf16[3,16,1024]{2,1,0:T(8,128)(2,1)S(1)}, bf16[3,16,1024]{2,1,0:T(8,128)(2,1)S(1)}, u32[]{:S(2)}, u32[]{:S(2)}) collective-permute-start(bf16[3,16,1024]{2,1,0:T(8,128)(2,1)S(1)} %get-tuple-element.229), channel_id=1, source_target_pairs={{0,4},{1,5},{2,6},{3,7},{4,0},{5,1},{6,2},{7,3},{8,12},{9,13},{10,... | collective-permute-start | bytes 294920 | tf_op jit(solution)/shard_map/ppermute | solution.py:299
  139.5 13.7 %collective-permute-start.44 = (bf16[896,128]{1,0:T(8,128)(2,1)S(1)}, bf16[896,128]{1,0:T(8,128)(2,1)S(1)}, u32[]{:S(2)}, u32[]{:S(2)}) collective-permute-start(bf16[896,128]{1,0:T(8,128)(2,1)S(1)} %shard_map.93.refs_0_), channel_id=1, source_target_pairs={{0,96},{16,112},{32,64},{48,80},{64,32},{80,48},{96,0},{112,16},{1... | collective-permute-start | bytes 688136 | tf_op jit(solution)/shard_map/ppermute | solution.py:303
  140.2 13.1 %collective-permute-start.43 = (bf16[896,128]{1,0:T(8,128)(2,1)S(1)}, bf16[896,128]{1,0:T(8,128)(2,1)S(1)}, u32[]{:S(2)}, u32[]{:S(2)}) collective-permute-start(bf16[896,128]{1,0:T(8,128)(2,1)S(1)} %shard_map.93.refs_0_), channel_id=1, source_target_pairs={{0,64},{16,80},{32,96},{48,112},{64,0},{80,16},{96,32},{112,48},{1... | collective-permute-start | bytes 688136 | tf_op jit(solution)/shard_map/ppermute | solution.py:303
  141.5 11.7 %collective-permute-start.42 = (bf16[896,128]{1,0:T(8,128)(2,1)S(1)}, bf16[896,128]{1,0:T(8,128)(2,1)S(1)}, u32[]{:S(2)}, u32[]{:S(2)}) collective-permute-start(bf16[896,128]{1,0:T(8,128)(2,1)S(1)} %shard_map.93.refs_0_), channel_id=1, source_target_pairs={{0,32},{16,48},{32,0},{48,16},{64,96},{80,112},{96,64},{112,80},{1... | collective-permute-start | bytes 688136 | tf_op jit(solution)/shard_map/ppermute | solution.py:303
  142.9 10.4 %collective-permute-start.45 = (bf16[3,16,1024]{2,1,0:T(8,128)(2,1)S(1)}, bf16[3,16,1024]{2,1,0:T(8,128)(2,1)S(1)}, u32[]{:S(2)}, u32[]{:S(2)}) collective-permute-start(bf16[3,16,1024]{2,1,0:T(8,128)(2,1)S(1)} %get-tuple-element.235), channel_id=1, source_target_pairs={{0,8},{1,9},{2,10},{3,11},{4,12},{5,13},{6,14},{7,15},{8,0},{9,1},... | collective-permute-start | bytes 294920 | tf_op jit(solution)/shard_map/ppermute | solution.py:299
  146.6 6.7 %collective-permute-start.46 = (bf16[3,16,1024]{2,1,0:T(8,128)(2,1)S(1)}, bf16[3,16,1024]{2,1,0:T(8,128)(2,1)S(1)}, u32[]{:S(2)}, u32[]{:S(2)}) collective-permute-start(bf16[3,16,1024]{2,1,0:T(8,128)(2,1)S(1)} %get-tuple-element.236), channel_id=1, source_target_pairs={{0,12},{1,13},{2,14},{3,15},{4,8},{5,9},{6,10},{7,11},{8,4},{9,5},... | collective-permute-start | bytes 294920 | tf_op jit(solution)/shard_map/ppermute | solution.py:299
  153.4 3.6 %collective-permute-start.47 = (bf16[896,128]{1,0:T(8,128)(2,1)S(1)}, bf16[896,128]{1,0:T(8,128)(2,1)S(1)}, u32[]{:S(2)}, u32[]{:S(2)}) collective-permute-start(bf16[896,128]{1,0:T(8,128)(2,1)S(1)} %shard_map.94.mine_ref), channel_id=1, source_target_pairs={{0,16},{16,0},{32,48},{48,32},{64,80},{80,64},{96,112},{112,96},{1... | collective-permute-start | bytes 688136 | tf_op jit(solution)/shard_map/ppermute | solution.py:303
  (4 other events, 36.5 us)

commit v2 on v1

--- a/solution.py
+++ b/solution.py
@@ -52,8 +52,7 @@
 
 
 HALF = 14 * PIECE
-TALL, SPLIT = 9 * PIECE, 5 * PIECE
-GRAD_ROWS = TALL + SPLIT
+GRAD_ROWS = 14 * PIECE
 HELD = SLOTS * GRAD_ROWS
 PLAIN = ((0, 0), (1, 0), (2, 0), (3, 0))
 PASSED = ((0, 0), (1, HALF), (1, 0), (2, 0))
@@ -93,7 +92,6 @@
 
 
 def arrange_body(spots, *refs):
-    fwd_ref, bwd_ref = refs[-2:]
     for a in range(3):
         for b in range(3):
             for c in range(3):
@@ -102,17 +100,31 @@
                 block = jnp.concatenate(
                     [refs[j][at + row : at + row + PIECE, lane : lane + BLOCK] for j, at in spots], axis=0
                 )
-                turned = block.astype(F32).T.astype(BF)
                 at = COLS * b + BLOCK * a
-                fwd_ref[BLOCK * c : BLOCK * (c + 1), at : at + BLOCK] = block
-                at = COLS * (2 - b) + BLOCK * (2 - a)
-                bwd_ref[BLOCK * (2 - c) : BLOCK * (3 - c), at : at + BLOCK] = turned
+                refs[-1][BLOCK * c : BLOCK * (c + 1), at : at + BLOCK] = block
 
 
 def arrange_weight(pieces, spots):
     return call(
-        functools.partial(arrange_body, spots), [shape((COLS, ROWS))] * 2, [], [], pieces, 0
-    )
+        functools.partial(arrange_body, spots), [shape((COLS, ROWS))], [], [], pieces, 0
+    )[0]
+
+
+def turn_body(fwd_ref, bwd_ref):
+    for a in range(3):
+        for b in range(3):
+
+            @pl.loop(0, 3)
+            def _(c):
+                here = pl.ds(pl.multiple_of(BLOCK * c, BLOCK), BLOCK)
+                there = pl.ds(pl.multiple_of(BLOCK * (2 - c), BLOCK), BLOCK)
+                at, to = COLS * b + BLOCK * a, COLS * (2 - b) + BLOCK * (2 - a)
+                block = fwd_ref[here, at : at + BLOCK].astype(F32)
+                bwd_ref[there, to : to + BLOCK] = block.T.astype(BF)
+
+
+def turn_weight(weight):
+    return call(turn_body, [shape((COLS, ROWS))], [], [], [weight], 0)[0]
 
 
 def edges():
@@ -142,15 +154,19 @@
     return jnp.concatenate([end, moved[:, LANES:]], axis=1)
 
 
+def lift_one(p, up, field, down, cell):
+    plane = pl.ds(pl.multiple_of(BLOCK * p, BLOCK), BLOCK)
+    rows = field[plane, :].astype(F32)
+    down[plane, :] = lift(rows, SIDE, cell).astype(BF)
+    up[plane, :] = lift(rows, -SIDE, cell).astype(BF)
+
+
 def conv_body(space_ref, weight_ref, *refs):
     own_ref, o1, o2, o3, up, field, down = refs[-7:]
     fill(space_ref[0], refs[:-7], field)
     cell, col = edges()
     for p in range(PLANES + 2):
-        plane = slice(BLOCK * p, BLOCK * (p + 1))
-        rows = field[plane, :].astype(F32)
-        down[plane, :] = lift(rows, SIDE, cell).astype(BF)
-        up[plane, :] = lift(rows, -SIDE, cell).astype(BF)
+        lift_one(p, up, field, down, cell)
     weight = weight_ref[...]
     for d in range(PLANES):
         window = slice(BLOCK * d, BLOCK * d + COLS)
@@ -179,64 +195,57 @@
     )
 
 
-def moves(err, cell, col):
-    for c in range(3):
-        if c == 0:
-            one = jnp.where(col < SIDE - 1, pltpu.roll(err, FLAT - 1, 1), 0.0)
-        elif c == 2:
-            one = jnp.where(col >= 1, pltpu.roll(err, 1, 1), 0.0)
-        else:
-            one = err
-        for b in range(3):
-            if b == 0:
-                two = jnp.where(cell < FLAT - SIDE, pltpu.roll(one, FLAT - SIDE, 1), 0.0)
-            elif b == 2:
-                two = jnp.where(cell >= SIDE, pltpu.roll(one, SIDE, 1), 0.0)
-            else:
-                two = one
-            yield 3 * b + c, two.astype(BF)
-
-
 def across(lhs, rhs):
     return lax.dot_general(lhs, rhs, (((1,), (1,)), ((), ())), preferred_element_type=F32)
 
 
-def grad_body(spots, space_ref, *refs):
+def looped(count):
+    return pl.loop(0, count)
+
+
+def straight(count):
+    return lambda step: [step(i) for i in range(count)]
+
+
+def grad_body(spots, each, space_ref, *refs):
     slots, errs = refs[:6], refs[6:10]
-    outs, (field, moved, total) = refs[10:-3], refs[-3:]
+    outs, (up, field, down, moved, total) = refs[10:-5], refs[-5:]
     fill(space_ref[0], slots, field)
     cell, col = edges()
-    total[...] = jnp.zeros((ROWS, COLS), F32)
-
-    @pl.loop(0, PLANES)
+    each(PLANES + 2)(lambda p: lift_one(p, up, field, down, cell))
+    total[...] = jnp.zeros((COLS, ROWS), F32)
+
+    @each(PLANES)
     def _(d):
-        err = jnp.concatenate([e[d] for e in errs], axis=0).astype(F32)
-        for q, two in moves(err, cell, col):
-            for n in range(SLOTS):
-                at = n * TALL + q * PIECE
-                moved[at : at + PIECE, :] = two[PIECE * n : PIECE * (n + 1)]
-        rows = pl.ds(pl.multiple_of(BLOCK * d, BLOCK), COLS)
-        total[...] += across(moved[...], field[rows, :])
-
-    for n in range(SLOTS):
-        part = total[n * TALL : (n + 1) * TALL, :].astype(BF)
-        out, at = outs[spots[n][0]], spots[n][1]
-        end = at + GRAD_ROWS
-        out[at : at + TALL, :] = part[:, : 2 * BLOCK]
-        out[at + TALL : end, :BLOCK] = part[:SPLIT, 2 * BLOCK :]
-        out[at + TALL : end - PIECE, BLOCK:] = part[SPLIT:, 2 * BLOCK :]
-        out[end - PIECE : end, BLOCK:] = jnp.zeros((PIECE, BLOCK), BF)
-
-
-def weight_grad(space, slots, errs, sent):
+        err = jnp.concatenate([e[d] for e in errs], axis=0)
+        wide = err.astype(F32)
+        left = jnp.where(col < SIDE - 1, pltpu.roll(wide, FLAT - 1, 1), 0.0)
+        right = jnp.where(col >= 1, pltpu.roll(wide, 1, 1), 0.0)
+        moved[:BLOCK, :] = left.astype(BF)
+        moved[BLOCK : 2 * BLOCK, :] = err
+        moved[2 * BLOCK :, :] = right.astype(BF)
+        window = pl.ds(pl.multiple_of(BLOCK * d, BLOCK), COLS)
+        for b, rows in enumerate((up, field, down)):
+            part, at = across(moved[...], rows[window, :]), slice(COLS * b, COLS * (b + 1))
+            total[:, at] += part
+    for n, (k, at) in enumerate(spots):
+        part = jnp.concatenate(
+            [total[BLOCK * c + PIECE * n : BLOCK * c + PIECE * (n + 1), :] for c in range(3)], axis=0
+        ).astype(BF)
+        out = outs[k]
+        for j in range(4):
+            out[at + 48 * j : at + 48 * (j + 1), :] = part[:, LANES * j : LANES * (j + 1)]
+        out[at + 192 : at + 224, :BLOCK] = part[:32, 4 * LANES :]
+        out[at + 192 : at + 208, BLOCK:] = part[32:, 4 * LANES :]
+        out[at + 208 : at + 224, BLOCK:] = jnp.zeros((PIECE, BLOCK), BF)
+
+
+def weight_grad(space, slots, errs, sent, each):
     return call(
-        functools.partial(grad_body, sent),
+        functools.partial(grad_body, sent, each),
         [shape((HALF * sum(k == j for k, _ in sent), LANES)) for j in range(1 + max(sent)[0])],
-        [
-            pltpu.VMEM((BLOCK * (PLANES + 2), FLAT), BF),
-            pltpu.VMEM((ROWS, FLAT), BF),
-            pltpu.VMEM((ROWS, COLS), F32),
-        ],
+        [pltpu.VMEM((BLOCK * (PLANES + 2), FLAT), BF)] * 3
+        + [pltpu.VMEM((COLS, FLAT), BF), pltpu.VMEM((COLS, ROWS), F32)],
         [space],
         [*slots, *errs],
         2 * ROWS * COLS * FLAT * PLANES,
@@ -247,17 +256,25 @@
     odd = space_ref[0] % 2 == 1
     pieces, (keep_ref, give_ref) = refs[:-2], refs[-2:]
     for n, (k, at) in enumerate(ARRIVED):
-        first, second = pieces[n][...], pieces[SLOTS + k][at : at + GRAD_ROWS, :]
-        rows = slice(n * GRAD_ROWS, (n + 1) * GRAD_ROWS)
-        keep_ref[rows, :] = jnp.where(odd, second, first)
-        give_ref[rows, :] = jnp.where(odd, first, second)
+
+        @pl.loop(0, GRAD_ROWS, step=PIECE * 2)
+        def _(i):
+            here, there, rows = (
+                pl.ds(pl.multiple_of(start + i, PIECE), PIECE * 2) for start in (0, at, n * GRAD_ROWS)
+            )
+            first, second = pieces[n][here, :], pieces[SLOTS + k][there, :]
+            keep_ref[rows, :] = jnp.where(odd, second, first)
+            give_ref[rows, :] = jnp.where(odd, first, second)
 
 
 def total_body(*refs):
-    terms = [ref[...].astype(F32) for ref in refs[:-1]]
-    while len(terms) > 1:
-        terms = [left + right for left, right in zip(terms[::2], terms[1::2])]
-    refs[-1][...] = terms[0].astype(BF)
+    @pl.loop(0, 7)
+    def _(i):
+        rows = pl.ds(pl.multiple_of(LANES * i, LANES), LANES)
+        terms = [ref[rows, :].astype(F32) for ref in refs[:-1]]
+        while len(terms) > 1:
+            terms = [left + right for left, right in zip(terms[::2], terms[1::2])]
+        refs[-1][rows, :] = terms[0].astype(BF)
 
 
 def total(pieces):
@@ -270,18 +287,19 @@
     second = jnp.where(odd, mine_ref[...], got_ref[...])
     for held, out, (take, give) in ((first, first_ref, FIRST), (second, second_ref, SECOND)):
         pick = chosen(chan_ref[0], take, give)
-        for a in range(3):
-            parts = []
-            for n in range(SLOTS):
-                at = n * GRAD_ROWS
-                if a < 2:
-                    parts.append(held[at : at + TALL, a * BLOCK : (a + 1) * BLOCK])
-                else:
-                    high = held[at + TALL : at + GRAD_ROWS, :BLOCK]
-                    low = held[at + TALL : at + GRAD_ROWS - PIECE, BLOCK:]
-                    parts.append(jnp.concatenate([high, low], axis=0))
-            wide = jnp.concatenate(parts, axis=1)
-            out[9 * a : 9 * (a + 1)] = across(wide, pick).reshape(9, PIECE, 256)
+        columns = []
+        for n in range(SLOTS):
+            at = n * GRAD_ROWS
+            parts = [
+                held[at + 48 * (j // 2) : at + 48 * (j // 2 + 1), BLOCK * (j % 2) : BLOCK * (j % 2 + 1)]
+                for j in range(8)
+            ]
+            parts += [held[at + 192 : at + 224, :BLOCK], held[at + 192 : at + 208, BLOCK:]]
+            columns.append(jnp.concatenate(parts, axis=0))
+        back = across(jnp.concatenate(columns, axis=1), pick).reshape(TAPS, PIECE, 256)
+        for j in range(9):
+            k = 9 * (j % 3) + 3 * (j // 3)
+            out[k : k + 3] = back[3 * j : 3 * j + 3]
 
 
 def finish(space, chan, mine, got):
@@ -365,7 +383,7 @@
     more = split_weight(chan, second_weight, *SECOND, PASSED)
     in_slots, pieces, more = tie((in_slots, pieces, more))
     in_slots += borders(space, in_slots, False)
-    fwd_first, bwd_first = arrange_weight(pieces, PLAIN)
+    fwd_first = arrange_weight(pieces, PLAIN)
     one = by_chan(more[1], FAR[2])
     in_slots, fwd_first = tie((in_slots, fwd_first))
     sums = over_chan(conv(space, fwd_first, in_slots), NEAR)
@@ -377,14 +395,18 @@
     hid_slots = gather(hidden, NEAR)
     hid_slots, two = tie((hid_slots, two))
     hid_slots += borders(space, hid_slots, True)
-    fwd_second, bwd_second = arrange_weight([more[0], one, two], ARRIVED)
-    pre_second = add(over_chan(conv(space, fwd_second, hid_slots), FAR))
+    fwd_second = arrange_weight([more[0], one, two], ARRIVED)
+    parts, fwd_second = tie((conv(space, fwd_second, hid_slots), fwd_second))
+    sums, bwd_second = tie((over_chan(parts, FAR), turn_weight(fwd_second)))
+    pre_second = add(sums)
     features = jax.nn.silu(pre_second).astype(BF)
     err_second = (cotangent.astype(F32) * slope(pre_second)).astype(BF)
 
+    err_second, fwd_first = tie((err_second, fwd_first))
     err2_slots = gather(err_second, FAR)
+    err2_slots, bwd_first = tie((err2_slots, turn_weight(fwd_first)))
     edge = borders(space, err2_slots, False)
-    grads = weight_grad(space, hid_slots, err2_slots, PASSED)
+    grads = weight_grad(space, hid_slots, err2_slots, PASSED, looped)
     edge, grads = tie((edge, grads))
     sums = over_chan(conv(space, bwd_second, err2_slots + edge), NEAR)
     one = by_chan(grads[1], FAR[2])
@@ -395,7 +417,7 @@
     err1_slots = gather(err_first, NEAR)
     two = by_chan(stitch(grads[2], one), FAR[3])
     err1_slots, two = tie((err1_slots, two))
-    firsts, err1_slots = tie((weight_grad(space, in_slots, err1_slots, PLAIN), err1_slots))
+    firsts, err1_slots = tie((weight_grad(space, in_slots, err1_slots, PLAIN, straight), err1_slots))
     firsts = over_chan(firsts, NEAR)
     edge = borders(space, err1_slots, True)
     firsts, edge = tie((firsts, edge))

time: 158 us -> 158 us (level)
  Pallas kernels: 15.4 us -> 20.4 us
  waiting for transfers between devices: 60.2 us -> 57.1 us
  starting transfers between devices: 79.1 us -> 77.1 us
    ppermute x34, waiting for transfers between devices: 57.6 us -> 52.5 us  [by_chan(): lax.ppermute(array, 'chan', [(i, i ^ mask) for i in range(16)])]
    pallas_call x21 -> x23, Pallas kernels: 15.4 us -> 20.4 us  [call(): pl.pallas_call(body, out_shape=outs, in_specs=[pl.BlockSpec(memory_space=...]
    ppermute x4, waiting for transfers between devices: 2.2 us -> 4.17 us  [borders(): return [lax.ppermute(off, ('space', 'chan'), pairs), by_space(core, 1)]]
    ppermute x34, starting transfers between devices: 47.1 us -> 45.2 us  [by_chan(): lax.ppermute(array, 'chan', [(i, i ^ mask) for i in range(16)])]
  transfers between devices with their start and end apart: 48 -> 48, of which waited for: 27 -> 25; matrix products, arithmetic and copies ran while one was open for 1% -> 1% of each run, Pallas kernels for 6% -> 10%
where the time goes in v2:
time: 158 us
  starting transfers between devices  77.1 us (49%)
  waiting for transfers between devices  57.1 us (36%)
  Pallas kernels  20.4 us (13%)
  other arithmetic  1.72 us (1%)
    ppermute x34, waiting for transfers between devices, by_chan(): lax.ppermute(array, 'chan', [(i, i ^ mask) for i in range(16)])  52.5 us
    ppermute x34, starting transfers between devices, by_chan(): lax.ppermute(array, 'chan', [(i, i ^ mask) for i in range(16)])  45.2 us
    pallas_call x23, Pallas kernels, call(): pl.pallas_call(body, out_shape=outs, in_specs=[pl.BlockSpec(memory_space=...  20.4 us
    ppermute x10, starting transfers between devices, by_space(): return lax.ppermute(array, 'space', [(i, i ^ mask) for i in range(16)])  16.4 us
    ppermute x4, starting transfers between devices, borders(): return [lax.ppermute(off, ('space', 'chan'), pairs), by_space(core, 1)]  15.6 us
    ppermute x4, waiting for transfers between devices, borders(): return [lax.ppermute(off, ('space', 'chan'), pairs), by_space(core, 1)]  4.17 us
  transfers between devices with their start and end apart: 48, of which 25 were waited for; matrix products, arithmetic and copies ran while one was open for 1% of the time, Pallas kernels for 10%

profile of v2, /device:TPU:1, one launch (start us, length us, event | category | flops | bytes accessed | tf_op | source)
XLA Modules:
  0.0 158.3 jit_solution(3666370211818544483)
XLA Ops:
  1.9 2.2 %collective-permute-start.3 = (bf16[224,128]{1,0:T(8,128)(2,1)S(1)}, bf16[224,128]{1,0:T(8,128)(2,1)S(1)}, u32[]{:S(2)}, u32[]{:S(2)}) collective-permute-start(bf16[224,128]{1,0:T(8,128)(2,1)S(1)} %get-tuple-element.139), channel_id=1, source_target_pairs={{0,1},{1,0},{2,3},{3,2},{4,5},{5,4},{6,7},{7,6},{8,9},{9,8},{10,11... | collective-permute-start | bytes 172040 | tf_op jit(solution)/shard_map/ppermute | solution.py:317
  4.2 6.0 %collective-permute-start.2 = (bf16[3,16,1024]{2,1,0:T(8,128)(2,1)}, bf16[3,16,1024]{2,1,0:T(8,128)(2,1)S(1)}, u32[]{:S(2)}, u32[]{:S(2)}) collective-permute-start(bf16[3,16,1024]{2,1,0:T(8,128)(2,1)} %bitcast.15), channel_id=1, source_target_pairs={{0,12},{1,13},{2,14},{3,15},{4,8},{5,9},{6,10},{7,11},{8,4},{9,5},... | collective-permute-start | bytes 294920 | tf_op jit(solution)/shard_map/ppermute | solution.py:317
  10.2 1.2 collective-permute-start.1
  14.0 5.8 %collective-permute-done.4.refs_2_ = bf16[224,128]{1,0:T(8,128)(2,1)S(1)} collective-permute-done((bf16[224,128]{1,0:T(8,128)(2,1)S(1)}, bf16[224,128]{1,0:T(8,128)(2,1)S(1)}, u32[]{:S(2)}, u32[]{:S(2)}) %collective-permute-start.4) | collective-permute-done | bytes 57376 | tf_op jit(solution)/shard_map/ppermute | solution.py:317
  19.9 2.9 %collective-permute-done.5.refs_3_ = bf16[224,128]{1,0:T(8,128)(2,1)S(1)} collective-permute-done((bf16[224,128]{1,0:T(8,128)(2,1)S(1)}, bf16[224,128]{1,0:T(8,128)(2,1)S(1)}, u32[]{:S(2)}, u32[]{:S(2)}) %collective-permute-start.5) | collective-permute-done | bytes 57376 | tf_op jit(solution)/shard_map/ppermute | solution.py:317
  22.8 2.6 %collective-permute-start.6 = (bf16[4,16,1024]{2,1,0:T(8,128)(2,1)S(1)}, bf16[4,16,1024]{2,1,0:T(8,128)(2,1)S(1)}, u32[]{:S(2)}, u32[]{:S(2)}) collective-permute-start(bf16[4,16,1024]{2,1,0:T(8,128)(2,1)S(1)} %get-tuple-element.150), channel_id=1, source_target_pairs={{0,1},{1,0},{2,3},{3,2},{4,5},{5,4},{6,7},{7,6},{8,9},{9,8},{10,11... | collective-permute-start | bytes 393224 | tf_op jit(solution)/shard_map/ppermute | solution.py:357
  26.9 1.5 collective-permute-done.6.refs_4_
  28.4 1.4 shard_map.79
  33.7 1.2 collective-permute-start.15
  35.0 3.0 %collective-permute-done.11 = bf16[3,16,1024]{2,1,0:T(8,128)(2,1)S(1)} collective-permute-done((bf16[3,16,1024]{2,1,0:T(8,128)(2,1)S(1)}, bf16[3,16,1024]{2,1,0:T(8,128)(2,1)S(1)}, u32[]{:S(2)}, u32[]{:S(2)}) %collective-permute-start.11) | collective-permute-done | bytes 98336 | tf_op jit(solution)/shard_map/ppermute | solution.py:317
  38.2 1.2 collective-permute-start.13
  39.5 1.4 collective-permute-start.12
  40.9 2.0 %collective-permute-done.14.s3.refs_3_ = bf16[3,16,1024]{2,1,0:T(8,128)(2,1)S(1)} collective-permute-done((bf16[3,16,1024]{2,1,0:T(8,128)(2,1)S(1)}, bf16[3,16,1024]{2,1,0:T(8,128)(2,1)S(1)}, u32[]{:S(2)}, u32[]{:S(2)}) %collective-permute-start.14) | collective-permute-done | bytes 98336 | tf_op jit(solution)/shard_map/ppermute | solution.py:317
  43.7 4.6 %collective-permute-start.16 = (bf16[4,16,1024]{2,1,0:T(8,128)(2,1)S(1)}, bf16[4,16,1024]{2,1,0:T(8,128)(2,1)S(1)}, u32[]{:S(2)}, u32[]{:S(2)}) collective-permute-start(bf16[4,16,1024]{2,1,0:T(8,128)(2,1)S(1)} %get-tuple-element.176), channel_id=1, source_target_pairs={{0,1},{1,0},{2,3},{3,2},{4,5},{5,4},{6,7},{7,6},{8,9},{9,8},{10,11... | collective-permute-start | bytes 393224 | tf_op jit(solution)/shard_map/ppermute | solution.py:357
  48.7 2.6 %collective-permute-done.16.refs_4_ = bf16[4,16,1024]{2,1,0:T(8,128)(2,1)S(1)} collective-permute-done((bf16[4,16,1024]{2,1,0:T(8,128)(2,1)S(1)}, bf16[4,16,1024]{2,1,0:T(8,128)(2,1)S(1)}, u32[]{:S(2)}, u32[]{:S(2)}) %collective-permute-start.16) | collective-permute-done | bytes 131104 | tf_op jit(solution)/shard_map/ppermute | solution.py:357
  51.3 1.4 shard_map.83
  52.7 2.0 %collective-permute-start.18 = (bf16[3,16,1024]{2,1,0:T(8,128)(2,1)S(1)}, bf16[3,16,1024]{2,1,0:T(8,128)(2,1)S(1)}, u32[]{:S(2)}, u32[]{:S(2)}) collective-permute-start(bf16[3,16,1024]{2,1,0:T(8,128)(2,1)S(1)} %get-tuple-element.183), channel_id=1, source_target_pairs={{0,8},{1,9},{2,10},{3,11},{4,12},{5,13},{6,14},{7,15},{8,0},{9,1},... | collective-permute-start | bytes 294920 | tf_op jit(solution)/shard_map/ppermute | solution.py:317
  54.6 1.2 collective-permute-start.19
  55.9 2.5 %collective-permute-start.20 = (bf16[3,16,1024]{2,1,0:T(8,128)(2,1)S(1)}, bf16[3,16,1024]{2,1,0:T(8,128)(2,1)S(1)}, u32[]{:S(2)}, u32[]{:S(2)}) collective-permute-start(bf16[3,16,1024]{2,1,0:T(8,128)(2,1)S(1)} %get-tuple-element.185), channel_id=1, source_target_pairs={{0,12},{1,13},{2,14},{3,15},{4,8},{5,9},{6,10},{7,11},{8,4},{9,5},... | collective-permute-start | bytes 294920 | tf_op jit(solution)/shard_map/ppermute | solution.py:317
  58.4 3.9 %shard_map.84.weight_ref = bf16[192,576]{1,0:T(8,128)(2,1)S(1)} custom-call(bf16[192,576]{1,0:T(8,128)(2,1)S(1)} %shard_map.81.weight_ref.fwd_ref), custom_call_target="tpu_custom_call" | custom-call | bytes 442368 | tf_op jit(solution)/shard_map/pallas_call | solution.py:31
  62.3 3.7 %collective-permute-done.19 = bf16[3,16,1024]{2,1,0:T(8,128)(2,1)S(1)} collective-permute-done((bf16[3,16,1024]{2,1,0:T(8,128)(2,1)S(1)}, bf16[3,16,1024]{2,1,0:T(8,128)(2,1)S(1)}, u32[]{:S(2)}, u32[]{:S(2)}) %collective-permute-start.19) | collective-permute-done | bytes 98336 | tf_op jit(solution)/shard_map/ppermute | solution.py:317
  66.8 2.6 %collective-permute-start.23 = (bf16[3,16,1024]{2,1,0:T(8,128)(2,1)S(1)}, bf16[3,16,1024]{2,1,0:T(8,128)(2,1)S(1)}, u32[]{:S(2)}, u32[]{:S(2)}) collective-permute-start(bf16[3,16,1024]{2,1,0:T(8,128)(2,1)S(1)} %get-tuple-element.194.s0.refs_6_.refs_0_), channel_id=1, source_target_pairs={{0,12},{1,13},{2,14},{3,15},{4,8},{5,9},{6,10},{7,11},{8,4},{9,5},... | collective-permute-start | bytes 294920 | tf_op jit(solution)/shard_map/ppermute | solution.py:317
  70.4 2.1 %collective-permute-start.21 = (bf16[3,16,1024]{2,1,0:T(8,128)(2,1)S(1)}, bf16[3,16,1024]{2,1,0:T(8,128)(2,1)S(1)}, u32[]{:S(2)}, u32[]{:S(2)}) collective-permute-start(bf16[3,16,1024]{2,1,0:T(8,128)(2,1)S(1)} %get-tuple-element.194.s0.refs_6_.refs_0_), channel_id=1, source_target_pairs={{0,8},{1,9},{2,10},{3,11},{4,12},{5,13},{6,14},{7,15},{8,0},{9,1},... | collective-permute-start | bytes 294920 | tf_op jit(solution)/shard_map/ppermute | solution.py:317
  72.5 3.9 %shard_map.85.weight_ref = bf16[192,576]{1,0:T(8,128)(2,1)S(1)} custom-call(bf16[192,576]{1,0:T(8,128)(2,1)S(1)} %shard_map.78.weight_ref.fwd_ref), custom_call_target="tpu_custom_call" | custom-call | bytes 442368 | tf_op jit(solution)/shard_map/pallas_call | solution.py:31
  76.5 3.0 %collective-permute-done.21.s1.refs_7_.refs_1_ = bf16[3,16,1024]{2,1,0:T(8,128)(2,1)S(1)} collective-permute-done((bf16[3,16,1024]{2,1,0:T(8,128)(2,1)S(1)}, bf16[3,16,1024]{2,1,0:T(8,128)(2,1)S(1)}, u32[]{:S(2)}, u32[]{:S(2)}) %collective-permute-start.21) | collective-permute-done | bytes 98336 | tf_op jit(solution)/shard_map/ppermute | solution.py:317
  79.5 3.3 %collective-permute-start.24 = (bf16[4,16,1024]{2,1,0:T(8,128)(2,1)S(1)}, bf16[4,16,1024]{2,1,0:T(8,128)(2,1)S(1)}, u32[]{:S(2)}, u32[]{:S(2)}) collective-permute-start(bf16[4,16,1024]{2,1,0:T(8,128)(2,1)S(1)} %get-tuple-element.198), channel_id=1, source_target_pairs={{0,1},{1,0},{2,3},{3,2},{4,5},{5,4},{6,7},{7,6},{8,9},{9,8},{10,11... | collective-permute-start | bytes 393224 | tf_op jit(solution)/shard_map/ppermute | solution.py:357
  83.1 2.6 %shard_map.87 = (bf16[224,128]{1,0:T(8,128)(2,1)S(1)}, bf16[448,128]{1,0:T(8,128)(2,1)S(1)}, bf16[224,128]{1,0:T(8,128)(2,1)S(1)}) custom-call(s32[1]{0:T(128)} %bitcast.space_ref, bf16[3,16,1024]{2,1,0:T(8,128)(2,1)S(1)} %multiply_convert_fusion.2.s0.refs_0_, bf16[3,16,1024]{2,1,0:T(8,128)(2,1)S(1)} %collective-permute-done.12.s1.refs_1_, ...), custom_call_target="tpu_custom_call" | custom-call | flops 679477248 | bytes 1277952 | tf_op jit(solution)/shard_map/pallas_call | solution.py:31
  85.8 2.9 %collective-permute-start.29 = (bf16[448,128]{1,0:T(8,128)(2,1)S(1)}, bf16[448,128]{1,0:T(8,128)(2,1)S(1)}, u32[]{:S(2)}, u32[]{:S(2)}) collective-permute-start(bf16[448,128]{1,0:T(8,128)(2,1)S(1)} %get-tuple-element.209), channel_id=1, source_target_pairs={{0,4},{1,5},{2,6},{3,7},{4,0},{5,1},{6,2},{7,3},{8,12},{9,13},{10,... | collective-permute-start | bytes 344072 | tf_op jit(solution)/shard_map/ppermute | solution.py:317
  88.7 1.4 shard_map.88
  90.1 1.3 collective-permute-start.26
  91.4 1.4 collective-permute-start.28
  92.8 1.1 collective-permute-done.26
  94.0 1.7 %collective-permute-done.27 = bf16[3,16,1024]{2,1,0:T(8,128)(2,1)S(1)} collective-permute-done((bf16[3,16,1024]{2,1,0:T(8,128)(2,1)S(1)}, bf16[3,16,1024]{2,1,0:T(8,128)(2,1)S(1)}, u32[]{:S(2)}, u32[]{:S(2)}) %collective-permute-start.27) | collective-permute-done | bytes 98336 | tf_op jit(solution)/shard_map/ppermute | solution.py:317
  95.6 2.5 %collective-permute-done.28 = bf16[3,16,1024]{2,1,0:T(8,128)(2,1)S(1)} collective-permute-done((bf16[3,16,1024]{2,1,0:T(8,128)(2,1)S(1)}, bf16[3,16,1024]{2,1,0:T(8,128)(2,1)S(1)}, u32[]{:S(2)}, u32[]{:S(2)}) %collective-permute-start.28) | collective-permute-done | bytes 98336 | tf_op jit(solution)/shard_map/ppermute | solution.py:317
  98.7 2.3 %collective-permute-start.32 = (bf16[3,16,1024]{2,1,0:T(8,128)(2,1)S(1)}, bf16[3,16,1024]{2,1,0:T(8,128)(2,1)S(1)}, u32[]{:S(2)}, u32[]{:S(2)}) collective-permute-start(bf16[3,16,1024]{2,1,0:T(8,128)(2,1)S(1)} %multiply_convert_fusion.refs_6_.s0.refs_0_), channel_id=1, source_target_pairs={{0,3},{1,2},{2,1},{3,0},{4,7},{5,6},{6,5},{7,4},{8,11},{9,10},{10,... | collective-permute-start | bytes 294920 | tf_op jit(solution)/shard_map/ppermute | solution.py:317
  101.6 2.4 %collective-permute-done.32.refs_9_.s3.refs_3_ = bf16[3,16,1024]{2,1,0:T(8,128)(2,1)S(1)} collective-permute-done((bf16[3,16,1024]{2,1,0:T(8,128)(2,1)S(1)}, bf16[3,16,1024]{2,1,0:T(8,128)(2,1)S(1)}, u32[]{:S(2)}, u32[]{:S(2)}) %collective-permute-start.32) | collective-permute-done | bytes 98336 | tf_op jit(solution)/shard_map/ppermute | solution.py:317
  104.0 1.7 %collective-permute-done.31.refs_8_.s2.refs_2_ = bf16[3,16,1024]{2,1,0:T(8,128)(2,1)S(1)} collective-permute-done((bf16[3,16,1024]{2,1,0:T(8,128)(2,1)S(1)}, bf16[3,16,1024]{2,1,0:T(8,128)(2,1)S(1)}, u32[]{:S(2)}, u32[]{:S(2)}) %collective-permute-start.31) | collective-permute-done | bytes 98336 | tf_op jit(solution)/shard_map/ppermute | solution.py:317
  105.7 1.4 shard_map.90
  107.2 5.0 %collective-permute-start.37 = (bf16[4,16,1024]{2,1,0:T(8,128)(2,1)S(1)}, bf16[4,16,1024]{2,1,0:T(8,128)(2,1)S(1)}, u32[]{:S(2)}, u32[]{:S(2)}) collective-permute-start(bf16[4,16,1024]{2,1,0:T(8,128)(2,1)S(1)} %get-tuple-element.232), channel_id=1, source_target_pairs={{0,1},{1,0},{2,3},{3,2},{4,5},{5,4},{6,7},{7,6},{8,9},{9,8},{10,11... | collective-permute-start | bytes 393224 | tf_op jit(solution)/shard_map/ppermute | solution.py:357
  116.4 1.9 %collective-permute-done.36.refs_3_ = bf16[224,128]{1,0:T(8,128)(2,1)S(1)} collective-permute-done((bf16[224,128]{1,0:T(8,128)(2,1)S(1)}, bf16[224,128]{1,0:T(8,128)(2,1)S(1)}, u32[]{:S(2)}, u32[]{:S(2)}) %collective-permute-start.36) | collective-permute-done | bytes 57376 | tf_op jit(solution)/shard_map/ppermute | solution.py:317
  118.5 2.1 %collective-permute-start.39 = (bf16[896,128]{1,0:T(8,128)(2,1)S(1)}, bf16[896,128]{1,0:T(8,128)(2,1)S(1)}, u32[]{:S(2)}, u32[]{:S(2)}) collective-permute-start(bf16[896,128]{1,0:T(8,128)(2,1)S(1)} %get-tuple-element.241), channel_id=1, source_target_pairs={{0,16},{16,0},{32,48},{48,32},{64,80},{80,64},{96,112},{112,96},{1... | collective-permute-start | bytes 688136 | tf_op jit(solution)/shard_map/ppermute | solution.py:321
  120.6 1.4 shard_map.93
  122.1 9.5 %collective-permute-start.40 = (bf16[896,128]{1,0:T(8,128)(2,1)S(1)}, bf16[896,128]{1,0:T(8,128)(2,1)S(1)}, u32[]{:S(2)}, u32[]{:S(2)}) collective-permute-start(bf16[896,128]{1,0:T(8,128)(2,1)S(1)} %shard_map.94.refs_0_), channel_id=1, source_target_pairs={{0,128},{16,144},{32,160},{48,176},{64,192},{80,208},{96,224},{112... | collective-permute-start | bytes 688136 | tf_op jit(solution)/shard_map/ppermute | solution.py:321
  131.6 7.6 %collective-permute-done.41 = bf16[3,16,1024]{2,1,0:T(8,128)(2,1)S(1)} collective-permute-done((bf16[3,16,1024]{2,1,0:T(8,128)(2,1)S(1)}, bf16[3,16,1024]{2,1,0:T(8,128)(2,1)S(1)}, u32[]{:S(2)}, u32[]{:S(2)}) %collective-permute-start.41) | collective-permute-done | bytes 98336 | tf_op jit(solution)/shard_map/ppermute | solution.py:317
  139.9 2.7 %collective-permute-start.42 = (bf16[896,128]{1,0:T(8,128)(2,1)S(1)}, bf16[896,128]{1,0:T(8,128)(2,1)S(1)}, u32[]{:S(2)}, u32[]{:S(2)}) collective-permute-start(bf16[896,128]{1,0:T(8,128)(2,1)S(1)} %shard_map.95.refs_0_), channel_id=1, source_target_pairs={{0,32},{16,48},{32,0},{48,16},{64,96},{80,112},{96,64},{112,80},{1... | collective-permute-start | bytes 688136 | tf_op jit(solution)/shard_map/ppermute | solution.py:321
  142.6 2.7 %collective-permute-start.45 = (bf16[3,16,1024]{2,1,0:T(8,128)(2,1)S(1)}, bf16[3,16,1024]{2,1,0:T(8,128)(2,1)S(1)}, u32[]{:S(2)}, u32[]{:S(2)}) collective-permute-start(bf16[3,16,1024]{2,1,0:T(8,128)(2,1)S(1)} %get-tuple-element.261), channel_id=1, source_target_pairs={{0,8},{1,9},{2,10},{3,11},{4,12},{5,13},{6,14},{7,15},{8,0},{9,1},... | collective-permute-start | bytes 294920 | tf_op jit(solution)/shard_map/ppermute | solution.py:317
  145.3 9.5 %collective-permute-done.45 = bf16[3,16,1024]{2,1,0:T(8,128)(2,1)S(1)} collective-permute-done((bf16[3,16,1024]{2,1,0:T(8,128)(2,1)S(1)}, bf16[3,16,1024]{2,1,0:T(8,128)(2,1)S(1)}, u32[]{:S(2)}, u32[]{:S(2)}) %collective-permute-start.45) | collective-permute-done | bytes 98336 | tf_op jit(solution)/shard_map/ppermute | solution.py:317
  156.9 1.4 shard_map.97
  (83 shorter events, 21.6 us)
Async XLA Ops:
  1.9 11.1 %collective-permute-start.3 = (bf16[224,128]{1,0:T(8,128)(2,1)S(1)}, bf16[224,128]{1,0:T(8,128)(2,1)S(1)}, u32[]{:S(2)}, u32[]{:S(2)}) collective-permute-start(bf16[224,128]{1,0:T(8,128)(2,1)S(1)} %get-tuple-element.139), channel_id=1, source_target_pairs={{0,1},{1,0},{2,3},{3,2},{4,5},{5,4},{6,7},{7,6},{8,9},{9,8},{10,11... | collective-permute-start | bytes 172040 | tf_op jit(solution)/shard_map/ppermute | solution.py:317
  4.2 18.6 %collective-permute-start.2 = (bf16[3,16,1024]{2,1,0:T(8,128)(2,1)}, bf16[3,16,1024]{2,1,0:T(8,128)(2,1)S(1)}, u32[]{:S(2)}, u32[]{:S(2)}) collective-permute-start(bf16[3,16,1024]{2,1,0:T(8,128)(2,1)} %bitcast.15), channel_id=1, source_target_pairs={{0,12},{1,13},{2,14},{3,15},{4,8},{5,9},{6,10},{7,11},{8,4},{9,5},... | collective-permute-start | bytes 294920 | tf_op jit(solution)/shard_map/ppermute | solution.py:317
  10.2 12.6 %collective-permute-start.1 = (bf16[3,16,1024]{2,1,0:T(8,128)(2,1)}, bf16[3,16,1024]{2,1,0:T(8,128)(2,1)S(1)}, u32[]{:S(2)}, u32[]{:S(2)}) collective-permute-start(bf16[3,16,1024]{2,1,0:T(8,128)(2,1)} %bitcast.16), channel_id=1, source_target_pairs={{0,4},{1,5},{2,6},{3,7},{4,0},{5,1},{6,2},{7,3},{8,12},{9,13},{10,... | collective-permute-start | bytes 294920 | tf_op jit(solution)/shard_map/ppermute | solution.py:317
  11.4 11.4 %collective-permute-start = (bf16[3,16,1024]{2,1,0:T(8,128)(2,1)}, bf16[3,16,1024]{2,1,0:T(8,128)(2,1)S(1)}, u32[]{:S(2)}, u32[]{:S(2)}) collective-permute-start(bf16[3,16,1024]{2,1,0:T(8,128)(2,1)} %bitcast.17), channel_id=1, source_target_pairs={{0,8},{1,9},{2,10},{3,11},{4,12},{5,13},{6,14},{7,15},{8,0},{9,1},... | collective-permute-start | bytes 294920 | tf_op jit(solution)/shard_map/ppermute | solution.py:317
  12.3 7.6 %collective-permute-start.4 = (bf16[224,128]{1,0:T(8,128)(2,1)S(1)}, bf16[224,128]{1,0:T(8,128)(2,1)S(1)}, u32[]{:S(2)}, u32[]{:S(2)}) collective-permute-start(bf16[224,128]{1,0:T(8,128)(2,1)S(1)} %get-tuple-element.140), channel_id=1, source_target_pairs={{0,2},{1,3},{2,0},{3,1},{4,6},{5,7},{6,4},{7,5},{8,10},{9,11},{10,... | collective-permute-start | bytes 172040 | tf_op jit(solution)/shard_map/ppermute | solution.py:317
  13.0 9.7 %collective-permute-start.5 = (bf16[224,128]{1,0:T(8,128)(2,1)S(1)}, bf16[224,128]{1,0:T(8,128)(2,1)S(1)}, u32[]{:S(2)}, u32[]{:S(2)}) collective-permute-start(bf16[224,128]{1,0:T(8,128)(2,1)S(1)} %get-tuple-element.141), channel_id=1, source_target_pairs={{0,3},{1,2},{2,1},{3,0},{4,7},{5,6},{6,5},{7,4},{8,11},{9,10},{10,... | collective-permute-start | bytes 172040 | tf_op jit(solution)/shard_map/ppermute | solution.py:317
  22.8 5.6 %collective-permute-start.6 = (bf16[4,16,1024]{2,1,0:T(8,128)(2,1)S(1)}, bf16[4,16,1024]{2,1,0:T(8,128)(2,1)S(1)}, u32[]{:S(2)}, u32[]{:S(2)}) collective-permute-start(bf16[4,16,1024]{2,1,0:T(8,128)(2,1)S(1)} %get-tuple-element.150), channel_id=1, source_target_pairs={{0,1},{1,0},{2,3},{3,2},{4,5},{5,4},{6,7},{7,6},{8,9},{9,8},{10,11... | collective-permute-start | bytes 393224 | tf_op jit(solution)/shard_map/ppermute | solution.py:357
  25.5 3.0 %collective-permute-start.7 = (bf16[4,16,1024]{2,1,0:T(8,128)(2,1)S(1)}, bf16[4,16,1024]{2,1,0:T(8,128)(2,1)S(1)}, u32[]{:S(2)}, u32[]{:S(2)}) collective-permute-start(bf16[4,16,1024]{2,1,0:T(8,128)(2,1)S(1)} %get-tuple-element.151), channel_id=1, source_target_pairs={{0,16},{16,0},{32,48},{48,32},{64,80},{80,64},{96,112},{112,96},{1... | collective-permute-start | bytes 393224 | tf_op jit(solution)/shard_map/ppermute | solution.py:321
  25.6 7.7 %collective-permute-start.9 = (bf16[448,128]{1,0:T(8,128)(2,1)S(1)}, bf16[448,128]{1,0:T(8,128)(2,1)S(1)}, u32[]{:S(2)}, u32[]{:S(2)}) collective-permute-start(bf16[448,128]{1,0:T(8,128)(2,1)S(1)} %get-tuple-element.164), channel_id=1, source_target_pairs={{0,4},{1,5},{2,6},{3,7},{4,0},{5,1},{6,2},{7,3},{8,12},{9,13},{10,... | collective-permute-start | bytes 344072 | tf_op jit(solution)/shard_map/ppermute | solution.py:317
  29.8 3.8 %collective-permute-start.8 = (bf16[3,16,1024]{2,1,0:T(8,128)(2,1)S(1)}, bf16[3,16,1024]{2,1,0:T(8,128)(2,1)S(1)}, u32[]{:S(2)}, u32[]{:S(2)}) collective-permute-start(bf16[3,16,1024]{2,1,0:T(8,128)(2,1)S(1)} %get-tuple-element.163), channel_id=1, source_target_pairs={{0,1},{1,0},{2,3},{3,2},{4,5},{5,4},{6,7},{7,6},{8,9},{9,8},{10,11... | collective-permute-start | bytes 294920 | tf_op jit(solution)/shard_map/ppermute | solution.py:317
  30.9 4.2 %collective-permute-start.10 = (bf16[3,16,1024]{2,1,0:T(8,128)(2,1)S(1)}, bf16[3,16,1024]{2,1,0:T(8,128)(2,1)S(1)}, u32[]{:S(2)}, u32[]{:S(2)}) collective-permute-start(bf16[3,16,1024]{2,1,0:T(8,128)(2,1)S(1)} %get-tuple-element.168), channel_id=1, source_target_pairs={{0,2},{1,3},{2,0},{3,1},{4,6},{5,7},{6,4},{7,5},{8,10},{9,11},{10,... | collective-permute-start | bytes 294920 | tf_op jit(solution)/shard_map/ppermute | solution.py:317
  31.9 6.1 %collective-permute-start.11 = (bf16[3,16,1024]{2,1,0:T(8,128)(2,1)S(1)}, bf16[3,16,1024]{2,1,0:T(8,128)(2,1)S(1)}, u32[]{:S(2)}, u32[]{:S(2)}) collective-permute-start(bf16[3,16,1024]{2,1,0:T(8,128)(2,1)S(1)} %get-tuple-element.169), channel_id=1, source_target_pairs={{0,3},{1,2},{2,1},{3,0},{4,7},{5,6},{6,5},{7,4},{8,11},{9,10},{10,... | collective-permute-start | bytes 294920 | tf_op jit(solution)/shard_map/ppermute | solution.py:317
  33.7 10.0 %collective-permute-start.15 = (bf16[448,128]{1,0:T(8,128)(2,1)S(1)}, bf16[448,128]{1,0:T(8,128)(2,1)S(1)}, u32[]{:S(2)}, u32[]{:S(2)}) collective-permute-start(bf16[448,128]{1,0:T(8,128)(2,1)S(1)} %shard_map.80), channel_id=1, source_target_pairs={{0,12},{1,13},{2,14},{3,15},{4,8},{5,9},{6,10},{7,11},{8,4},{9,5},... | collective-permute-start | bytes 344072 | tf_op jit(solution)/shard_map/ppermute | solution.py:317
  38.1 4.7 %collective-permute-start.14 = (bf16[3,16,1024]{2,1,0:T(8,128)(2,1)S(1)}, bf16[3,16,1024]{2,1,0:T(8,128)(2,1)S(1)}, u32[]{:S(2)}, u32[]{:S(2)}) collective-permute-start(bf16[3,16,1024]{2,1,0:T(8,128)(2,1)S(1)} %multiply_convert_fusion.2.s0.refs_0_), channel_id=1, source_target_pairs={{0,3},{1,2},{2,1},{3,0},{4,7},{5,6},{6,5},{7,4},{8,11},{9,10},{10,... | collective-permute-start | bytes 294920 | tf_op jit(solution)/shard_map/ppermute | solution.py:317
  38.2 4.7 %collective-permute-start.13 = (bf16[3,16,1024]{2,1,0:T(8,128)(2,1)S(1)}, bf16[3,16,1024]{2,1,0:T(8,128)(2,1)S(1)}, u32[]{:S(2)}, u32[]{:S(2)}) collective-permute-start(bf16[3,16,1024]{2,1,0:T(8,128)(2,1)S(1)} %multiply_convert_fusion.2.s0.refs_0_), channel_id=1, source_target_pairs={{0,2},{1,3},{2,0},{3,1},{4,6},{5,7},{6,4},{7,5},{8,10},{9,11},{10,... | collective-permute-start | bytes 294920 | tf_op jit(solution)/shard_map/ppermute | solution.py:317
  39.5 4.2 %collective-permute-start.12 = (bf16[3,16,1024]{2,1,0:T(8,128)(2,1)S(1)}, bf16[3,16,1024]{2,1,0:T(8,128)(2,1)S(1)}, u32[]{:S(2)}, u32[]{:S(2)}) collective-permute-start(bf16[3,16,1024]{2,1,0:T(8,128)(2,1)S(1)} %multiply_convert_fusion.2.s0.refs_0_), channel_id=1, source_target_pairs={{0,1},{1,0},{2,3},{3,2},{4,5},{5,4},{6,7},{7,6},{8,9},{9,8},{10,11... | collective-permute-start | bytes 294920 | tf_op jit(solution)/shard_map/ppermute | solution.py:317
  43.7 7.6 %collective-permute-start.16 = (bf16[4,16,1024]{2,1,0:T(8,128)(2,1)S(1)}, bf16[4,16,1024]{2,1,0:T(8,128)(2,1)S(1)}, u32[]{:S(2)}, u32[]{:S(2)}) collective-permute-start(bf16[4,16,1024]{2,1,0:T(8,128)(2,1)S(1)} %get-tuple-element.176), channel_id=1, source_target_pairs={{0,1},{1,0},{2,3},{3,2},{4,5},{5,4},{6,7},{7,6},{8,9},{9,8},{10,11... | collective-permute-start | bytes 393224 | tf_op jit(solution)/shard_map/ppermute | solution.py:357
  48.3 3.0 %collective-permute-start.17 = (bf16[4,16,1024]{2,1,0:T(8,128)(2,1)S(1)}, bf16[4,16,1024]{2,1,0:T(8,128)(2,1)S(1)}, u32[]{:S(2)}, u32[]{:S(2)}) collective-permute-start(bf16[4,16,1024]{2,1,0:T(8,128)(2,1)S(1)} %get-tuple-element.177), channel_id=1, source_target_pairs={{0,16},{16,0},{32,48},{48,32},{64,80},{80,64},{96,112},{112,96},{1... | collective-permute-start | bytes 393224 | tf_op jit(solution)/shard_map/ppermute | solution.py:321
  52.7 9.7 %collective-permute-start.18 = (bf16[3,16,1024]{2,1,0:T(8,128)(2,1)S(1)}, bf16[3,16,1024]{2,1,0:T(8,128)(2,1)S(1)}, u32[]{:S(2)}, u32[]{:S(2)}) collective-permute-start(bf16[3,16,1024]{2,1,0:T(8,128)(2,1)S(1)} %get-tuple-element.183), channel_id=1, source_target_pairs={{0,8},{1,9},{2,10},{3,11},{4,12},{5,13},{6,14},{7,15},{8,0},{9,1},... | collective-permute-start | bytes 294920 | tf_op jit(solution)/shard_map/ppermute | solution.py:317
  54.6 11.4 %collective-permute-start.19 = (bf16[3,16,1024]{2,1,0:T(8,128)(2,1)S(1)}, bf16[3,16,1024]{2,1,0:T(8,128)(2,1)S(1)}, u32[]{:S(2)}, u32[]{:S(2)}) collective-permute-start(bf16[3,16,1024]{2,1,0:T(8,128)(2,1)S(1)} %get-tuple-element.184), channel_id=1, source_target_pairs={{0,4},{1,5},{2,6},{3,7},{4,0},{5,1},{6,2},{7,3},{8,12},{9,13},{10,... | collective-permute-start | bytes 294920 | tf_op jit(solution)/shard_map/ppermute | solution.py:317
  55.9 10.1 %collective-permute-start.20 = (bf16[3,16,1024]{2,1,0:T(8,128)(2,1)S(1)}, bf16[3,16,1024]{2,1,0:T(8,128)(2,1)S(1)}, u32[]{:S(2)}, u32[]{:S(2)}) collective-permute-start(bf16[3,16,1024]{2,1,0:T(8,128)(2,1)S(1)} %get-tuple-element.185), channel_id=1, source_target_pairs={{0,12},{1,13},{2,14},{3,15},{4,8},{5,9},{6,10},{7,11},{8,4},{9,5},... | collective-permute-start | bytes 294920 | tf_op jit(solution)/shard_map/ppermute | solution.py:317
  66.8 9.6 %collective-permute-start.23 = (bf16[3,16,1024]{2,1,0:T(8,128)(2,1)S(1)}, bf16[3,16,1024]{2,1,0:T(8,128)(2,1)S(1)}, u32[]{:S(2)}, u32[]{:S(2)}) collective-permute-start(bf16[3,16,1024]{2,1,0:T(8,128)(2,1)S(1)} %get-tuple-element.194.s0.refs_6_.refs_0_), channel_id=1, source_target_pairs={{0,12},{1,13},{2,14},{3,15},{4,8},{5,9},{6,10},{7,11},{8,4},{9,5},... | collective-permute-start | bytes 294920 | tf_op jit(solution)/shard_map/ppermute | solution.py:317
  69.4 7.0 %collective-permute-start.22 = (bf16[3,16,1024]{2,1,0:T(8,128)(2,1)S(1)}, bf16[3,16,1024]{2,1,0:T(8,128)(2,1)S(1)}, u32[]{:S(2)}, u32[]{:S(2)}) collective-permute-start(bf16[3,16,1024]{2,1,0:T(8,128)(2,1)S(1)} %get-tuple-element.194.s0.refs_6_.refs_0_), channel_id=1, source_target_pairs={{0,4},{1,5},{2,6},{3,7},{4,0},{5,1},{6,2},{7,3},{8,12},{9,13},{10,... | collective-permute-start | bytes 294920 | tf_op jit(solution)/shard_map/ppermute | solution.py:317
  70.4 9.1 %collective-permute-start.21 = (bf16[3,16,1024]{2,1,0:T(8,128)(2,1)S(1)}, bf16[3,16,1024]{2,1,0:T(8,128)(2,1)S(1)}, u32[]{:S(2)}, u32[]{:S(2)}) collective-permute-start(bf16[3,16,1024]{2,1,0:T(8,128)(2,1)S(1)} %get-tuple-element.194.s0.refs_6_.refs_0_), channel_id=1, source_target_pairs={{0,8},{1,9},{2,10},{3,11},{4,12},{5,13},{6,14},{7,15},{8,0},{9,1},... | collective-permute-start | bytes 294920 | tf_op jit(solution)/shard_map/ppermute | solution.py:317
  79.5 6.2 %collective-permute-start.24 = (bf16[4,16,1024]{2,1,0:T(8,128)(2,1)S(1)}, bf16[4,16,1024]{2,1,0:T(8,128)(2,1)S(1)}, u32[]{:S(2)}, u32[]{:S(2)}) collective-permute-start(bf16[4,16,1024]{2,1,0:T(8,128)(2,1)S(1)} %get-tuple-element.198), channel_id=1, source_target_pairs={{0,1},{1,0},{2,3},{3,2},{4,5},{5,4},{6,7},{7,6},{8,9},{9,8},{10,11... | collective-permute-start | bytes 393224 | tf_op jit(solution)/shard_map/ppermute | solution.py:357
  82.8 3.0 %collective-permute-start.25 = (bf16[4,16,1024]{2,1,0:T(8,128)(2,1)S(1)}, bf16[4,16,1024]{2,1,0:T(8,128)(2,1)S(1)}, u32[]{:S(2)}, u32[]{:S(2)}) collective-permute-start(bf16[4,16,1024]{2,1,0:T(8,128)(2,1)S(1)} %get-tuple-element.199), channel_id=1, source_target_pairs={{0,16},{16,0},{32,48},{48,32},{64,80},{80,64},{96,112},{112,96},{1... | collective-permute-start | bytes 393224 | tf_op jit(solution)/shard_map/ppermute | solution.py:321
  85.8 12.4 %collective-permute-start.29 = (bf16[448,128]{1,0:T(8,128)(2,1)S(1)}, bf16[448,128]{1,0:T(8,128)(2,1)S(1)}, u32[]{:S(2)}, u32[]{:S(2)}) collective-permute-start(bf16[448,128]{1,0:T(8,128)(2,1)S(1)} %get-tuple-element.209), channel_id=1, source_target_pairs={{0,4},{1,5},{2,6},{3,7},{4,0},{5,1},{6,2},{7,3},{8,12},{9,13},{10,... | collective-permute-start | bytes 344072 | tf_op jit(solution)/shard_map/ppermute | solution.py:317
  90.1 3.9 %collective-permute-start.26 = (bf16[3,16,1024]{2,1,0:T(8,128)(2,1)S(1)}, bf16[3,16,1024]{2,1,0:T(8,128)(2,1)S(1)}, u32[]{:S(2)}, u32[]{:S(2)}) collective-permute-start(bf16[3,16,1024]{2,1,0:T(8,128)(2,1)S(1)} %get-tuple-element.206), channel_id=1, source_target_pairs={{0,1},{1,0},{2,3},{3,2},{4,5},{5,4},{6,7},{7,6},{8,9},{9,8},{10,11... | collective-permute-start | bytes 294920 | tf_op jit(solution)/shard_map/ppermute | solution.py:317
  91.4 4.2 %collective-permute-start.27 = (bf16[3,16,1024]{2,1,0:T(8,128)(2,1)S(1)}, bf16[3,16,1024]{2,1,0:T(8,128)(2,1)S(1)}, u32[]{:S(2)}, u32[]{:S(2)}) collective-permute-start(bf16[3,16,1024]{2,1,0:T(8,128)(2,1)S(1)} %get-tuple-element.207), channel_id=1, source_target_pairs={{0,2},{1,3},{2,0},{3,1},{4,6},{5,7},{6,4},{7,5},{8,10},{9,11},{10,... | collective-permute-start | bytes 294920 | tf_op jit(solution)/shard_map/ppermute | solution.py:317
  91.4 6.7 %collective-permute-start.28 = (bf16[3,16,1024]{2,1,0:T(8,128)(2,1)S(1)}, bf16[3,16,1024]{2,1,0:T(8,128)(2,1)S(1)}, u32[]{:S(2)}, u32[]{:S(2)}) collective-permute-start(bf16[3,16,1024]{2,1,0:T(8,128)(2,1)S(1)} %get-tuple-element.208), channel_id=1, source_target_pairs={{0,3},{1,2},{2,1},{3,0},{4,7},{5,6},{6,5},{7,4},{8,11},{9,10},{10,... | collective-permute-start | bytes 294920 | tf_op jit(solution)/shard_map/ppermute | solution.py:317
  98.1 7.6 %collective-permute-start.33 = (bf16[448,128]{1,0:T(8,128)(2,1)S(1)}, bf16[448,128]{1,0:T(8,128)(2,1)S(1)}, u32[]{:S(2)}, u32[]{:S(2)}) collective-permute-start(bf16[448,128]{1,0:T(8,128)(2,1)S(1)} %shard_map.89), channel_id=1, source_target_pairs={{0,12},{1,13},{2,14},{3,15},{4,8},{5,9},{6,10},{7,11},{8,4},{9,5},... | collective-permute-start | bytes 344072 | tf_op jit(solution)/shard_map/ppermute | solution.py:317
  98.7 5.3 %collective-permute-start.32 = (bf16[3,16,1024]{2,1,0:T(8,128)(2,1)S(1)}, bf16[3,16,1024]{2,1,0:T(8,128)(2,1)S(1)}, u32[]{:S(2)}, u32[]{:S(2)}) collective-permute-start(bf16[3,16,1024]{2,1,0:T(8,128)(2,1)S(1)} %multiply_convert_fusion.refs_6_.s0.refs_0_), channel_id=1, source_target_pairs={{0,3},{1,2},{2,1},{3,0},{4,7},{5,6},{6,5},{7,4},{8,11},{9,10},{10,... | collective-permute-start | bytes 294920 | tf_op jit(solution)/shard_map/ppermute | solution.py:317
  101.0 4.8 %collective-permute-start.31 = (bf16[3,16,1024]{2,1,0:T(8,128)(2,1)S(1)}, bf16[3,16,1024]{2,1,0:T(8,128)(2,1)S(1)}, u32[]{:S(2)}, u32[]{:S(2)}) collective-permute-start(bf16[3,16,1024]{2,1,0:T(8,128)(2,1)S(1)} %multiply_convert_fusion.refs_6_.s0.refs_0_), channel_id=1, source_target_pairs={{0,2},{1,3},{2,0},{3,1},{4,6},{5,7},{6,4},{7,5},{8,10},{9,11},{10,... | collective-permute-start | bytes 294920 | tf_op jit(solution)/shard_map/ppermute | solution.py:317
  101.0 4.8 %collective-permute-start.30 = (bf16[3,16,1024]{2,1,0:T(8,128)(2,1)S(1)}, bf16[3,16,1024]{2,1,0:T(8,128)(2,1)S(1)}, u32[]{:S(2)}, u32[]{:S(2)}) collective-permute-start(bf16[3,16,1024]{2,1,0:T(8,128)(2,1)S(1)} %multiply_convert_fusion.refs_6_.s0.refs_0_), channel_id=1, source_target_pairs={{0,1},{1,0},{2,3},{3,2},{4,5},{5,4},{6,7},{7,6},{8,9},{9,8},{10,11... | collective-permute-start | bytes 294920 | tf_op jit(solution)/shard_map/ppermute | solution.py:317
  107.2 11.1 %collective-permute-start.37 = (bf16[4,16,1024]{2,1,0:T(8,128)(2,1)S(1)}, bf16[4,16,1024]{2,1,0:T(8,128)(2,1)S(1)}, u32[]{:S(2)}, u32[]{:S(2)}) collective-permute-start(bf16[4,16,1024]{2,1,0:T(8,128)(2,1)S(1)} %get-tuple-element.232), channel_id=1, source_target_pairs={{0,1},{1,0},{2,3},{3,2},{4,5},{5,4},{6,7},{7,6},{8,9},{9,8},{10,11... | collective-permute-start | bytes 393224 | tf_op jit(solution)/shard_map/ppermute | solution.py:357
  112.2 6.1 %collective-permute-start.38 = (bf16[4,16,1024]{2,1,0:T(8,128)(2,1)S(1)}, bf16[4,16,1024]{2,1,0:T(8,128)(2,1)S(1)}, u32[]{:S(2)}, u32[]{:S(2)}) collective-permute-start(bf16[4,16,1024]{2,1,0:T(8,128)(2,1)S(1)} %get-tuple-element.233), channel_id=1, source_target_pairs={{0,16},{16,0},{32,48},{48,32},{64,80},{80,64},{96,112},{112,96},{1... | collective-permute-start | bytes 393224 | tf_op jit(solution)/shard_map/ppermute | solution.py:321
  112.3 3.2 %collective-permute-start.34 = (bf16[224,128]{1,0:T(8,128)(2,1)S(1)}, bf16[224,128]{1,0:T(8,128)(2,1)S(1)}, u32[]{:S(2)}, u32[]{:S(2)}) collective-permute-start(bf16[224,128]{1,0:T(8,128)(2,1)S(1)} %get-tuple-element.225), channel_id=1, source_target_pairs={{0,1},{1,0},{2,3},{3,2},{4,5},{5,4},{6,7},{7,6},{8,9},{9,8},{10,11... | collective-permute-start | bytes 172040 | tf_op jit(solution)/shard_map/ppermute | solution.py:317
  113.1 3.3 %collective-permute-start.35 = (bf16[224,128]{1,0:T(8,128)(2,1)S(1)}, bf16[224,128]{1,0:T(8,128)(2,1)S(1)}, u32[]{:S(2)}, u32[]{:S(2)}) collective-permute-start(bf16[224,128]{1,0:T(8,128)(2,1)S(1)} %get-tuple-element.226), channel_id=1, source_target_pairs={{0,2},{1,3},{2,0},{3,1},{4,6},{5,7},{6,4},{7,5},{8,10},{9,11},{10,... | collective-permute-start | bytes 172040 | tf_op jit(solution)/shard_map/ppermute | solution.py:317
  114.2 4.1 %collective-permute-start.36 = (bf16[224,128]{1,0:T(8,128)(2,1)S(1)}, bf16[224,128]{1,0:T(8,128)(2,1)S(1)}, u32[]{:S(2)}, u32[]{:S(2)}) collective-permute-start(bf16[224,128]{1,0:T(8,128)(2,1)S(1)} %get-tuple-element.227), channel_id=1, source_target_pairs={{0,3},{1,2},{2,1},{3,0},{4,7},{5,6},{6,5},{7,4},{8,11},{9,10},{10,... | collective-permute-start | bytes 172040 | tf_op jit(solution)/shard_map/ppermute | solution.py:317
  118.5 3.5 %collective-permute-start.39 = (bf16[896,128]{1,0:T(8,128)(2,1)S(1)}, bf16[896,128]{1,0:T(8,128)(2,1)S(1)}, u32[]{:S(2)}, u32[]{:S(2)}) collective-permute-start(bf16[896,128]{1,0:T(8,128)(2,1)S(1)} %get-tuple-element.241), channel_id=1, source_target_pairs={{0,16},{16,0},{32,48},{48,32},{64,80},{80,64},{96,112},{112,96},{1... | collective-permute-start | bytes 688136 | tf_op jit(solution)/shard_map/ppermute | solution.py:321
  122.1 17.0 %collective-permute-start.40 = (bf16[896,128]{1,0:T(8,128)(2,1)S(1)}, bf16[896,128]{1,0:T(8,128)(2,1)S(1)}, u32[]{:S(2)}, u32[]{:S(2)}) collective-permute-start(bf16[896,128]{1,0:T(8,128)(2,1)S(1)} %shard_map.94.refs_0_), channel_id=1, source_target_pairs={{0,128},{16,144},{32,160},{48,176},{64,192},{80,208},{96,224},{112... | collective-permute-start | bytes 688136 | tf_op jit(solution)/shard_map/ppermute | solution.py:321
  131.6 7.6 %collective-permute-start.41 = (bf16[3,16,1024]{2,1,0:T(8,128)(2,1)S(1)}, bf16[3,16,1024]{2,1,0:T(8,128)(2,1)S(1)}, u32[]{:S(2)}, u32[]{:S(2)}) collective-permute-start(bf16[3,16,1024]{2,1,0:T(8,128)(2,1)S(1)} %get-tuple-element.255), channel_id=1, source_target_pairs={{0,4},{1,5},{2,6},{3,7},{4,0},{5,1},{6,2},{7,3},{8,12},{9,13},{10,... | collective-permute-start | bytes 294920 | tf_op jit(solution)/shard_map/ppermute | solution.py:317
  139.3 15.5 %collective-permute-start.44 = (bf16[896,128]{1,0:T(8,128)(2,1)S(1)}, bf16[896,128]{1,0:T(8,128)(2,1)S(1)}, u32[]{:S(2)}, u32[]{:S(2)}) collective-permute-start(bf16[896,128]{1,0:T(8,128)(2,1)S(1)} %shard_map.95.refs_0_), channel_id=1, source_target_pairs={{0,96},{16,112},{32,64},{48,80},{64,32},{80,48},{96,0},{112,16},{1... | collective-permute-start | bytes 688136 | tf_op jit(solution)/shard_map/ppermute | solution.py:321
  139.4 15.5 %collective-permute-start.43 = (bf16[896,128]{1,0:T(8,128)(2,1)S(1)}, bf16[896,128]{1,0:T(8,128)(2,1)S(1)}, u32[]{:S(2)}, u32[]{:S(2)}) collective-permute-start(bf16[896,128]{1,0:T(8,128)(2,1)S(1)} %shard_map.95.refs_0_), channel_id=1, source_target_pairs={{0,64},{16,80},{32,96},{48,112},{64,0},{80,16},{96,32},{112,48},{1... | collective-permute-start | bytes 688136 | tf_op jit(solution)/shard_map/ppermute | solution.py:321
  139.9 14.9 %collective-permute-start.42 = (bf16[896,128]{1,0:T(8,128)(2,1)S(1)}, bf16[896,128]{1,0:T(8,128)(2,1)S(1)}, u32[]{:S(2)}, u32[]{:S(2)}) collective-permute-start(bf16[896,128]{1,0:T(8,128)(2,1)S(1)} %shard_map.95.refs_0_), channel_id=1, source_target_pairs={{0,32},{16,48},{32,0},{48,16},{64,96},{80,112},{96,64},{112,80},{1... | collective-permute-start | bytes 688136 | tf_op jit(solution)/shard_map/ppermute | solution.py:321
  142.6 12.2 %collective-permute-start.45 = (bf16[3,16,1024]{2,1,0:T(8,128)(2,1)S(1)}, bf16[3,16,1024]{2,1,0:T(8,128)(2,1)S(1)}, u32[]{:S(2)}, u32[]{:S(2)}) collective-permute-start(bf16[3,16,1024]{2,1,0:T(8,128)(2,1)S(1)} %get-tuple-element.261), channel_id=1, source_target_pairs={{0,8},{1,9},{2,10},{3,11},{4,12},{5,13},{6,14},{7,15},{8,0},{9,1},... | collective-permute-start | bytes 294920 | tf_op jit(solution)/shard_map/ppermute | solution.py:317
  145.3 9.5 %collective-permute-start.46 = (bf16[3,16,1024]{2,1,0:T(8,128)(2,1)S(1)}, bf16[3,16,1024]{2,1,0:T(8,128)(2,1)S(1)}, u32[]{:S(2)}, u32[]{:S(2)}) collective-permute-start(bf16[3,16,1024]{2,1,0:T(8,128)(2,1)S(1)} %get-tuple-element.262), channel_id=1, source_target_pairs={{0,12},{1,13},{2,14},{3,15},{4,8},{5,9},{6,10},{7,11},{8,4},{9,5},... | collective-permute-start | bytes 294920 | tf_op jit(solution)/shard_map/ppermute | solution.py:317
  155.0 1.9 %collective-permute-start.47 = (bf16[896,128]{1,0:T(8,128)(2,1)S(1)}, bf16[896,128]{1,0:T(8,128)(2,1)S(1)}, u32[]{:S(2)}, u32[]{:S(2)}) collective-permute-start(bf16[896,128]{1,0:T(8,128)(2,1)S(1)} %shard_map.96.mine_ref), channel_id=1, source_target_pairs={{0,16},{16,0},{32,48},{48,32},{64,80},{80,64},{96,112},{112,96},{1... | collective-permute-start | bytes 688136 | tf_op jit(solution)/shard_map/ppermute | solution.py:321
  (4 other events, 35.5 us)

commit v3 on v2

--- a/solution.py
+++ b/solution.py
@@ -92,6 +92,7 @@
 
 
 def arrange_body(spots, *refs):
+    fwd_ref, bwd_ref, held = refs[-3:]
     for a in range(3):
         for b in range(3):
             for c in range(3):
@@ -101,30 +102,28 @@
                     [refs[j][at + row : at + row + PIECE, lane : lane + BLOCK] for j, at in spots], axis=0
                 )
                 at = COLS * b + BLOCK * a
-                refs[-1][BLOCK * c : BLOCK * (c + 1), at : at + BLOCK] = block
+                fwd_ref[BLOCK * c : BLOCK * (c + 1), at : at + BLOCK] = block
+                held[BLOCK * k : BLOCK * (k + 1), :] = block
+    for a in range(3):
+        for b in range(3):
+
+            @pl.loop(0, 3)
+            def _(c):
+                block = held[pl.ds(pl.multiple_of(BLOCK * (9 * a + 3 * b + c), BLOCK), BLOCK), :]
+                at = COLS * (2 - b) + BLOCK * (2 - a)
+                rows = pl.ds(pl.multiple_of(BLOCK * (2 - c), BLOCK), BLOCK)
+                bwd_ref[rows, at : at + BLOCK] = block.astype(F32).T.astype(BF)
 
 
 def arrange_weight(pieces, spots):
     return call(
-        functools.partial(arrange_body, spots), [shape((COLS, ROWS))], [], [], pieces, 0
-    )[0]
-
-
-def turn_body(fwd_ref, bwd_ref):
-    for a in range(3):
-        for b in range(3):
-
-            @pl.loop(0, 3)
-            def _(c):
-                here = pl.ds(pl.multiple_of(BLOCK * c, BLOCK), BLOCK)
-                there = pl.ds(pl.multiple_of(BLOCK * (2 - c), BLOCK), BLOCK)
-                at, to = COLS * b + BLOCK * a, COLS * (2 - b) + BLOCK * (2 - a)
-                block = fwd_ref[here, at : at + BLOCK].astype(F32)
-                bwd_ref[there, to : to + BLOCK] = block.T.astype(BF)
-
-
-def turn_weight(weight):
-    return call(turn_body, [shape((COLS, ROWS))], [], [], [weight], 0)[0]
+        functools.partial(arrange_body, spots),
+        [shape((COLS, ROWS))] * 2,
+        [pltpu.VMEM((TAPS * BLOCK, BLOCK), BF)],
+        [],
+        pieces,
+        0,
+    )
 
 
 def edges():
@@ -383,7 +382,7 @@
     more = split_weight(chan, second_weight, *SECOND, PASSED)
     in_slots, pieces, more = tie((in_slots, pieces, more))
     in_slots += borders(space, in_slots, False)
-    fwd_first = arrange_weight(pieces, PLAIN)
+    fwd_first, bwd_first = arrange_weight(pieces, PLAIN)
     one = by_chan(more[1], FAR[2])
     in_slots, fwd_first = tie((in_slots, fwd_first))
     sums = over_chan(conv(space, fwd_first, in_slots), NEAR)
@@ -395,16 +394,12 @@
     hid_slots = gather(hidden, NEAR)
     hid_slots, two = tie((hid_slots, two))
     hid_slots += borders(space, hid_slots, True)
-    fwd_second = arrange_weight([more[0], one, two], ARRIVED)
-    parts, fwd_second = tie((conv(space, fwd_second, hid_slots), fwd_second))
-    sums, bwd_second = tie((over_chan(parts, FAR), turn_weight(fwd_second)))
-    pre_second = add(sums)
+    fwd_second, bwd_second = arrange_weight([more[0], one, two], ARRIVED)
+    pre_second = add(over_chan(conv(space, fwd_second, hid_slots), FAR))
     features = jax.nn.silu(pre_second).astype(BF)
     err_second = (cotangent.astype(F32) * slope(pre_second)).astype(BF)
 
-    err_second, fwd_first = tie((err_second, fwd_first))
     err2_slots = gather(err_second, FAR)
-    err2_slots, bwd_first = tie((err2_slots, turn_weight(fwd_first)))
     edge = borders(space, err2_slots, False)
     grads = weight_grad(space, hid_slots, err2_slots, PASSED, looped)
     edge, grads = tie((edge, grads))

time: 158 us -> 158 us (level)
  waiting for transfers between devices: 57.1 us -> 62.9 us
  starting transfers between devices: 77.1 us -> 72.3 us
    ppermute x34, waiting for transfers between devices: 52.5 us -> 61.7 us  [by_chan(): lax.ppermute(array, 'chan', [(i, i ^ mask) for i in range(16)])]
    ppermute x4, waiting for transfers between devices: 4.17 us -> 0.71 us  [borders(): return [lax.ppermute(off, ('space', 'chan'), pairs), by_space(core, 1)]]
    ppermute x10, starting transfers between devices: 16.4 us -> 13.4 us  [by_space(): return lax.ppermute(array, 'space', [(i, i ^ mask) for i in range(16)])]
    pallas_call x23 -> x21, Pallas kernels: 20.4 us -> 18.9 us  [call(): pl.pallas_call(body, out_shape=outs, in_specs=[pl.BlockSpec(memory_space=...]
  transfers between devices with their start and end apart: 48 -> 48, of which waited for: 25 -> 23; matrix products, arithmetic and copies ran while one was open for 1% -> 1% of each run, Pallas kernels for 10% -> 9%
where the time goes in v3:
time: 158 us
  starting transfers between devices  72.3 us (46%)
  waiting for transfers between devices  62.9 us (40%)
  Pallas kernels  18.9 us (12%)
  other arithmetic  1.72 us (1%)
    ppermute x34, waiting for transfers between devices, by_chan(): lax.ppermute(array, 'chan', [(i, i ^ mask) for i in range(16)])  61.7 us
    ppermute x34, starting transfers between devices, by_chan(): lax.ppermute(array, 'chan', [(i, i ^ mask) for i in range(16)])  44.7 us
    pallas_call x21, Pallas kernels, call(): pl.pallas_call(body, out_shape=outs, in_specs=[pl.BlockSpec(memory_space=...  18.9 us
    ppermute x4, starting transfers between devices, borders(): return [lax.ppermute(off, ('space', 'chan'), pairs), by_space(core, 1)]  14.2 us
    ppermute x10, starting transfers between devices, by_space(): return lax.ppermute(array, 'space', [(i, i ^ mask) for i in range(16)])  13.4 us
  transfers between devices with their start and end apart: 48, of which 23 were waited for; matrix products, arithmetic and copies ran while one was open for 1% of the time, Pallas kernels for 9%

profile of v3, /device:TPU:1, one launch (start us, length us, event | category | flops | bytes accessed | tf_op | source)
XLA Modules:
  0.0 157.6 jit_solution(12701474023024829903)
XLA Ops:
  1.9 2.2 %collective-permute-start.3 = (bf16[224,128]{1,0:T(8,128)(2,1)S(1)}, bf16[224,128]{1,0:T(8,128)(2,1)S(1)}, u32[]{:S(2)}, u32[]{:S(2)}) collective-permute-start(bf16[224,128]{1,0:T(8,128)(2,1)S(1)} %get-tuple-element.126), channel_id=1, source_target_pairs={{0,1},{1,0},{2,3},{3,2},{4,5},{5,4},{6,7},{7,6},{8,9},{9,8},{10,11... | collective-permute-start | bytes 172040 | tf_op jit(solution)/shard_map/ppermute | solution.py:316
  4.2 6.0 %collective-permute-start.2 = (bf16[3,16,1024]{2,1,0:T(8,128)(2,1)}, bf16[3,16,1024]{2,1,0:T(8,128)(2,1)S(1)}, u32[]{:S(2)}, u32[]{:S(2)}) collective-permute-start(bf16[3,16,1024]{2,1,0:T(8,128)(2,1)} %bitcast.15), channel_id=1, source_target_pairs={{0,12},{1,13},{2,14},{3,15},{4,8},{5,9},{6,10},{7,11},{8,4},{9,5},... | collective-permute-start | bytes 294920 | tf_op jit(solution)/shard_map/ppermute | solution.py:316
  10.2 1.2 collective-permute-start.1
  14.0 5.8 %collective-permute-done.4.refs_2_ = bf16[224,128]{1,0:T(8,128)(2,1)S(1)} collective-permute-done((bf16[224,128]{1,0:T(8,128)(2,1)S(1)}, bf16[224,128]{1,0:T(8,128)(2,1)S(1)}, u32[]{:S(2)}, u32[]{:S(2)}) %collective-permute-start.4) | collective-permute-done | bytes 57376 | tf_op jit(solution)/shard_map/ppermute | solution.py:316
  19.9 2.9 %collective-permute-done.5.refs_3_ = bf16[224,128]{1,0:T(8,128)(2,1)S(1)} collective-permute-done((bf16[224,128]{1,0:T(8,128)(2,1)S(1)}, bf16[224,128]{1,0:T(8,128)(2,1)S(1)}, u32[]{:S(2)}, u32[]{:S(2)}) %collective-permute-start.5) | collective-permute-done | bytes 57376 | tf_op jit(solution)/shard_map/ppermute | solution.py:316
  22.8 2.6 %collective-permute-start.6 = (bf16[4,16,1024]{2,1,0:T(8,128)(2,1)S(1)}, bf16[4,16,1024]{2,1,0:T(8,128)(2,1)S(1)}, u32[]{:S(2)}, u32[]{:S(2)}) collective-permute-start(bf16[4,16,1024]{2,1,0:T(8,128)(2,1)S(1)} %get-tuple-element.137), channel_id=1, source_target_pairs={{0,1},{1,0},{2,3},{3,2},{4,5},{5,4},{6,7},{7,6},{8,9},{9,8},{10,11... | collective-permute-start | bytes 393224 | tf_op jit(solution)/shard_map/ppermute | solution.py:356
  25.6 1.1 collective-permute-start.9
  26.8 3.3 %shard_map.78 = (bf16[192,576]{1,0:T(8,128)(2,1)S(1)}, bf16[192,576]{1,0:T(8,128)(2,1)S(1)}) custom-call(bf16[224,128]{1,0:T(8,128)(2,1)S(1)} %get-tuple-element.139.refs_0_, bf16[224,128]{1,0:T(8,128)(2,1)S(1)} %collective-permute-done.3.refs_1_, bf16[224,128]{1,0:T(8,128)(2,1)S(1)} %collective-permute-done.4.refs_2_, ...), custom_call_target="tpu_custom_call" | custom-call | bytes 671744 | tf_op jit(solution)/shard_map/pallas_call | solution.py:31
  30.1 1.4 shard_map.79
  34.2 1.5 collective-permute-done.8
  36.6 1.8 %collective-permute-done.11 = bf16[3,16,1024]{2,1,0:T(8,128)(2,1)S(1)} collective-permute-done((bf16[3,16,1024]{2,1,0:T(8,128)(2,1)S(1)}, bf16[3,16,1024]{2,1,0:T(8,128)(2,1)S(1)}, u32[]{:S(2)}, u32[]{:S(2)}) %collective-permute-start.11) | collective-permute-done | bytes 98336 | tf_op jit(solution)/shard_map/ppermute | solution.py:316
  41.2 3.0 %collective-permute-done.14.s3.refs_3_ = bf16[3,16,1024]{2,1,0:T(8,128)(2,1)S(1)} collective-permute-done((bf16[3,16,1024]{2,1,0:T(8,128)(2,1)S(1)}, bf16[3,16,1024]{2,1,0:T(8,128)(2,1)S(1)}, u32[]{:S(2)}, u32[]{:S(2)}) %collective-permute-start.14) | collective-permute-done | bytes 98336 | tf_op jit(solution)/shard_map/ppermute | solution.py:316
  44.9 4.5 %collective-permute-start.16 = (bf16[4,16,1024]{2,1,0:T(8,128)(2,1)S(1)}, bf16[4,16,1024]{2,1,0:T(8,128)(2,1)S(1)}, u32[]{:S(2)}, u32[]{:S(2)}) collective-permute-start(bf16[4,16,1024]{2,1,0:T(8,128)(2,1)S(1)} %get-tuple-element.165), channel_id=1, source_target_pairs={{0,1},{1,0},{2,3},{3,2},{4,5},{5,4},{6,7},{7,6},{8,9},{9,8},{10,11... | collective-permute-start | bytes 393224 | tf_op jit(solution)/shard_map/ppermute | solution.py:356
  49.4 3.3 %shard_map.81 = (bf16[192,576]{1,0:T(8,128)(2,1)S(1)}, bf16[192,576]{1,0:T(8,128)(2,1)S(1)}) custom-call(bf16[224,128]{1,0:T(8,128)(2,1)S(1)} %get-tuple-element.132.refs_0_, bf16[448,128]{1,0:T(8,128)(2,1)S(1)} %collective-permute-done.9.right_ref.refs_1_, bf16[448,128]{1,0:T(8,128)(2,1)S(1)} %collective-permute-done.15.refs_2_), custom_call_target="tpu_custom_call" | custom-call | bytes 729088 | tf_op jit(solution)/shard_map/pallas_call | solution.py:31
  52.8 1.4 shard_map.83
  54.1 2.5 %collective-permute-start.18 = (bf16[3,16,1024]{2,1,0:T(8,128)(2,1)S(1)}, bf16[3,16,1024]{2,1,0:T(8,128)(2,1)S(1)}, u32[]{:S(2)}, u32[]{:S(2)}) collective-permute-start(bf16[3,16,1024]{2,1,0:T(8,128)(2,1)S(1)} %get-tuple-element.168), channel_id=1, source_target_pairs={{0,8},{1,9},{2,10},{3,11},{4,12},{5,13},{6,14},{7,15},{8,0},{9,1},... | collective-permute-start | bytes 294920 | tf_op jit(solution)/shard_map/ppermute | solution.py:316
  57.7 2.1 %collective-permute-start.20 = (bf16[3,16,1024]{2,1,0:T(8,128)(2,1)S(1)}, bf16[3,16,1024]{2,1,0:T(8,128)(2,1)S(1)}, u32[]{:S(2)}, u32[]{:S(2)}) collective-permute-start(bf16[3,16,1024]{2,1,0:T(8,128)(2,1)S(1)} %get-tuple-element.170), channel_id=1, source_target_pairs={{0,12},{1,13},{2,14},{3,15},{4,8},{5,9},{6,10},{7,11},{8,4},{9,5},... | collective-permute-start | bytes 294920 | tf_op jit(solution)/shard_map/ppermute | solution.py:316
  59.9 2.1 %collective-permute-done.18 = bf16[3,16,1024]{2,1,0:T(8,128)(2,1)S(1)} collective-permute-done((bf16[3,16,1024]{2,1,0:T(8,128)(2,1)S(1)}, bf16[3,16,1024]{2,1,0:T(8,128)(2,1)S(1)}, u32[]{:S(2)}, u32[]{:S(2)}) %collective-permute-start.18) | collective-permute-done | bytes 98336 | tf_op jit(solution)/shard_map/ppermute | solution.py:316
  62.0 6.3 %collective-permute-done.19 = bf16[3,16,1024]{2,1,0:T(8,128)(2,1)S(1)} collective-permute-done((bf16[3,16,1024]{2,1,0:T(8,128)(2,1)S(1)}, bf16[3,16,1024]{2,1,0:T(8,128)(2,1)S(1)}, u32[]{:S(2)}, u32[]{:S(2)}) %collective-permute-start.19) | collective-permute-done | bytes 98336 | tf_op jit(solution)/shard_map/ppermute | solution.py:316
  69.1 1.9 %collective-permute-start.23 = (bf16[3,16,1024]{2,1,0:T(8,128)(2,1)S(1)}, bf16[3,16,1024]{2,1,0:T(8,128)(2,1)S(1)}, u32[]{:S(2)}, u32[]{:S(2)}) collective-permute-start(bf16[3,16,1024]{2,1,0:T(8,128)(2,1)S(1)} %get-tuple-element.246.s0.refs_6_.refs_0_), channel_id=1, source_target_pairs={{0,12},{1,13},{2,14},{3,15},{4,8},{5,9},{6,10},{7,11},{8,4},{9,5},... | collective-permute-start | bytes 294920 | tf_op jit(solution)/shard_map/ppermute | solution.py:316
  71.0 1.5 collective-permute-start.22
  72.6 2.2 %collective-permute-start.21 = (bf16[3,16,1024]{2,1,0:T(8,128)(2,1)S(1)}, bf16[3,16,1024]{2,1,0:T(8,128)(2,1)S(1)}, u32[]{:S(2)}, u32[]{:S(2)}) collective-permute-start(bf16[3,16,1024]{2,1,0:T(8,128)(2,1)S(1)} %get-tuple-element.246.s0.refs_6_.refs_0_), channel_id=1, source_target_pairs={{0,8},{1,9},{2,10},{3,11},{4,12},{5,13},{6,14},{7,15},{8,0},{9,1},... | collective-permute-start | bytes 294920 | tf_op jit(solution)/shard_map/ppermute | solution.py:316
  75.5 3.2 %collective-permute-done.22.s2.refs_8_.refs_2_ = bf16[3,16,1024]{2,1,0:T(8,128)(2,1)S(1)} collective-permute-done((bf16[3,16,1024]{2,1,0:T(8,128)(2,1)S(1)}, bf16[3,16,1024]{2,1,0:T(8,128)(2,1)S(1)}, u32[]{:S(2)}, u32[]{:S(2)}) %collective-permute-start.22) | collective-permute-done | bytes 98336 | tf_op jit(solution)/shard_map/ppermute | solution.py:316
  78.7 5.5 %collective-permute-done.21.s1.refs_7_.refs_1_ = bf16[3,16,1024]{2,1,0:T(8,128)(2,1)S(1)} collective-permute-done((bf16[3,16,1024]{2,1,0:T(8,128)(2,1)S(1)}, bf16[3,16,1024]{2,1,0:T(8,128)(2,1)S(1)}, u32[]{:S(2)}, u32[]{:S(2)}) %collective-permute-start.21) | collective-permute-done | bytes 98336 | tf_op jit(solution)/shard_map/ppermute | solution.py:316
  84.2 1.5 collective-permute-start.24
  85.7 2.6 %shard_map.85 = (bf16[224,128]{1,0:T(8,128)(2,1)S(1)}, bf16[448,128]{1,0:T(8,128)(2,1)S(1)}, bf16[224,128]{1,0:T(8,128)(2,1)S(1)}) custom-call(s32[1]{0:T(128)} %bitcast.space_ref, bf16[3,16,1024]{2,1,0:T(8,128)(2,1)S(1)} %multiply_convert_fusion.2.s0.refs_0_, bf16[3,16,1024]{2,1,0:T(8,128)(2,1)S(1)} %collective-permute-done.12.s1.refs_1_, ...), custom_call_target="tpu_custom_call" | custom-call | flops 679477248 | bytes 1277952 | tf_op jit(solution)/shard_map/pallas_call | solution.py:31
  88.9 1.2 collective-permute-start.29
  90.1 1.4 shard_map.86
  91.5 1.3 collective-permute-start.26
  92.7 1.5 collective-permute-start.28
  95.0 2.8 %collective-permute-done.27 = bf16[3,16,1024]{2,1,0:T(8,128)(2,1)S(1)} collective-permute-done((bf16[3,16,1024]{2,1,0:T(8,128)(2,1)S(1)}, bf16[3,16,1024]{2,1,0:T(8,128)(2,1)S(1)}, u32[]{:S(2)}, u32[]{:S(2)}) %collective-permute-start.27) | collective-permute-done | bytes 98336 | tf_op jit(solution)/shard_map/ppermute | solution.py:316
  97.9 1.3 collective-permute-done.28
  99.9 2.7 %collective-permute-start.32 = (bf16[3,16,1024]{2,1,0:T(8,128)(2,1)S(1)}, bf16[3,16,1024]{2,1,0:T(8,128)(2,1)S(1)}, u32[]{:S(2)}, u32[]{:S(2)}) collective-permute-start(bf16[3,16,1024]{2,1,0:T(8,128)(2,1)S(1)} %multiply_convert_fusion.refs_6_.s0.refs_0_), channel_id=1, source_target_pairs={{0,3},{1,2},{2,1},{3,0},{4,7},{5,6},{6,5},{7,4},{8,11},{9,10},{10,... | collective-permute-start | bytes 294920 | tf_op jit(solution)/shard_map/ppermute | solution.py:316
  103.2 2.5 %collective-permute-done.32.refs_9_.s3.refs_3_ = bf16[3,16,1024]{2,1,0:T(8,128)(2,1)S(1)} collective-permute-done((bf16[3,16,1024]{2,1,0:T(8,128)(2,1)S(1)}, bf16[3,16,1024]{2,1,0:T(8,128)(2,1)S(1)}, u32[]{:S(2)}, u32[]{:S(2)}) %collective-permute-start.32) | collective-permute-done | bytes 98336 | tf_op jit(solution)/shard_map/ppermute | solution.py:316
  105.6 1.3 collective-permute-done.31.refs_8_.s2.refs_2_
  106.9 1.5 shard_map.88
  108.4 5.5 %collective-permute-start.37 = (bf16[4,16,1024]{2,1,0:T(8,128)(2,1)S(1)}, bf16[4,16,1024]{2,1,0:T(8,128)(2,1)S(1)}, u32[]{:S(2)}, u32[]{:S(2)}) collective-permute-start(bf16[4,16,1024]{2,1,0:T(8,128)(2,1)S(1)} %get-tuple-element.206), channel_id=1, source_target_pairs={{0,1},{1,0},{2,3},{3,2},{4,5},{5,4},{6,7},{7,6},{8,9},{9,8},{10,11... | collective-permute-start | bytes 393224 | tf_op jit(solution)/shard_map/ppermute | solution.py:356
  114.6 1.3 collective-permute-start.35
  116.7 1.1 collective-permute-done.34.refs_1_
  117.9 2.1 %collective-permute-done.36.refs_3_ = bf16[224,128]{1,0:T(8,128)(2,1)S(1)} collective-permute-done((bf16[224,128]{1,0:T(8,128)(2,1)S(1)}, bf16[224,128]{1,0:T(8,128)(2,1)S(1)}, u32[]{:S(2)}, u32[]{:S(2)}) %collective-permute-start.36) | collective-permute-done | bytes 57376 | tf_op jit(solution)/shard_map/ppermute | solution.py:316
  120.3 1.9 %collective-permute-start.39 = (bf16[896,128]{1,0:T(8,128)(2,1)S(1)}, bf16[896,128]{1,0:T(8,128)(2,1)S(1)}, u32[]{:S(2)}, u32[]{:S(2)}) collective-permute-start(bf16[896,128]{1,0:T(8,128)(2,1)S(1)} %get-tuple-element.215), channel_id=1, source_target_pairs={{0,16},{16,0},{32,48},{48,32},{64,80},{80,64},{96,112},{112,96},{1... | collective-permute-start | bytes 688136 | tf_op jit(solution)/shard_map/ppermute | solution.py:320
  122.2 1.4 shard_map.91
  123.7 7.2 %collective-permute-start.40 = (bf16[896,128]{1,0:T(8,128)(2,1)S(1)}, bf16[896,128]{1,0:T(8,128)(2,1)S(1)}, u32[]{:S(2)}, u32[]{:S(2)}) collective-permute-start(bf16[896,128]{1,0:T(8,128)(2,1)S(1)} %shard_map.92.refs_0_), channel_id=1, source_target_pairs={{0,128},{16,144},{32,160},{48,176},{64,192},{80,208},{96,224},{112... | collective-permute-start | bytes 688136 | tf_op jit(solution)/shard_map/ppermute | solution.py:320
  131.6 6.7 %collective-permute-done.41 = bf16[3,16,1024]{2,1,0:T(8,128)(2,1)S(1)} collective-permute-done((bf16[3,16,1024]{2,1,0:T(8,128)(2,1)S(1)}, bf16[3,16,1024]{2,1,0:T(8,128)(2,1)S(1)}, u32[]{:S(2)}, u32[]{:S(2)}) %collective-permute-start.41) | collective-permute-done | bytes 98336 | tf_op jit(solution)/shard_map/ppermute | solution.py:316
  138.6 3.1 %collective-permute-start.42 = (bf16[896,128]{1,0:T(8,128)(2,1)S(1)}, bf16[896,128]{1,0:T(8,128)(2,1)S(1)}, u32[]{:S(2)}, u32[]{:S(2)}) collective-permute-start(bf16[896,128]{1,0:T(8,128)(2,1)S(1)} %shard_map.93.refs_0_), channel_id=1, source_target_pairs={{0,32},{16,48},{32,0},{48,16},{64,96},{80,112},{96,64},{112,80},{1... | collective-permute-start | bytes 688136 | tf_op jit(solution)/shard_map/ppermute | solution.py:320
  141.8 3.0 %collective-permute-start.45 = (bf16[3,16,1024]{2,1,0:T(8,128)(2,1)S(1)}, bf16[3,16,1024]{2,1,0:T(8,128)(2,1)S(1)}, u32[]{:S(2)}, u32[]{:S(2)}) collective-permute-start(bf16[3,16,1024]{2,1,0:T(8,128)(2,1)S(1)} %get-tuple-element.235), channel_id=1, source_target_pairs={{0,8},{1,9},{2,10},{3,11},{4,12},{5,13},{6,14},{7,15},{8,0},{9,1},... | collective-permute-start | bytes 294920 | tf_op jit(solution)/shard_map/ppermute | solution.py:316
  144.8 9.5 %collective-permute-done.45 = bf16[3,16,1024]{2,1,0:T(8,128)(2,1)S(1)} collective-permute-done((bf16[3,16,1024]{2,1,0:T(8,128)(2,1)S(1)}, bf16[3,16,1024]{2,1,0:T(8,128)(2,1)S(1)}, u32[]{:S(2)}, u32[]{:S(2)}) %collective-permute-start.45) | collective-permute-done | bytes 98336 | tf_op jit(solution)/shard_map/ppermute | solution.py:316
  156.3 1.4 shard_map.95
  (81 shorter events, 21.7 us)
Async XLA Ops:
  1.9 11.1 %collective-permute-start.3 = (bf16[224,128]{1,0:T(8,128)(2,1)S(1)}, bf16[224,128]{1,0:T(8,128)(2,1)S(1)}, u32[]{:S(2)}, u32[]{:S(2)}) collective-permute-start(bf16[224,128]{1,0:T(8,128)(2,1)S(1)} %get-tuple-element.126), channel_id=1, source_target_pairs={{0,1},{1,0},{2,3},{3,2},{4,5},{5,4},{6,7},{7,6},{8,9},{9,8},{10,11... | collective-permute-start | bytes 172040 | tf_op jit(solution)/shard_map/ppermute | solution.py:316
  4.2 18.6 %collective-permute-start.2 = (bf16[3,16,1024]{2,1,0:T(8,128)(2,1)}, bf16[3,16,1024]{2,1,0:T(8,128)(2,1)S(1)}, u32[]{:S(2)}, u32[]{:S(2)}) collective-permute-start(bf16[3,16,1024]{2,1,0:T(8,128)(2,1)} %bitcast.15), channel_id=1, source_target_pairs={{0,12},{1,13},{2,14},{3,15},{4,8},{5,9},{6,10},{7,11},{8,4},{9,5},... | collective-permute-start | bytes 294920 | tf_op jit(solution)/shard_map/ppermute | solution.py:316
  10.2 12.6 %collective-permute-start.1 = (bf16[3,16,1024]{2,1,0:T(8,128)(2,1)}, bf16[3,16,1024]{2,1,0:T(8,128)(2,1)S(1)}, u32[]{:S(2)}, u32[]{:S(2)}) collective-permute-start(bf16[3,16,1024]{2,1,0:T(8,128)(2,1)} %bitcast.16), channel_id=1, source_target_pairs={{0,4},{1,5},{2,6},{3,7},{4,0},{5,1},{6,2},{7,3},{8,12},{9,13},{10,... | collective-permute-start | bytes 294920 | tf_op jit(solution)/shard_map/ppermute | solution.py:316
  11.4 11.4 %collective-permute-start = (bf16[3,16,1024]{2,1,0:T(8,128)(2,1)}, bf16[3,16,1024]{2,1,0:T(8,128)(2,1)S(1)}, u32[]{:S(2)}, u32[]{:S(2)}) collective-permute-start(bf16[3,16,1024]{2,1,0:T(8,128)(2,1)} %bitcast.17), channel_id=1, source_target_pairs={{0,8},{1,9},{2,10},{3,11},{4,12},{5,13},{6,14},{7,15},{8,0},{9,1},... | collective-permute-start | bytes 294920 | tf_op jit(solution)/shard_map/ppermute | solution.py:316
  12.3 7.6 %collective-permute-start.4 = (bf16[224,128]{1,0:T(8,128)(2,1)S(1)}, bf16[224,128]{1,0:T(8,128)(2,1)S(1)}, u32[]{:S(2)}, u32[]{:S(2)}) collective-permute-start(bf16[224,128]{1,0:T(8,128)(2,1)S(1)} %get-tuple-element.127), channel_id=1, source_target_pairs={{0,2},{1,3},{2,0},{3,1},{4,6},{5,7},{6,4},{7,5},{8,10},{9,11},{10,... | collective-permute-start | bytes 172040 | tf_op jit(solution)/shard_map/ppermute | solution.py:316
  13.0 9.7 %collective-permute-start.5 = (bf16[224,128]{1,0:T(8,128)(2,1)S(1)}, bf16[224,128]{1,0:T(8,128)(2,1)S(1)}, u32[]{:S(2)}, u32[]{:S(2)}) collective-permute-start(bf16[224,128]{1,0:T(8,128)(2,1)S(1)} %get-tuple-element.128), channel_id=1, source_target_pairs={{0,3},{1,2},{2,1},{3,0},{4,7},{5,6},{6,5},{7,4},{8,11},{9,10},{10,... | collective-permute-start | bytes 172040 | tf_op jit(solution)/shard_map/ppermute | solution.py:316
  22.8 7.3 %collective-permute-start.6 = (bf16[4,16,1024]{2,1,0:T(8,128)(2,1)S(1)}, bf16[4,16,1024]{2,1,0:T(8,128)(2,1)S(1)}, u32[]{:S(2)}, u32[]{:S(2)}) collective-permute-start(bf16[4,16,1024]{2,1,0:T(8,128)(2,1)S(1)} %get-tuple-element.137), channel_id=1, source_target_pairs={{0,1},{1,0},{2,3},{3,2},{4,5},{5,4},{6,7},{7,6},{8,9},{9,8},{10,11... | collective-permute-start | bytes 393224 | tf_op jit(solution)/shard_map/ppermute | solution.py:356
  25.5 4.6 %collective-permute-start.7 = (bf16[4,16,1024]{2,1,0:T(8,128)(2,1)S(1)}, bf16[4,16,1024]{2,1,0:T(8,128)(2,1)S(1)}, u32[]{:S(2)}, u32[]{:S(2)}) collective-permute-start(bf16[4,16,1024]{2,1,0:T(8,128)(2,1)S(1)} %get-tuple-element.138), channel_id=1, source_target_pairs={{0,16},{16,0},{32,48},{48,32},{64,80},{80,64},{96,112},{112,96},{1... | collective-permute-start | bytes 393224 | tf_op jit(solution)/shard_map/ppermute | solution.py:320
  25.6 8.6 %collective-permute-start.9 = (bf16[448,128]{1,0:T(8,128)(2,1)S(1)}, bf16[448,128]{1,0:T(8,128)(2,1)S(1)}, u32[]{:S(2)}, u32[]{:S(2)}) collective-permute-start(bf16[448,128]{1,0:T(8,128)(2,1)S(1)} %get-tuple-element.152), channel_id=1, source_target_pairs={{0,4},{1,5},{2,6},{3,7},{4,0},{5,1},{6,2},{7,3},{8,12},{9,13},{10,... | collective-permute-start | bytes 344072 | tf_op jit(solution)/shard_map/ppermute | solution.py:316
  31.5 4.2 %collective-permute-start.8 = (bf16[3,16,1024]{2,1,0:T(8,128)(2,1)S(1)}, bf16[3,16,1024]{2,1,0:T(8,128)(2,1)S(1)}, u32[]{:S(2)}, u32[]{:S(2)}) collective-permute-start(bf16[3,16,1024]{2,1,0:T(8,128)(2,1)S(1)} %get-tuple-element.151), channel_id=1, source_target_pairs={{0,1},{1,0},{2,3},{3,2},{4,5},{5,4},{6,7},{7,6},{8,9},{9,8},{10,11... | collective-permute-start | bytes 294920 | tf_op jit(solution)/shard_map/ppermute | solution.py:316
  32.4 4.2 %collective-permute-start.10 = (bf16[3,16,1024]{2,1,0:T(8,128)(2,1)S(1)}, bf16[3,16,1024]{2,1,0:T(8,128)(2,1)S(1)}, u32[]{:S(2)}, u32[]{:S(2)}) collective-permute-start(bf16[3,16,1024]{2,1,0:T(8,128)(2,1)S(1)} %get-tuple-element.156), channel_id=1, source_target_pairs={{0,2},{1,3},{2,0},{3,1},{4,6},{5,7},{6,4},{7,5},{8,10},{9,11},{10,... | collective-permute-start | bytes 294920 | tf_op jit(solution)/shard_map/ppermute | solution.py:316
  33.2 5.2 %collective-permute-start.11 = (bf16[3,16,1024]{2,1,0:T(8,128)(2,1)S(1)}, bf16[3,16,1024]{2,1,0:T(8,128)(2,1)S(1)}, u32[]{:S(2)}, u32[]{:S(2)}) collective-permute-start(bf16[3,16,1024]{2,1,0:T(8,128)(2,1)S(1)} %get-tuple-element.157), channel_id=1, source_target_pairs={{0,3},{1,2},{2,1},{3,0},{4,7},{5,6},{6,5},{7,4},{8,11},{9,10},{10,... | collective-permute-start | bytes 294920 | tf_op jit(solution)/shard_map/ppermute | solution.py:316
  35.7 9.1 %collective-permute-start.15 = (bf16[448,128]{1,0:T(8,128)(2,1)S(1)}, bf16[448,128]{1,0:T(8,128)(2,1)S(1)}, u32[]{:S(2)}, u32[]{:S(2)}) collective-permute-start(bf16[448,128]{1,0:T(8,128)(2,1)S(1)} %shard_map.80), channel_id=1, source_target_pairs={{0,12},{1,13},{2,14},{3,15},{4,8},{5,9},{6,10},{7,11},{8,4},{9,5},... | collective-permute-start | bytes 344072 | tf_op jit(solution)/shard_map/ppermute | solution.py:316
  38.4 5.7 %collective-permute-start.14 = (bf16[3,16,1024]{2,1,0:T(8,128)(2,1)S(1)}, bf16[3,16,1024]{2,1,0:T(8,128)(2,1)S(1)}, u32[]{:S(2)}, u32[]{:S(2)}) collective-permute-start(bf16[3,16,1024]{2,1,0:T(8,128)(2,1)S(1)} %multiply_convert_fusion.2.s0.refs_0_), channel_id=1, source_target_pairs={{0,3},{1,2},{2,1},{3,0},{4,7},{5,6},{6,5},{7,4},{8,11},{9,10},{10,... | collective-permute-start | bytes 294920 | tf_op jit(solution)/shard_map/ppermute | solution.py:316
  39.5 5.4 %collective-permute-start.13 = (bf16[3,16,1024]{2,1,0:T(8,128)(2,1)S(1)}, bf16[3,16,1024]{2,1,0:T(8,128)(2,1)S(1)}, u32[]{:S(2)}, u32[]{:S(2)}) collective-permute-start(bf16[3,16,1024]{2,1,0:T(8,128)(2,1)S(1)} %multiply_convert_fusion.2.s0.refs_0_), channel_id=1, source_target_pairs={{0,2},{1,3},{2,0},{3,1},{4,6},{5,7},{6,4},{7,5},{8,10},{9,11},{10,... | collective-permute-start | bytes 294920 | tf_op jit(solution)/shard_map/ppermute | solution.py:316
  40.3 4.5 %collective-permute-start.12 = (bf16[3,16,1024]{2,1,0:T(8,128)(2,1)S(1)}, bf16[3,16,1024]{2,1,0:T(8,128)(2,1)S(1)}, u32[]{:S(2)}, u32[]{:S(2)}) collective-permute-start(bf16[3,16,1024]{2,1,0:T(8,128)(2,1)S(1)} %multiply_convert_fusion.2.s0.refs_0_), channel_id=1, source_target_pairs={{0,1},{1,0},{2,3},{3,2},{4,5},{5,4},{6,7},{7,6},{8,9},{9,8},{10,11... | collective-permute-start | bytes 294920 | tf_op jit(solution)/shard_map/ppermute | solution.py:316
  44.9 7.9 %collective-permute-start.16 = (bf16[4,16,1024]{2,1,0:T(8,128)(2,1)S(1)}, bf16[4,16,1024]{2,1,0:T(8,128)(2,1)S(1)}, u32[]{:S(2)}, u32[]{:S(2)}) collective-permute-start(bf16[4,16,1024]{2,1,0:T(8,128)(2,1)S(1)} %get-tuple-element.165), channel_id=1, source_target_pairs={{0,1},{1,0},{2,3},{3,2},{4,5},{5,4},{6,7},{7,6},{8,9},{9,8},{10,11... | collective-permute-start | bytes 393224 | tf_op jit(solution)/shard_map/ppermute | solution.py:356
  49.4 3.4 %collective-permute-start.17 = (bf16[4,16,1024]{2,1,0:T(8,128)(2,1)S(1)}, bf16[4,16,1024]{2,1,0:T(8,128)(2,1)S(1)}, u32[]{:S(2)}, u32[]{:S(2)}) collective-permute-start(bf16[4,16,1024]{2,1,0:T(8,128)(2,1)S(1)} %get-tuple-element.166), channel_id=1, source_target_pairs={{0,16},{16,0},{32,48},{48,32},{64,80},{80,64},{96,112},{112,96},{1... | collective-permute-start | bytes 393224 | tf_op jit(solution)/shard_map/ppermute | solution.py:320
  54.1 7.8 %collective-permute-start.18 = (bf16[3,16,1024]{2,1,0:T(8,128)(2,1)S(1)}, bf16[3,16,1024]{2,1,0:T(8,128)(2,1)S(1)}, u32[]{:S(2)}, u32[]{:S(2)}) collective-permute-start(bf16[3,16,1024]{2,1,0:T(8,128)(2,1)S(1)} %get-tuple-element.168), channel_id=1, source_target_pairs={{0,8},{1,9},{2,10},{3,11},{4,12},{5,13},{6,14},{7,15},{8,0},{9,1},... | collective-permute-start | bytes 294920 | tf_op jit(solution)/shard_map/ppermute | solution.py:316
  56.7 11.6 %collective-permute-start.19 = (bf16[3,16,1024]{2,1,0:T(8,128)(2,1)S(1)}, bf16[3,16,1024]{2,1,0:T(8,128)(2,1)S(1)}, u32[]{:S(2)}, u32[]{:S(2)}) collective-permute-start(bf16[3,16,1024]{2,1,0:T(8,128)(2,1)S(1)} %get-tuple-element.169), channel_id=1, source_target_pairs={{0,4},{1,5},{2,6},{3,7},{4,0},{5,1},{6,2},{7,3},{8,12},{9,13},{10,... | collective-permute-start | bytes 294920 | tf_op jit(solution)/shard_map/ppermute | solution.py:316
  57.7 10.6 %collective-permute-start.20 = (bf16[3,16,1024]{2,1,0:T(8,128)(2,1)S(1)}, bf16[3,16,1024]{2,1,0:T(8,128)(2,1)S(1)}, u32[]{:S(2)}, u32[]{:S(2)}) collective-permute-start(bf16[3,16,1024]{2,1,0:T(8,128)(2,1)S(1)} %get-tuple-element.170), channel_id=1, source_target_pairs={{0,12},{1,13},{2,14},{3,15},{4,8},{5,9},{6,10},{7,11},{8,4},{9,5},... | collective-permute-start | bytes 294920 | tf_op jit(solution)/shard_map/ppermute | solution.py:316
  69.1 6.4 %collective-permute-start.23 = (bf16[3,16,1024]{2,1,0:T(8,128)(2,1)S(1)}, bf16[3,16,1024]{2,1,0:T(8,128)(2,1)S(1)}, u32[]{:S(2)}, u32[]{:S(2)}) collective-permute-start(bf16[3,16,1024]{2,1,0:T(8,128)(2,1)S(1)} %get-tuple-element.246.s0.refs_6_.refs_0_), channel_id=1, source_target_pairs={{0,12},{1,13},{2,14},{3,15},{4,8},{5,9},{6,10},{7,11},{8,4},{9,5},... | collective-permute-start | bytes 294920 | tf_op jit(solution)/shard_map/ppermute | solution.py:316
  71.0 7.6 %collective-permute-start.22 = (bf16[3,16,1024]{2,1,0:T(8,128)(2,1)S(1)}, bf16[3,16,1024]{2,1,0:T(8,128)(2,1)S(1)}, u32[]{:S(2)}, u32[]{:S(2)}) collective-permute-start(bf16[3,16,1024]{2,1,0:T(8,128)(2,1)S(1)} %get-tuple-element.246.s0.refs_6_.refs_0_), channel_id=1, source_target_pairs={{0,4},{1,5},{2,6},{3,7},{4,0},{5,1},{6,2},{7,3},{8,12},{9,13},{10,... | collective-permute-start | bytes 294920 | tf_op jit(solution)/shard_map/ppermute | solution.py:316
  72.6 11.6 %collective-permute-start.21 = (bf16[3,16,1024]{2,1,0:T(8,128)(2,1)S(1)}, bf16[3,16,1024]{2,1,0:T(8,128)(2,1)S(1)}, u32[]{:S(2)}, u32[]{:S(2)}) collective-permute-start(bf16[3,16,1024]{2,1,0:T(8,128)(2,1)S(1)} %get-tuple-element.246.s0.refs_6_.refs_0_), channel_id=1, source_target_pairs={{0,8},{1,9},{2,10},{3,11},{4,12},{5,13},{6,14},{7,15},{8,0},{9,1},... | collective-permute-start | bytes 294920 | tf_op jit(solution)/shard_map/ppermute | solution.py:316
  84.2 4.8 %collective-permute-start.24 = (bf16[4,16,1024]{2,1,0:T(8,128)(2,1)S(1)}, bf16[4,16,1024]{2,1,0:T(8,128)(2,1)S(1)}, u32[]{:S(2)}, u32[]{:S(2)}) collective-permute-start(bf16[4,16,1024]{2,1,0:T(8,128)(2,1)S(1)} %get-tuple-element.172), channel_id=1, source_target_pairs={{0,1},{1,0},{2,3},{3,2},{4,5},{5,4},{6,7},{7,6},{8,9},{9,8},{10,11... | collective-permute-start | bytes 393224 | tf_op jit(solution)/shard_map/ppermute | solution.py:356
  85.7 3.3 %collective-permute-start.25 = (bf16[4,16,1024]{2,1,0:T(8,128)(2,1)S(1)}, bf16[4,16,1024]{2,1,0:T(8,128)(2,1)S(1)}, u32[]{:S(2)}, u32[]{:S(2)}) collective-permute-start(bf16[4,16,1024]{2,1,0:T(8,128)(2,1)S(1)} %get-tuple-element.173), channel_id=1, source_target_pairs={{0,16},{16,0},{32,48},{48,32},{64,80},{80,64},{96,112},{112,96},{1... | collective-permute-start | bytes 393224 | tf_op jit(solution)/shard_map/ppermute | solution.py:320
  88.9 10.3 %collective-permute-start.29 = (bf16[448,128]{1,0:T(8,128)(2,1)S(1)}, bf16[448,128]{1,0:T(8,128)(2,1)S(1)}, u32[]{:S(2)}, u32[]{:S(2)}) collective-permute-start(bf16[448,128]{1,0:T(8,128)(2,1)S(1)} %get-tuple-element.183), channel_id=1, source_target_pairs={{0,4},{1,5},{2,6},{3,7},{4,0},{5,1},{6,2},{7,3},{8,12},{9,13},{10,... | collective-permute-start | bytes 344072 | tf_op jit(solution)/shard_map/ppermute | solution.py:316
  91.5 3.6 %collective-permute-start.26 = (bf16[3,16,1024]{2,1,0:T(8,128)(2,1)S(1)}, bf16[3,16,1024]{2,1,0:T(8,128)(2,1)S(1)}, u32[]{:S(2)}, u32[]{:S(2)}) collective-permute-start(bf16[3,16,1024]{2,1,0:T(8,128)(2,1)S(1)} %get-tuple-element.180), channel_id=1, source_target_pairs={{0,1},{1,0},{2,3},{3,2},{4,5},{5,4},{6,7},{7,6},{8,9},{9,8},{10,11... | collective-permute-start | bytes 294920 | tf_op jit(solution)/shard_map/ppermute | solution.py:316
  92.7 5.1 %collective-permute-start.27 = (bf16[3,16,1024]{2,1,0:T(8,128)(2,1)S(1)}, bf16[3,16,1024]{2,1,0:T(8,128)(2,1)S(1)}, u32[]{:S(2)}, u32[]{:S(2)}) collective-permute-start(bf16[3,16,1024]{2,1,0:T(8,128)(2,1)S(1)} %get-tuple-element.181), channel_id=1, source_target_pairs={{0,2},{1,3},{2,0},{3,1},{4,6},{5,7},{6,4},{7,5},{8,10},{9,11},{10,... | collective-permute-start | bytes 294920 | tf_op jit(solution)/shard_map/ppermute | solution.py:316
  92.7 6.4 %collective-permute-start.28 = (bf16[3,16,1024]{2,1,0:T(8,128)(2,1)S(1)}, bf16[3,16,1024]{2,1,0:T(8,128)(2,1)S(1)}, u32[]{:S(2)}, u32[]{:S(2)}) collective-permute-start(bf16[3,16,1024]{2,1,0:T(8,128)(2,1)S(1)} %get-tuple-element.182), channel_id=1, source_target_pairs={{0,3},{1,2},{2,1},{3,0},{4,7},{5,6},{6,5},{7,4},{8,11},{9,10},{10,... | collective-permute-start | bytes 294920 | tf_op jit(solution)/shard_map/ppermute | solution.py:316
  99.2 7.7 %collective-permute-start.33 = (bf16[448,128]{1,0:T(8,128)(2,1)S(1)}, bf16[448,128]{1,0:T(8,128)(2,1)S(1)}, u32[]{:S(2)}, u32[]{:S(2)}) collective-permute-start(bf16[448,128]{1,0:T(8,128)(2,1)S(1)} %shard_map.87), channel_id=1, source_target_pairs={{0,12},{1,13},{2,14},{3,15},{4,8},{5,9},{6,10},{7,11},{8,4},{9,5},... | collective-permute-start | bytes 344072 | tf_op jit(solution)/shard_map/ppermute | solution.py:316
  99.9 5.7 %collective-permute-start.32 = (bf16[3,16,1024]{2,1,0:T(8,128)(2,1)S(1)}, bf16[3,16,1024]{2,1,0:T(8,128)(2,1)S(1)}, u32[]{:S(2)}, u32[]{:S(2)}) collective-permute-start(bf16[3,16,1024]{2,1,0:T(8,128)(2,1)S(1)} %multiply_convert_fusion.refs_6_.s0.refs_0_), channel_id=1, source_target_pairs={{0,3},{1,2},{2,1},{3,0},{4,7},{5,6},{6,5},{7,4},{8,11},{9,10},{10,... | collective-permute-start | bytes 294920 | tf_op jit(solution)/shard_map/ppermute | solution.py:316
  102.5 4.4 %collective-permute-start.31 = (bf16[3,16,1024]{2,1,0:T(8,128)(2,1)S(1)}, bf16[3,16,1024]{2,1,0:T(8,128)(2,1)S(1)}, u32[]{:S(2)}, u32[]{:S(2)}) collective-permute-start(bf16[3,16,1024]{2,1,0:T(8,128)(2,1)S(1)} %multiply_convert_fusion.refs_6_.s0.refs_0_), channel_id=1, source_target_pairs={{0,2},{1,3},{2,0},{3,1},{4,6},{5,7},{6,4},{7,5},{8,10},{9,11},{10,... | collective-permute-start | bytes 294920 | tf_op jit(solution)/shard_map/ppermute | solution.py:316
  102.7 4.2 %collective-permute-start.30 = (bf16[3,16,1024]{2,1,0:T(8,128)(2,1)S(1)}, bf16[3,16,1024]{2,1,0:T(8,128)(2,1)S(1)}, u32[]{:S(2)}, u32[]{:S(2)}) collective-permute-start(bf16[3,16,1024]{2,1,0:T(8,128)(2,1)S(1)} %multiply_convert_fusion.refs_6_.s0.refs_0_), channel_id=1, source_target_pairs={{0,1},{1,0},{2,3},{3,2},{4,5},{5,4},{6,7},{7,6},{8,9},{9,8},{10,11... | collective-permute-start | bytes 294920 | tf_op jit(solution)/shard_map/ppermute | solution.py:316
  108.4 11.6 %collective-permute-start.37 = (bf16[4,16,1024]{2,1,0:T(8,128)(2,1)S(1)}, bf16[4,16,1024]{2,1,0:T(8,128)(2,1)S(1)}, u32[]{:S(2)}, u32[]{:S(2)}) collective-permute-start(bf16[4,16,1024]{2,1,0:T(8,128)(2,1)S(1)} %get-tuple-element.206), channel_id=1, source_target_pairs={{0,1},{1,0},{2,3},{3,2},{4,5},{5,4},{6,7},{7,6},{8,9},{9,8},{10,11... | collective-permute-start | bytes 393224 | tf_op jit(solution)/shard_map/ppermute | solution.py:356
  114.0 6.1 %collective-permute-start.38 = (bf16[4,16,1024]{2,1,0:T(8,128)(2,1)S(1)}, bf16[4,16,1024]{2,1,0:T(8,128)(2,1)S(1)}, u32[]{:S(2)}, u32[]{:S(2)}) collective-permute-start(bf16[4,16,1024]{2,1,0:T(8,128)(2,1)S(1)} %get-tuple-element.207), channel_id=1, source_target_pairs={{0,16},{16,0},{32,48},{48,32},{64,80},{80,64},{96,112},{112,96},{1... | collective-permute-start | bytes 393224 | tf_op jit(solution)/shard_map/ppermute | solution.py:320
  114.1 3.7 %collective-permute-start.34 = (bf16[224,128]{1,0:T(8,128)(2,1)S(1)}, bf16[224,128]{1,0:T(8,128)(2,1)S(1)}, u32[]{:S(2)}, u32[]{:S(2)}) collective-permute-start(bf16[224,128]{1,0:T(8,128)(2,1)S(1)} %get-tuple-element.199), channel_id=1, source_target_pairs={{0,1},{1,0},{2,3},{3,2},{4,5},{5,4},{6,7},{7,6},{8,9},{9,8},{10,11... | collective-permute-start | bytes 172040 | tf_op jit(solution)/shard_map/ppermute | solution.py:316
  114.6 3.3 %collective-permute-start.35 = (bf16[224,128]{1,0:T(8,128)(2,1)S(1)}, bf16[224,128]{1,0:T(8,128)(2,1)S(1)}, u32[]{:S(2)}, u32[]{:S(2)}) collective-permute-start(bf16[224,128]{1,0:T(8,128)(2,1)S(1)} %get-tuple-element.200), channel_id=1, source_target_pairs={{0,2},{1,3},{2,0},{3,1},{4,6},{5,7},{6,4},{7,5},{8,10},{9,11},{10,... | collective-permute-start | bytes 172040 | tf_op jit(solution)/shard_map/ppermute | solution.py:316
  115.9 4.1 %collective-permute-start.36 = (bf16[224,128]{1,0:T(8,128)(2,1)S(1)}, bf16[224,128]{1,0:T(8,128)(2,1)S(1)}, u32[]{:S(2)}, u32[]{:S(2)}) collective-permute-start(bf16[224,128]{1,0:T(8,128)(2,1)S(1)} %get-tuple-element.201), channel_id=1, source_target_pairs={{0,3},{1,2},{2,1},{3,0},{4,7},{5,6},{6,5},{7,4},{8,11},{9,10},{10,... | collective-permute-start | bytes 172040 | tf_op jit(solution)/shard_map/ppermute | solution.py:316
  120.3 3.3 %collective-permute-start.39 = (bf16[896,128]{1,0:T(8,128)(2,1)S(1)}, bf16[896,128]{1,0:T(8,128)(2,1)S(1)}, u32[]{:S(2)}, u32[]{:S(2)}) collective-permute-start(bf16[896,128]{1,0:T(8,128)(2,1)S(1)} %get-tuple-element.215), channel_id=1, source_target_pairs={{0,16},{16,0},{32,48},{48,32},{64,80},{80,64},{96,112},{112,96},{1... | collective-permute-start | bytes 688136 | tf_op jit(solution)/shard_map/ppermute | solution.py:320
  123.7 14.7 %collective-permute-start.40 = (bf16[896,128]{1,0:T(8,128)(2,1)S(1)}, bf16[896,128]{1,0:T(8,128)(2,1)S(1)}, u32[]{:S(2)}, u32[]{:S(2)}) collective-permute-start(bf16[896,128]{1,0:T(8,128)(2,1)S(1)} %shard_map.92.refs_0_), channel_id=1, source_target_pairs={{0,128},{16,144},{32,160},{48,176},{64,192},{80,208},{96,224},{112... | collective-permute-start | bytes 688136 | tf_op jit(solution)/shard_map/ppermute | solution.py:320
  130.8 7.5 %collective-permute-start.41 = (bf16[3,16,1024]{2,1,0:T(8,128)(2,1)S(1)}, bf16[3,16,1024]{2,1,0:T(8,128)(2,1)S(1)}, u32[]{:S(2)}, u32[]{:S(2)}) collective-permute-start(bf16[3,16,1024]{2,1,0:T(8,128)(2,1)S(1)} %get-tuple-element.229), channel_id=1, source_target_pairs={{0,4},{1,5},{2,6},{3,7},{4,0},{5,1},{6,2},{7,3},{8,12},{9,13},{10,... | collective-permute-start | bytes 294920 | tf_op jit(solution)/shard_map/ppermute | solution.py:316
  138.4 15.9 %collective-permute-start.44 = (bf16[896,128]{1,0:T(8,128)(2,1)S(1)}, bf16[896,128]{1,0:T(8,128)(2,1)S(1)}, u32[]{:S(2)}, u32[]{:S(2)}) collective-permute-start(bf16[896,128]{1,0:T(8,128)(2,1)S(1)} %shard_map.93.refs_0_), channel_id=1, source_target_pairs={{0,96},{16,112},{32,64},{48,80},{64,32},{80,48},{96,0},{112,16},{1... | collective-permute-start | bytes 688136 | tf_op jit(solution)/shard_map/ppermute | solution.py:320
  138.5 15.8 %collective-permute-start.43 = (bf16[896,128]{1,0:T(8,128)(2,1)S(1)}, bf16[896,128]{1,0:T(8,128)(2,1)S(1)}, u32[]{:S(2)}, u32[]{:S(2)}) collective-permute-start(bf16[896,128]{1,0:T(8,128)(2,1)S(1)} %shard_map.93.refs_0_), channel_id=1, source_target_pairs={{0,64},{16,80},{32,96},{48,112},{64,0},{80,16},{96,32},{112,48},{1... | collective-permute-start | bytes 688136 | tf_op jit(solution)/shard_map/ppermute | solution.py:320
  138.6 15.7 %collective-permute-start.42 = (bf16[896,128]{1,0:T(8,128)(2,1)S(1)}, bf16[896,128]{1,0:T(8,128)(2,1)S(1)}, u32[]{:S(2)}, u32[]{:S(2)}) collective-permute-start(bf16[896,128]{1,0:T(8,128)(2,1)S(1)} %shard_map.93.refs_0_), channel_id=1, source_target_pairs={{0,32},{16,48},{32,0},{48,16},{64,96},{80,112},{96,64},{112,80},{1... | collective-permute-start | bytes 688136 | tf_op jit(solution)/shard_map/ppermute | solution.py:320
  141.8 12.5 %collective-permute-start.45 = (bf16[3,16,1024]{2,1,0:T(8,128)(2,1)S(1)}, bf16[3,16,1024]{2,1,0:T(8,128)(2,1)S(1)}, u32[]{:S(2)}, u32[]{:S(2)}) collective-permute-start(bf16[3,16,1024]{2,1,0:T(8,128)(2,1)S(1)} %get-tuple-element.235), channel_id=1, source_target_pairs={{0,8},{1,9},{2,10},{3,11},{4,12},{5,13},{6,14},{7,15},{8,0},{9,1},... | collective-permute-start | bytes 294920 | tf_op jit(solution)/shard_map/ppermute | solution.py:316
  144.8 9.5 %collective-permute-start.46 = (bf16[3,16,1024]{2,1,0:T(8,128)(2,1)S(1)}, bf16[3,16,1024]{2,1,0:T(8,128)(2,1)S(1)}, u32[]{:S(2)}, u32[]{:S(2)}) collective-permute-start(bf16[3,16,1024]{2,1,0:T(8,128)(2,1)S(1)} %get-tuple-element.236), channel_id=1, source_target_pairs={{0,12},{1,13},{2,14},{3,15},{4,8},{5,9},{6,10},{7,11},{8,4},{9,5},... | collective-permute-start | bytes 294920 | tf_op jit(solution)/shard_map/ppermute | solution.py:316
  154.5 1.8 %collective-permute-start.47 = (bf16[896,128]{1,0:T(8,128)(2,1)S(1)}, bf16[896,128]{1,0:T(8,128)(2,1)S(1)}, u32[]{:S(2)}, u32[]{:S(2)}) collective-permute-start(bf16[896,128]{1,0:T(8,128)(2,1)S(1)} %shard_map.94.mine_ref), channel_id=1, source_target_pairs={{0,16},{16,0},{32,48},{48,32},{64,80},{80,64},{96,112},{112,96},{1... | collective-permute-start | bytes 688136 | tf_op jit(solution)/shard_map/ppermute | solution.py:320
  (4 other events, 37.7 us)
